TPU v7x, 32 devices: a whole 2x2x4 slice. The times are simulated.
32 devices in a mesh: groups: 2 (over x), rows: 16 (over z, y, core).
Axes of the slice: x: 2, y: 2, z: 4, core: 2. Of those that a mesh axis runs over, the one named last changes fastest.
Arguments:
- latents: bfloat16 [2, 64, 256, 128], P('groups', 'rows'), parts along dimension 0, may hold values from -60 to 60
- gain_one: float32 [128], replicated, may hold values from 0.25 to 1.75
- shift_one: float32 [128], replicated, may hold values from -3 to 3
- weight_one: bfloat16 [3, 3, 3, 128, 128], replicated, may hold values from -0.109375 to 0.109375
- bias_one: float32 [128], replicated, may hold values from -3 to 3
- gain_two: float32 [128], replicated, may hold values from 0.25 to 1.75
- shift_two: float32 [128], replicated, may hold values from -3 to 3
- weight_two: bfloat16 [3, 3, 3, 128, 128], replicated, may hold values from -0.109375 to 0.109375
- bias_two: float32 [128], replicated, may hold values from -3 to 3
Outputs:
- decoded: bfloat16 [2, 64, 256, 128], P('groups', 'rows'), parts along dimension 0
There are 2 independent parts, one for each index of `groups`. A program takes and returns all parts, laid end to end along the dimension named above; an argument that names none is the same for every part. Nothing has to cross between parts.
All inputs are finite; a program needn't handle non-finite values.
Results may differ from a plain program's by a relative error of at most 0.004.
Values may be sent and summed in bfloat16 or wider, within the bound.
No kernel may reach another device: no remote copies, remote signals or barrier semaphores. Data moves between devices by JAX's collectives and lax.ppermute only.
A program may use at most 64 MiB of HBM per device.

v0:
```python
import functools

import jax
import jax.numpy as jnp
from jax import lax
from jax.experimental import pallas as pl
from jax.experimental.pallas import tpu as pltpu
from jax.sharding import PartitionSpec as P

GROUPS = 32
ANY = pl.BlockSpec(memory_space=pl.ANY)
VMEM = pl.BlockSpec(memory_space=pltpu.VMEM)
PARAMS = pltpu.CompilerParams(vmem_limit_bytes=24 * 1024 * 1024)


def store_sums(total, square, out_ref):
    total = jnp.sum(total, axis=0, keepdims=True)
    square = jnp.sum(square, axis=0, keepdims=True)
    both = jnp.concatenate([total, square], axis=0)
    out_ref[...] = jnp.broadcast_to(both[None], out_ref.shape)


def add_sums(values, total, square):
    width, channels = values.shape
    split = (width // 8, 8, channels)
    total += jnp.sum(values.reshape(split), axis=0)
    square += jnp.sum((values * values).reshape(split), axis=0)
    return total, square


def sums_kernel(own_ref, out_ref, pair_ref, other_ref):
    rows, _, channels = own_ref.shape
    even = lax.axis_index("rows") % 2 == 0
    for row in range(2):
        top = own_ref[row]
        bottom = own_ref[rows - 2 + row]
        pair_ref[row] = jnp.where(even, bottom, top)
        other_ref[row] = jnp.where(even, top, bottom)
    total = jnp.zeros((8, channels), jnp.float32)
    square = jnp.zeros((8, channels), jnp.float32)
    for row in range(rows):
        total, square = add_sums(own_ref[row].astype(jnp.float32), total, square)
    store_sums(total, square, out_ref)


def sum_weight(source, target):
    taps, channels = source.shape[1], source.shape[2]
    for tap in range(taps):
        total = source[0, tap].astype(jnp.float32)
        total += source[1, tap].astype(jnp.float32)
        total += source[2, tap].astype(jnp.float32)
        high = total.astype(jnp.bfloat16)
        low = (total - high.astype(jnp.float32)).astype(jnp.bfloat16)
        target[pl.ds(tap * channels, channels), :] = jnp.concatenate([high, low], axis=1)


def sum_paired(source, target):
    taps, channels = source.shape[1], source.shape[2]
    columns = taps // 3
    zeros = jnp.zeros((columns * channels, channels), jnp.bfloat16)
    for tap in range(taps):
        total = source[0, tap].astype(jnp.float32)
        total += source[1, tap].astype(jnp.float32)
        total += source[2, tap].astype(jnp.float32)
        total = total.astype(jnp.bfloat16)
        target[pl.ds(tap * channels, channels), 0:channels] = total
        target[pl.ds((tap + columns) * channels, channels), channels : 2 * channels] = total
    target[pl.ds(taps * channels, columns * channels), 0:channels] = zeros
    target[pl.ds(0, columns * channels), channels : 2 * channels] = zeros


def scale_offset(sums_ref, gain_ref, shift_ref, entries):
    sums = jnp.sum(sums_ref[...], axis=0)
    channels = sums.shape[1]
    per_group = channels // GROUPS
    sums = jnp.concatenate([sums, jnp.zeros((6, channels), jnp.float32)], axis=0)
    member = lax.broadcasted_iota(jnp.int32, sums.shape, 1) % per_group
    total = sums
    for step in range(1, per_group):
        total += jnp.where(member >= step, pltpu.roll(sums, step, 1), 0.0)
        total += jnp.where(member < per_group - step, pltpu.roll(sums, channels - step, 1), 0.0)
    total = total * (1.0 / (entries * per_group))
    mean = total[0:1]
    var = total[1:2] - mean * mean
    scale = gain_ref[...] * lax.rsqrt(var + 1e-06)
    return 0.5 * scale, 0.5 * (shift_ref[...] - mean * scale)


def store_taps(values, scale, offset, wide_ref, taps_ref, row):
    width, channels = values.shape
    half = values.astype(jnp.float32) * scale + offset
    act = half * jnp.tanh(half) + half
    wide_ref[row, 8 : 8 + width, :] = act
    wide_ref[row, 7:8, :] = act[0:1]
    wide_ref[row, 8 + width : 9 + width, :] = act[width - 1 : width]
    for tap in range(3):
        shifted = wide_ref[row, 7 + tap : 7 + tap + width, :]
        taps_ref[row, :, tap * channels : (tap + 1) * channels] = shifted.astype(jnp.bfloat16)


def conv_rows(taps_ref, row, count, weight_ref):
    _, width, lanes = taps_ref.shape
    window = jnp.concatenate(
        [taps_ref[row + tap : row + tap + count].reshape(count * width, lanes) for tap in range(3)],
        axis=1,
    )
    both = jnp.dot(window, weight_ref[...], preferred_element_type=jnp.float32)
    half = both.shape[1] // 2
    return both[:, :half] + both[:, half:]


def first_kernel(
    count, sums_ref, own_ref, pair_ref, other_ref, weight_ref, bias_ref, gain_ref, shift_ref,
    hidden_ref, out_ref, wide_ref, taps_ref, summed_ref,
):
    index = lax.axis_index("rows")
    rows, width, channels = own_ref.shape
    even = index % 2 == 0
    scale, offset = scale_offset(sums_ref, gain_ref, shift_ref, rows * width * count)
    sum_weight(weight_ref, summed_ref)

    def make(row):
        if row < 2:
            values = jnp.where(even, other_ref[row], pair_ref[row])
            values = jnp.where(index == 0, own_ref[0], values)
        elif row < rows + 2:
            values = own_ref[row - 2]
        else:
            values = jnp.where(even, pair_ref[row - rows - 2], other_ref[row - rows - 2])
            values = jnp.where(index == count - 1, own_ref[rows - 1], values)
        store_taps(values, scale, offset, wide_ref, taps_ref, row)

    total = jnp.zeros((8, channels), jnp.float32)
    square = jnp.zeros((8, channels), jnp.float32)
    for row in range(rows + 4):
        make(row)
    hidden = conv_rows(taps_ref, 0, rows + 2, summed_ref) + bias_ref[...]
    hidden = hidden.astype(jnp.bfloat16)
    for row in range(rows + 2):
        values = hidden[row * width : (row + 1) * width]
        hidden_ref[row] = values
        if 0 < row <= rows:
            total, square = add_sums(values.astype(jnp.float32), total, square)
    store_sums(total, square, out_ref)

    @pl.when(index == 0)
    def _():
        hidden_ref[0] = hidden_ref[1]

    @pl.when(index == count - 1)
    def _():
        hidden_ref[rows + 1] = hidden_ref[rows]


def second_kernel(
    count, sums_ref, hidden_ref, own_ref, weight_ref, bias_ref, gain_ref, shift_ref,
    out_ref, wide_ref, taps_ref, summed_ref, done_ref, sems,
):
    rows, width, channels = own_ref.shape
    scale, offset = scale_offset(sums_ref, gain_ref, shift_ref, rows * width * count)
    sum_paired(weight_ref, summed_ref)
    copies = [
        pltpu.make_async_copy(done_ref.at[row], out_ref.at[row], sems.at[row])
        for row in range(rows)
    ]
    for row in range(2):
        store_taps(hidden_ref[row], scale, offset, wide_ref, taps_ref, row)
    for row in range(0, rows, 2):
        for i in range(2, 4):
            store_taps(hidden_ref[row + i], scale, offset, wide_ref, taps_ref, row + i)
        window = jnp.concatenate([taps_ref[row + tap] for tap in range(4)], axis=1)
        both = jnp.dot(window, summed_ref[...], preferred_element_type=jnp.float32)
        for i in range(2):
            branch = both[:, i * channels : (i + 1) * channels] + bias_ref[...]
            values = own_ref[row + i].astype(jnp.float32) + branch
            done_ref[row + i] = values.astype(jnp.bfloat16)
            copies[row + i].start()
    for copy in copies:
        copy.wait()


def exchanged(sums):
    return lax.all_to_all(sums, "rows", 0, 0)


def body(
    latents, gain_one, shift_one, weight_one, bias_one, gain_two, shift_two, weight_two, bias_two
):
    count = lax.axis_size("rows")
    own = latents[0]
    rows, width, channels = own.shape
    sums_shape = jax.ShapeDtypeStruct((count, 2, channels), jnp.float32)
    taps = weight_one.shape[1] * weight_one.shape[2]
    slab_shape = jax.ShapeDtypeStruct((2, width, channels), jnp.bfloat16)

    def operands(weight, *vectors):
        vectors = [vector.reshape(1, channels) for vector in vectors]
        return weight.reshape(3, taps, channels, channels), *vectors

    swap_pair = [(i, i ^ 1) for i in range(count)]
    swap_other = [(i, i + 1 if i % 2 else i - 1) for i in range(1, count - 1)]

    sums, pair, other = pl.pallas_call(
        sums_kernel,
        out_shape=[sums_shape, slab_shape, slab_shape],
        in_specs=[VMEM],
        out_specs=[VMEM] * 3,
        compiler_params=PARAMS,
        name="sums",
        cost_estimate=pl.CostEstimate(
            flops=40000000000, bytes_accessed=10000000, transcendentals=0
        ),
    )(own)
    other = lax.ppermute(other, "rows", swap_other)
    pair = lax.ppermute(pair, "rows", swap_pair)
    sums = exchanged(sums)
    hidden, sums = pl.pallas_call(
        functools.partial(first_kernel, count),
        out_shape=[jax.ShapeDtypeStruct((rows + 2, width, channels), jnp.bfloat16), sums_shape],
        in_specs=[VMEM] * 8,
        out_specs=[VMEM] * 2,
        scratch_shapes=[
            pltpu.VMEM((rows + 4, width + 16, channels), jnp.float32),
            pltpu.VMEM((rows + 4, width, 3 * channels), jnp.bfloat16),
            pltpu.VMEM((taps * channels, 2 * channels), jnp.bfloat16),
        ],
        compiler_params=PARAMS, name="first",
    )(sums, own, pair, other, *operands(weight_one, bias_one, gain_one, shift_one))
    sums = exchanged(sums)
    decoded = pl.pallas_call(
        functools.partial(second_kernel, count),
        out_shape=jax.ShapeDtypeStruct(own.shape, jnp.bfloat16),
        in_specs=[VMEM] * 7,
        out_specs=ANY,
        scratch_shapes=[
            pltpu.VMEM((rows + 2, width + 16, channels), jnp.float32),
            pltpu.VMEM((rows + 2, width, 3 * channels), jnp.bfloat16),
            pltpu.VMEM((taps // 3 * 4 * channels, 2 * channels), jnp.bfloat16),
            pltpu.VMEM(own.shape, jnp.bfloat16),
            pltpu.SemaphoreType.DMA((rows,)),
        ],
        compiler_params=PARAMS, name="second",
    )(sums, hidden, own, *operands(weight_two, bias_two, gain_two, shift_two))
    return decoded[None]


def solution(mesh):
    return jax.shard_map(
        body,
        mesh=mesh,
        in_specs=(P("groups", "rows", None, None), P(), P(), P(), P(), P(), P(), P(), P()),
        out_specs=P("groups", "rows", None, None),
        check_vma=False,
    )
```

profile of v0, /device:TPU:0, one launch (start us, length us, event | category | flops | bytes accessed | tf_op | source)
XLA Modules:
  0.0 30.2 jit_solution(4181318183146084689)
XLA Ops:
  0.0 0.0 copy-start
  0.0 0.9 %copy-done = bf16[1,4,256,128]{3,2,1,0:T(8,128)(2,1)S(1)} copy-done((bf16[1,4,256,128]{3,2,1,0:T(8,128)(2,1)S(1)}, bf16[1,4,256,128]{3,2,1,0:T(8,128)(2,1)}, u32[]{:S(2)}) %copy-start) | copy-done | bytes 262168
  1.0 0.0 copy-start.1
  1.0 0.0 copy-start.3
  1.0 0.0 copy-start.4
  1.0 0.0 copy-start.5
  1.0 0.1 sums.1
  1.1 0.0 copy-start.2
  1.1 0.5 %collective-permute-start = (bf16[2,256,128]{2,1,0:T(8,128)(2,1)S(1)}, bf16[2,256,128]{2,1,0:T(8,128)(2,1)S(1)}, u32[]{:S(2)}, u32[]{:S(2)}) collective-permute-start(bf16[2,256,128]{2,1,0:T(8,128)(2,1)S(1)} %get-tuple-element.11), channel_id=1, source_target_pairs={{0,1},{1,0},{2,3},{3,2},{4,5},{5,4},{6,7},{7,6},{8,9},{9,8},{10,11... | collective-permute-start | bytes 393224 | tf_op jit(solution)/shard_map/ppermute | solution.py:215
  1.6 0.7 %collective-permute-start.1 = (bf16[2,256,128]{2,1,0:T(8,128)(2,1)S(1)}, bf16[2,256,128]{2,1,0:T(8,128)(2,1)S(1)}, u32[]{:S(2)}, u32[]{:S(2)}) collective-permute-start(bf16[2,256,128]{2,1,0:T(8,128)(2,1)S(1)} %get-tuple-element.12), channel_id=1, source_target_pairs={{1,2},{2,1},{3,4},{4,3},{5,6},{6,5},{7,8},{8,7},{9,10},{10,9},{11,... | collective-permute-start | bytes 393224 | tf_op jit(solution)/shard_map/ppermute | solution.py:214
  2.3 15.1 %all_to_all.10.sums_ref = f32[16,2,128]{2,1,0:T(2,128)S(1)} all-to-all(f32[16,2,128]{2,1,0:T(2,128)S(1)} %get-tuple-element.10), channel_id=1, replica_groups=mesh['groups'=2,'rows'=16] {'rows'}, dimensions={0} | all-to-all | bytes 32768 | tf_op jit(solution)/shard_map/all_to_all | solution.py:183
  17.4 0.0 collective-permute-done.pair_ref
  17.4 0.0 collective-permute-done.1.other_ref
  17.4 0.0 copy-done.1
  17.4 0.0 copy-done.3
  17.4 0.0 copy-done.4
  17.4 0.0 copy-done.5
  17.4 1.5 %first.1 = (bf16[6,256,128]{2,1,0:T(8,128)(2,1)S(1)}, f32[16,2,128]{2,1,0:T(2,128)S(1)}) custom-call(f32[16,2,128]{2,1,0:T(2,128)S(1)} %all_to_all.10.sums_ref, bf16[4,256,128]{2,1,0:T(8,128)(2,1)S(1)} %bitcast.11, bf16[2,256,128]{2,1,0:T(8,128)(2,1)S(1)} %collective-permute-done.pair_ref, bf16[2,256,128]{2,1,0:T(8,128)(2,1)S(1)} %collective-permute-done.1.other_ref, ...), custom_call_target="tpu_custom_call" | custom-call | tf_op jit(solution)/shard_map/first/pallas_call | solution.py:217
  18.9 9.1 %all_to_all.11.sums_ref = f32[16,2,128]{2,1,0:T(2,128)S(1)} all-to-all(f32[16,2,128]{2,1,0:T(2,128)S(1)} %get-tuple-element.13), channel_id=1, replica_groups=mesh['groups'=2,'rows'=16] {'rows'}, dimensions={0} | all-to-all | bytes 32768 | tf_op jit(solution)/shard_map/all_to_all | solution.py:183
  28.0 0.0 copy-start.6
  28.0 0.0 copy-start.7
  28.0 0.0 copy-start.8
  28.0 0.0 copy-done.2
  28.0 0.6 %copy-done.6 = f32[128]{0:T(128)S(1)} copy-done((f32[128]{0:T(128)S(1)}, f32[128]{0:T(128)}, u32[]{:S(2)}) %copy-start.6) | copy-done | bytes 536
  28.6 0.0 copy-done.7
  28.6 0.0 copy-done.8
  28.7 1.6 %second.1 = bf16[4,256,128]{2,1,0:T(8,128)(2,1)} custom-call(f32[16,2,128]{2,1,0:T(2,128)S(1)} %all_to_all.11.sums_ref, bf16[6,256,128]{2,1,0:T(8,128)(2,1)S(1)} %get-tuple-element.14.hidden_ref, bf16[4,256,128]{2,1,0:T(8,128)(2,1)S(1)} %bitcast.12, bf16[3,9,128,128]{3,2,1,0:T(8,128)(2,1)S(1)} %bitcast.14, f32[1,128]{1,0:T(1,128)S(1)} %bitcast.18, ...), custom_call_target="tpu_custom_call" | custom-call | tf_op jit(solution)/shard_map/second/pallas_call | solution.py:230
Async XLA Ops:
  0.0 0.9 %copy-start = (bf16[1,4,256,128]{3,2,1,0:T(8,128)(2,1)S(1)}, bf16[1,4,256,128]{3,2,1,0:T(8,128)(2,1)}, u32[]{:S(2)}) copy-start(bf16[1,4,256,128]{3,2,1,0:T(8,128)(2,1)} %param.9) | copy-start | bytes 786436
  1.0 16.4 %copy-start.1 = (bf16[3,3,3,128,128]{4,3,2,1,0:T(8,128)(2,1)S(1)}, bf16[3,3,3,128,128]{4,3,2,1,0:T(8,128)(2,1)}, u32[]{:S(2)}) copy-start(bf16[3,3,3,128,128]{4,3,2,1,0:T(8,128)(2,1)} %param.12) | copy-start | bytes 2654212
  1.0 16.5 %copy-start.3 = (f32[128]{0:T(128)S(1)}, f32[128]{0:T(128)}, u32[]{:S(2)}) copy-start(f32[128]{0:T(128)} %param.13) | copy-start | bytes 1540
  1.0 16.5 %copy-start.4 = (f32[128]{0:T(128)S(1)}, f32[128]{0:T(128)}, u32[]{:S(2)}) copy-start(f32[128]{0:T(128)} %param.10) | copy-start | bytes 1540
  1.0 16.5 %copy-start.5 = (f32[128]{0:T(128)S(1)}, f32[128]{0:T(128)}, u32[]{:S(2)}) copy-start(f32[128]{0:T(128)} %param.11) | copy-start | bytes 1540
  1.1 26.9 %copy-start.2 = (bf16[3,3,3,128,128]{4,3,2,1,0:T(8,128)(2,1)S(1)}, bf16[3,3,3,128,128]{4,3,2,1,0:T(8,128)(2,1)}, u32[]{:S(2)}) copy-start(bf16[3,3,3,128,128]{4,3,2,1,0:T(8,128)(2,1)} %param.16) | copy-start | bytes 2654212
  1.1 16.3 %collective-permute-start = (bf16[2,256,128]{2,1,0:T(8,128)(2,1)S(1)}, bf16[2,256,128]{2,1,0:T(8,128)(2,1)S(1)}, u32[]{:S(2)}, u32[]{:S(2)}) collective-permute-start(bf16[2,256,128]{2,1,0:T(8,128)(2,1)S(1)} %get-tuple-element.11), channel_id=1, source_target_pairs={{0,1},{1,0},{2,3},{3,2},{4,5},{5,4},{6,7},{7,6},{8,9},{9,8},{10,11... | collective-permute-start | bytes 393224 | tf_op jit(solution)/shard_map/ppermute | solution.py:215
  1.6 15.8 %collective-permute-start.1 = (bf16[2,256,128]{2,1,0:T(8,128)(2,1)S(1)}, bf16[2,256,128]{2,1,0:T(8,128)(2,1)S(1)}, u32[]{:S(2)}, u32[]{:S(2)}) collective-permute-start(bf16[2,256,128]{2,1,0:T(8,128)(2,1)S(1)} %get-tuple-element.12), channel_id=1, source_target_pairs={{1,2},{2,1},{3,4},{4,3},{5,6},{6,5},{7,8},{8,7},{9,10},{10,9},{11,... | collective-permute-start | bytes 393224 | tf_op jit(solution)/shard_map/ppermute | solution.py:214
  28.0 0.7 %copy-start.6 = (f32[128]{0:T(128)S(1)}, f32[128]{0:T(128)}, u32[]{:S(2)}) copy-start(f32[128]{0:T(128)} %param.17) | copy-start | bytes 1540
  28.0 0.7 %copy-start.7 = (f32[128]{0:T(128)S(1)}, f32[128]{0:T(128)}, u32[]{:S(2)}) copy-start(f32[128]{0:T(128)} %param.14) | copy-start | bytes 1540
  28.0 0.7 %copy-start.8 = (f32[128]{0:T(128)S(1)}, f32[128]{0:T(128)}, u32[]{:S(2)}) copy-start(f32[128]{0:T(128)} %param.15) | copy-start | bytes 1540
where the time goes:
time: 30.5 us; the launch traced here: 30.2 us
  blocking collectives  24.2 us (79%)
  Pallas kernels  3.19 us (10%)
  local copies, waits for them, and re-layouts  1.65 us (5%)
  starting transfers between devices  1.17 us (4%)
    all_to_all x2, blocking collectives, exchanged(): return lax.all_to_all(sums, 'rows', 0, 0)  24.2 us
    unnamed x18, local copies, waits for them, and re-layouts  1.65 us
    pallas_call x1, Pallas kernels, body(): pl.pallas_call(functools.partial(second_kernel, count), out_shape=jax.Sha...  1.59 us
    pallas_call x1, Pallas kernels, body(): pl.pallas_call(functools.partial(first_kernel, count), out_shape=[jax.Sha...  1.46 us
    ppermute x1, starting transfers between devices, body(): other = lax.ppermute(other, 'rows', swap_other)  0.66 us
  transfers between devices with their start and end apart: 2, of which 0 were waited for; matrix products, arithmetic and copies ran while one was open for 0% of the time, Pallas kernels for 0%

commit v1 on v0

--- a/solution.py
+++ b/solution.py
@@ -8,6 +8,7 @@
 from jax.sharding import PartitionSpec as P
 
 GROUPS = 32
+HBM = pl.BlockSpec(memory_space=pltpu.HBM)
 ANY = pl.BlockSpec(memory_space=pl.ANY)
 VMEM = pl.BlockSpec(memory_space=pltpu.VMEM)
 PARAMS = pltpu.CompilerParams(vmem_limit_bytes=24 * 1024 * 1024)
@@ -111,8 +112,15 @@
 
 def first_kernel(
     count, sums_ref, own_ref, pair_ref, other_ref, weight_ref, bias_ref, gain_ref, shift_ref,
-    hidden_ref, out_ref, wide_ref, taps_ref, summed_ref,
+    bias_two_ref, gain_two_ref, shift_two_ref,
+    hidden_ref, out_ref, next_ref, wide_ref, taps_ref, summed_ref, vectors_ref, sems,
 ):
+    copies = [
+        pltpu.make_async_copy(source, vectors_ref.at[i], sems.at[i])
+        for i, source in enumerate((bias_two_ref, gain_two_ref, shift_two_ref))
+    ]
+    for copy in copies:
+        copy.start()
     index = lax.axis_index("rows")
     rows, width, channels = own_ref.shape
     even = index % 2 == 0
@@ -142,6 +150,9 @@
         if 0 < row <= rows:
             total, square = add_sums(values.astype(jnp.float32), total, square)
     store_sums(total, square, out_ref)
+    for i in range(3):
+        copies[i].wait()
+        next_ref[pl.ds(i, 1), :] = vectors_ref[i]
 
     @pl.when(index == 0)
     def _():
@@ -153,11 +164,13 @@
 
 
 def second_kernel(
-    count, sums_ref, hidden_ref, own_ref, weight_ref, bias_ref, gain_ref, shift_ref,
+    count, sums_ref, hidden_ref, own_ref, weight_ref, params_ref,
     out_ref, wide_ref, taps_ref, summed_ref, done_ref, sems,
 ):
     rows, width, channels = own_ref.shape
-    scale, offset = scale_offset(sums_ref, gain_ref, shift_ref, rows * width * count)
+    scale, offset = scale_offset(
+        sums_ref, params_ref.at[1:2], params_ref.at[2:3], rows * width * count
+    )
     sum_paired(weight_ref, summed_ref)
     copies = [
         pltpu.make_async_copy(done_ref.at[row], out_ref.at[row], sems.at[row])
@@ -171,7 +184,7 @@
         window = jnp.concatenate([taps_ref[row + tap] for tap in range(4)], axis=1)
         both = jnp.dot(window, summed_ref[...], preferred_element_type=jnp.float32)
         for i in range(2):
-            branch = both[:, i * channels : (i + 1) * channels] + bias_ref[...]
+            branch = both[:, i * channels : (i + 1) * channels] + params_ref[0:1, :]
             values = own_ref[row + i].astype(jnp.float32) + branch
             done_ref[row + i] = values.astype(jnp.bfloat16)
             copies[row + i].start()
@@ -193,9 +206,8 @@
     taps = weight_one.shape[1] * weight_one.shape[2]
     slab_shape = jax.ShapeDtypeStruct((2, width, channels), jnp.bfloat16)
 
-    def operands(weight, *vectors):
-        vectors = [vector.reshape(1, channels) for vector in vectors]
-        return weight.reshape(3, taps, channels, channels), *vectors
+    def raw(weight):
+        return weight.reshape(3, taps, channels, channels)
 
     swap_pair = [(i, i ^ 1) for i in range(count)]
     swap_other = [(i, i + 1 if i % 2 else i - 1) for i in range(1, count - 1)]
@@ -214,23 +226,40 @@
     other = lax.ppermute(other, "rows", swap_other)
     pair = lax.ppermute(pair, "rows", swap_pair)
     sums = exchanged(sums)
-    hidden, sums = pl.pallas_call(
+    hidden, sums, params = pl.pallas_call(
         functools.partial(first_kernel, count),
-        out_shape=[jax.ShapeDtypeStruct((rows + 2, width, channels), jnp.bfloat16), sums_shape],
-        in_specs=[VMEM] * 8,
-        out_specs=[VMEM] * 2,
+        out_shape=[
+            jax.ShapeDtypeStruct((rows + 2, width, channels), jnp.bfloat16),
+            sums_shape,
+            jax.ShapeDtypeStruct((8, channels), jnp.float32),
+        ],
+        in_specs=[VMEM] * 8 + [HBM] * 3,
+        out_specs=[VMEM] * 3,
         scratch_shapes=[
             pltpu.VMEM((rows + 4, width + 16, channels), jnp.float32),
             pltpu.VMEM((rows + 4, width, 3 * channels), jnp.bfloat16),
             pltpu.VMEM((taps * channels, 2 * channels), jnp.bfloat16),
+            pltpu.VMEM((3, 1, channels), jnp.float32),
+            pltpu.SemaphoreType.DMA((3,)),
         ],
         compiler_params=PARAMS, name="first",
-    )(sums, own, pair, other, *operands(weight_one, bias_one, gain_one, shift_one))
+    )(
+        sums,
+        own,
+        pair,
+        other,
+        raw(weight_one),
+        *[vector.reshape(1, channels) for vector in (bias_one, gain_one, shift_one)],
+        *[
+            pltpu.with_memory_space_constraint(vector.reshape(1, channels), pltpu.HBM)
+            for vector in (bias_two, gain_two, shift_two)
+        ],
+    )
     sums = exchanged(sums)
     decoded = pl.pallas_call(
         functools.partial(second_kernel, count),
         out_shape=jax.ShapeDtypeStruct(own.shape, jnp.bfloat16),
-        in_specs=[VMEM] * 7,
+        in_specs=[VMEM] * 5,
         out_specs=ANY,
         scratch_shapes=[
             pltpu.VMEM((rows + 2, width + 16, channels), jnp.float32),
@@ -240,7 +269,7 @@
             pltpu.SemaphoreType.DMA((rows,)),
         ],
         compiler_params=PARAMS, name="second",
-    )(sums, hidden, own, *operands(weight_two, bias_two, gain_two, shift_two))
+    )(sums, hidden, own, raw(weight_two), params)
     return decoded[None]
 
 

time: 30.5 us -> 29.8 us (0.977)
  local copies, waits for them, and re-layouts: 1.65 us -> 0.97 us
    unnamed x18 -> x12, local copies, waits for them, and re-layouts: 1.65 us -> 0.97 us
where the time goes in v1:
time: 29.8 us; the launch traced here: 29.6 us
  blocking collectives  24.2 us (81%)
  Pallas kernels  3.22 us (11%)
  starting transfers between devices  1.17 us (4%)
  local copies, waits for them, and re-layouts  0.97 us (3%)
    all_to_all x2, blocking collectives, exchanged(): return lax.all_to_all(sums, 'rows', 0, 0)  24.2 us
    pallas_call x1, Pallas kernels, body(): pl.pallas_call(functools.partial(second_kernel, count), out_shape=jax.Sha...  1.58 us
    pallas_call x1, Pallas kernels, body(): pl.pallas_call(functools.partial(first_kernel, count), out_shape=[jax.Sha...  1.49 us
    unnamed x12, local copies, waits for them, and re-layouts  0.97 us
    ppermute x1, starting transfers between devices, body(): other = lax.ppermute(other, 'rows', swap_other)  0.66 us
  transfers between devices with their start and end apart: 2, of which 0 were waited for; matrix products, arithmetic and copies ran while one was open for 0% of the time, Pallas kernels for 0%

profile of v1, /device:TPU:0, one launch (start us, length us, event | category | flops | bytes accessed | tf_op | source)
XLA Modules:
  0.0 29.6 jit_solution(16768335176289115976)
XLA Ops:
  0.0 0.0 copy-start
  0.0 0.9 %copy-done = bf16[1,4,256,128]{3,2,1,0:T(8,128)(2,1)S(1)} copy-done((bf16[1,4,256,128]{3,2,1,0:T(8,128)(2,1)S(1)}, bf16[1,4,256,128]{3,2,1,0:T(8,128)(2,1)}, u32[]{:S(2)}) %copy-start) | copy-done | bytes 262168
  1.0 0.0 copy-start.1
  1.0 0.0 copy-start.3
  1.0 0.0 copy-start.4
  1.0 0.0 copy-start.5
  1.0 0.1 sums.1
  1.1 0.0 copy-start.2
  1.1 0.5 %collective-permute-start = (bf16[2,256,128]{2,1,0:T(8,128)(2,1)S(1)}, bf16[2,256,128]{2,1,0:T(8,128)(2,1)S(1)}, u32[]{:S(2)}, u32[]{:S(2)}) collective-permute-start(bf16[2,256,128]{2,1,0:T(8,128)(2,1)S(1)} %get-tuple-element.12), channel_id=1, source_target_pairs={{0,1},{1,0},{2,3},{3,2},{4,5},{5,4},{6,7},{7,6},{8,9},{9,8},{10,11... | collective-permute-start | bytes 393224 | tf_op jit(solution)/shard_map/ppermute | solution.py:227
  1.6 0.7 %collective-permute-start.1 = (bf16[2,256,128]{2,1,0:T(8,128)(2,1)S(1)}, bf16[2,256,128]{2,1,0:T(8,128)(2,1)S(1)}, u32[]{:S(2)}, u32[]{:S(2)}) collective-permute-start(bf16[2,256,128]{2,1,0:T(8,128)(2,1)S(1)} %get-tuple-element.13), channel_id=1, source_target_pairs={{1,2},{2,1},{3,4},{4,3},{5,6},{6,5},{7,8},{8,7},{9,10},{10,9},{11,... | collective-permute-start | bytes 393224 | tf_op jit(solution)/shard_map/ppermute | solution.py:226
  2.3 15.1 %all_to_all.10.sums_ref = f32[16,2,128]{2,1,0:T(2,128)S(1)} all-to-all(f32[16,2,128]{2,1,0:T(2,128)S(1)} %get-tuple-element.11), channel_id=1, replica_groups=mesh['groups'=2,'rows'=16] {'rows'}, dimensions={0} | all-to-all | bytes 32768 | tf_op jit(solution)/shard_map/all_to_all | solution.py:196
  17.4 0.0 collective-permute-done.pair_ref
  17.4 0.0 collective-permute-done.1.other_ref
  17.4 0.0 copy-done.1
  17.4 0.0 copy-done.3
  17.4 0.0 copy-done.4
  17.4 0.0 copy-done.5
  17.4 1.5 %first.1 = (bf16[6,256,128]{2,1,0:T(8,128)(2,1)S(1)}, f32[16,2,128]{2,1,0:T(2,128)S(1)}, f32[8,128]{1,0:T(8,128)S(1)}) custom-call(f32[16,2,128]{2,1,0:T(2,128)S(1)} %all_to_all.10.sums_ref, bf16[4,256,128]{2,1,0:T(8,128)(2,1)S(1)} %bitcast.11, bf16[2,256,128]{2,1,0:T(8,128)(2,1)S(1)} %collective-permute-done.pair_ref, ...), custom_call_target="tpu_custom_call" | custom-call | tf_op jit(solution)/shard_map/first/pallas_call | solution.py:229
  18.9 9.1 %all_to_all.11.sums_ref = f32[16,2,128]{2,1,0:T(2,128)S(1)} all-to-all(f32[16,2,128]{2,1,0:T(2,128)S(1)} %get-tuple-element.14), channel_id=1, replica_groups=mesh['groups'=2,'rows'=16] {'rows'}, dimensions={0} | all-to-all | bytes 32768 | tf_op jit(solution)/shard_map/all_to_all | solution.py:196
  28.0 0.0 copy-done.2
  28.0 1.6 %second.1 = bf16[4,256,128]{2,1,0:T(8,128)(2,1)} custom-call(f32[16,2,128]{2,1,0:T(2,128)S(1)} %all_to_all.11.sums_ref, bf16[6,256,128]{2,1,0:T(8,128)(2,1)S(1)} %get-tuple-element.15.hidden_ref, bf16[4,256,128]{2,1,0:T(8,128)(2,1)S(1)} %bitcast.12, bf16[3,9,128,128]{3,2,1,0:T(8,128)(2,1)S(1)} %bitcast.14, f32[8,128]{1,0:T(8,128)S(1)} %get-tuple-element.16.params_ref), custom_call_target="tpu_custom_call" | custom-call | tf_op jit(solution)/shard_map/second/pallas_call | solution.py:259
Async XLA Ops:
  0.0 0.9 %copy-start = (bf16[1,4,256,128]{3,2,1,0:T(8,128)(2,1)S(1)}, bf16[1,4,256,128]{3,2,1,0:T(8,128)(2,1)}, u32[]{:S(2)}) copy-start(bf16[1,4,256,128]{3,2,1,0:T(8,128)(2,1)} %param.9) | copy-start | bytes 786436
  1.0 16.4 %copy-start.1 = (bf16[3,3,3,128,128]{4,3,2,1,0:T(8,128)(2,1)S(1)}, bf16[3,3,3,128,128]{4,3,2,1,0:T(8,128)(2,1)}, u32[]{:S(2)}) copy-start(bf16[3,3,3,128,128]{4,3,2,1,0:T(8,128)(2,1)} %param.12) | copy-start | bytes 2654212
  1.0 16.5 %copy-start.3 = (f32[128]{0:T(128)S(1)}, f32[128]{0:T(128)}, u32[]{:S(2)}) copy-start(f32[128]{0:T(128)} %param.13) | copy-start | bytes 1540
  1.0 16.5 %copy-start.4 = (f32[128]{0:T(128)S(1)}, f32[128]{0:T(128)}, u32[]{:S(2)}) copy-start(f32[128]{0:T(128)} %param.10) | copy-start | bytes 1540
  1.0 16.5 %copy-start.5 = (f32[128]{0:T(128)S(1)}, f32[128]{0:T(128)}, u32[]{:S(2)}) copy-start(f32[128]{0:T(128)} %param.11) | copy-start | bytes 1540
  1.1 26.9 %copy-start.2 = (bf16[3,3,3,128,128]{4,3,2,1,0:T(8,128)(2,1)S(1)}, bf16[3,3,3,128,128]{4,3,2,1,0:T(8,128)(2,1)}, u32[]{:S(2)}) copy-start(bf16[3,3,3,128,128]{4,3,2,1,0:T(8,128)(2,1)} %param.16) | copy-start | bytes 2654212
  1.1 16.3 %collective-permute-start = (bf16[2,256,128]{2,1,0:T(8,128)(2,1)S(1)}, bf16[2,256,128]{2,1,0:T(8,128)(2,1)S(1)}, u32[]{:S(2)}, u32[]{:S(2)}) collective-permute-start(bf16[2,256,128]{2,1,0:T(8,128)(2,1)S(1)} %get-tuple-element.12), channel_id=1, source_target_pairs={{0,1},{1,0},{2,3},{3,2},{4,5},{5,4},{6,7},{7,6},{8,9},{9,8},{10,11... | collective-permute-start | bytes 393224 | tf_op jit(solution)/shard_map/ppermute | solution.py:227
  1.6 15.8 %collective-permute-start.1 = (bf16[2,256,128]{2,1,0:T(8,128)(2,1)S(1)}, bf16[2,256,128]{2,1,0:T(8,128)(2,1)S(1)}, u32[]{:S(2)}, u32[]{:S(2)}) collective-permute-start(bf16[2,256,128]{2,1,0:T(8,128)(2,1)S(1)} %get-tuple-element.13), channel_id=1, source_target_pairs={{1,2},{2,1},{3,4},{4,3},{5,6},{6,5},{7,8},{8,7},{9,10},{10,9},{11,... | collective-permute-start | bytes 393224 | tf_op jit(solution)/shard_map/ppermute | solution.py:226

commit v2 on v1

--- a/solution.py
+++ b/solution.py
@@ -11,6 +11,7 @@
 HBM = pl.BlockSpec(memory_space=pltpu.HBM)
 ANY = pl.BlockSpec(memory_space=pl.ANY)
 VMEM = pl.BlockSpec(memory_space=pltpu.VMEM)
+LONG = pl.CostEstimate(flops=40000000000, bytes_accessed=10000000, transcendentals=0)
 PARAMS = pltpu.CompilerParams(vmem_limit_bytes=24 * 1024 * 1024)
 
 
@@ -29,14 +30,23 @@
     return total, square
 
 
-def sums_kernel(own_ref, out_ref, pair_ref, other_ref):
+def slabs_kernel(latents_ref, pair_ref, other_ref, sems):
+    even = 1 - lax.axis_index("rows") % 2
+    last = latents_ref.shape[0] - 2
+    copies = [
+        pltpu.make_async_copy(latents_ref.at[pl.ds(start, 2)], target, sems.at[i])
+        for i, (start, target) in enumerate(
+            ((last * even, pair_ref), (last * (1 - even), other_ref))
+        )
+    ]
+    for copy in copies:
+        copy.start()
+    for copy in copies:
+        copy.wait()
+
+
+def sums_kernel(own_ref, out_ref):
     rows, _, channels = own_ref.shape
-    even = lax.axis_index("rows") % 2 == 0
-    for row in range(2):
-        top = own_ref[row]
-        bottom = own_ref[rows - 2 + row]
-        pair_ref[row] = jnp.where(even, bottom, top)
-        other_ref[row] = jnp.where(even, top, bottom)
     total = jnp.zeros((8, channels), jnp.float32)
     square = jnp.zeros((8, channels), jnp.float32)
     for row in range(rows):
@@ -212,16 +222,24 @@
     swap_pair = [(i, i ^ 1) for i in range(count)]
     swap_other = [(i, i + 1 if i % 2 else i - 1) for i in range(1, count - 1)]
 
-    sums, pair, other = pl.pallas_call(
+    pair, other = pl.pallas_call(
+        slabs_kernel,
+        out_shape=[slab_shape] * 2,
+        in_specs=[HBM],
+        out_specs=[VMEM] * 2,
+        scratch_shapes=[pltpu.SemaphoreType.DMA((2,))],
+        compiler_params=PARAMS,
+        name="slabs",
+        cost_estimate=LONG,
+    )(pltpu.with_memory_space_constraint(own, pltpu.HBM))
+    sums = pl.pallas_call(
         sums_kernel,
-        out_shape=[sums_shape, slab_shape, slab_shape],
+        out_shape=sums_shape,
         in_specs=[VMEM],
-        out_specs=[VMEM] * 3,
+        out_specs=VMEM,
         compiler_params=PARAMS,
         name="sums",
-        cost_estimate=pl.CostEstimate(
-            flops=40000000000, bytes_accessed=10000000, transcendentals=0
-        ),
+        cost_estimate=LONG,
     )(own)
     other = lax.ppermute(other, "rows", swap_other)
     pair = lax.ppermute(pair, "rows", swap_pair)

time: 29.8 us -> 30.1 us (1.010)
  Pallas kernels: 3.22 us -> 4.19 us
  local copies, waits for them, and re-layouts: 0.97 us -> 0.03 us
    pallas_call x1 -> x2, Pallas kernels: 0.14 us -> 1.11 us  [the longest x1 1.03 us: body(): pl.pallas_call(slabs_kernel, out_shape=[slab_shape] * 2, in_specs=[HBM],...]
    unnamed x12, local copies, waits for them, and re-layouts: 0.97 us -> 0.03 us
where the time goes in v2:
time: 30.1 us; the launch traced here: 29.9 us
  blocking collectives  24.3 us (81%)
  Pallas kernels  4.19 us (14%)
  starting transfers between devices  1.31 us (4%)
    all_to_all x2, blocking collectives, exchanged(): return lax.all_to_all(sums, 'rows', 0, 0)  24.3 us
    pallas_call x1, Pallas kernels, body(): pl.pallas_call(functools.partial(second_kernel, count), out_shape=jax.Sha...  1.58 us
    pallas_call x1, Pallas kernels, body(): pl.pallas_call(functools.partial(first_kernel, count), out_shape=[jax.Sha...  1.49 us
    pallas_call x1, Pallas kernels, body(): pl.pallas_call(slabs_kernel, out_shape=[slab_shape] * 2, in_specs=[HBM],...  1.03 us
    ppermute x1, starting transfers between devices, body(): other = lax.ppermute(other, 'rows', swap_other)  0.79 us
  transfers between devices with their start and end apart: 2, of which 0 were waited for; matrix products, arithmetic and copies ran while one was open for 0% of the time, Pallas kernels for 0%

profile of v2, /device:TPU:0, one launch (start us, length us, event | category | flops | bytes accessed | tf_op | source)
XLA Modules:
  0.0 29.9 jit_solution(3740857752966569563)
XLA Ops:
  0.0 0.0 copy-start
  0.0 1.0 %slabs.1 = (bf16[2,256,128]{2,1,0:T(8,128)(2,1)S(1)}, bf16[2,256,128]{2,1,0:T(8,128)(2,1)S(1)}) custom-call(bf16[4,256,128]{2,1,0:T(8,128)(2,1)} %bitcast.10), custom_call_target="tpu_custom_call" | custom-call | flops 40000000000 | bytes 10000000 | tf_op jit(solution)/shard_map/slabs/pallas_call | solution.py:225
  1.0 0.5 %collective-permute-start = (bf16[2,256,128]{2,1,0:T(8,128)(2,1)S(1)}, bf16[2,256,128]{2,1,0:T(8,128)(2,1)S(1)}, u32[]{:S(2)}, u32[]{:S(2)}) collective-permute-start(bf16[2,256,128]{2,1,0:T(8,128)(2,1)S(1)} %get-tuple-element.10), channel_id=1, source_target_pairs={{0,1},{1,0},{2,3},{3,2},{4,5},{5,4},{6,7},{7,6},{8,9},{9,8},{10,11... | collective-permute-start | bytes 393224 | tf_op jit(solution)/shard_map/ppermute | solution.py:245
  1.6 0.0 copy-start.1
  1.6 0.8 %collective-permute-start.1 = (bf16[2,256,128]{2,1,0:T(8,128)(2,1)S(1)}, bf16[2,256,128]{2,1,0:T(8,128)(2,1)S(1)}, u32[]{:S(2)}, u32[]{:S(2)}) collective-permute-start(bf16[2,256,128]{2,1,0:T(8,128)(2,1)S(1)} %get-tuple-element.11), channel_id=1, source_target_pairs={{1,2},{2,1},{3,4},{4,3},{5,6},{6,5},{7,8},{8,7},{9,10},{10,9},{11,... | collective-permute-start | bytes 393224 | tf_op jit(solution)/shard_map/ppermute | solution.py:244
  2.4 0.0 copy-done
  2.4 0.0 copy-start.3
  2.4 0.0 copy-start.4
  2.4 0.0 copy-start.5
  2.4 0.1 sums.1
  2.5 0.0 copy-start.2
  2.5 15.2 %all_to_all.10.sums_ref = f32[16,2,128]{2,1,0:T(2,128)S(1)} all-to-all(f32[16,2,128]{2,1,0:T(2,128)S(1)} %sums.1), channel_id=1, replica_groups=mesh['groups'=2,'rows'=16] {'rows'}, dimensions={0} | all-to-all | bytes 32768 | tf_op jit(solution)/shard_map/all_to_all | solution.py:206
  17.7 0.0 collective-permute-done.pair_ref
  17.7 0.0 collective-permute-done.1.other_ref
  17.7 0.0 copy-done.1
  17.7 0.0 copy-done.3
  17.7 0.0 copy-done.4
  17.8 0.0 copy-done.5
  17.8 1.5 %first.1 = (bf16[6,256,128]{2,1,0:T(8,128)(2,1)S(1)}, f32[16,2,128]{2,1,0:T(2,128)S(1)}, f32[8,128]{1,0:T(8,128)S(1)}) custom-call(f32[16,2,128]{2,1,0:T(2,128)S(1)} %all_to_all.10.sums_ref, bf16[4,256,128]{2,1,0:T(8,128)(2,1)S(1)} %bitcast.12, bf16[2,256,128]{2,1,0:T(8,128)(2,1)S(1)} %collective-permute-done.pair_ref, ...), custom_call_target="tpu_custom_call" | custom-call | tf_op jit(solution)/shard_map/first/pallas_call | solution.py:247
  19.3 9.1 %all_to_all.11.sums_ref = f32[16,2,128]{2,1,0:T(2,128)S(1)} all-to-all(f32[16,2,128]{2,1,0:T(2,128)S(1)} %get-tuple-element.12), channel_id=1, replica_groups=mesh['groups'=2,'rows'=16] {'rows'}, dimensions={0} | all-to-all | bytes 32768 | tf_op jit(solution)/shard_map/all_to_all | solution.py:206
  28.3 0.0 copy-done.2
  28.3 1.6 %second.1 = bf16[4,256,128]{2,1,0:T(8,128)(2,1)} custom-call(f32[16,2,128]{2,1,0:T(2,128)S(1)} %all_to_all.11.sums_ref, bf16[6,256,128]{2,1,0:T(8,128)(2,1)S(1)} %get-tuple-element.13.hidden_ref, bf16[4,256,128]{2,1,0:T(8,128)(2,1)S(1)} %bitcast.13, bf16[3,9,128,128]{3,2,1,0:T(8,128)(2,1)S(1)} %bitcast.15, f32[8,128]{1,0:T(8,128)S(1)} %get-tuple-element.14.params_ref), custom_call_target="tpu_custom_call" | custom-call | tf_op jit(solution)/shard_map/second/pallas_call | solution.py:277
Async XLA Ops:
  0.0 2.4 %copy-start = (bf16[1,4,256,128]{3,2,1,0:T(8,128)(2,1)S(1)}, bf16[1,4,256,128]{3,2,1,0:T(8,128)(2,1)}, u32[]{:S(2)}) copy-start(bf16[1,4,256,128]{3,2,1,0:T(8,128)(2,1)} %param.9) | copy-start | bytes 786436
  1.0 16.7 %collective-permute-start = (bf16[2,256,128]{2,1,0:T(8,128)(2,1)S(1)}, bf16[2,256,128]{2,1,0:T(8,128)(2,1)S(1)}, u32[]{:S(2)}, u32[]{:S(2)}) collective-permute-start(bf16[2,256,128]{2,1,0:T(8,128)(2,1)S(1)} %get-tuple-element.10), channel_id=1, source_target_pairs={{0,1},{1,0},{2,3},{3,2},{4,5},{5,4},{6,7},{7,6},{8,9},{9,8},{10,11... | collective-permute-start | bytes 393224 | tf_op jit(solution)/shard_map/ppermute | solution.py:245
  1.6 16.2 %copy-start.1 = (bf16[3,3,3,128,128]{4,3,2,1,0:T(8,128)(2,1)S(1)}, bf16[3,3,3,128,128]{4,3,2,1,0:T(8,128)(2,1)}, u32[]{:S(2)}) copy-start(bf16[3,3,3,128,128]{4,3,2,1,0:T(8,128)(2,1)} %param.12) | copy-start | bytes 2654212
  1.6 16.2 %collective-permute-start.1 = (bf16[2,256,128]{2,1,0:T(8,128)(2,1)S(1)}, bf16[2,256,128]{2,1,0:T(8,128)(2,1)S(1)}, u32[]{:S(2)}, u32[]{:S(2)}) collective-permute-start(bf16[2,256,128]{2,1,0:T(8,128)(2,1)S(1)} %get-tuple-element.11), channel_id=1, source_target_pairs={{1,2},{2,1},{3,4},{4,3},{5,6},{6,5},{7,8},{8,7},{9,10},{10,9},{11,... | collective-permute-start | bytes 393224 | tf_op jit(solution)/shard_map/ppermute | solution.py:244
  2.4 15.4 %copy-start.3 = (f32[128]{0:T(128)S(1)}, f32[128]{0:T(128)}, u32[]{:S(2)}) copy-start(f32[128]{0:T(128)} %param.13) | copy-start | bytes 1540
  2.4 15.4 %copy-start.4 = (f32[128]{0:T(128)S(1)}, f32[128]{0:T(128)}, u32[]{:S(2)}) copy-start(f32[128]{0:T(128)} %param.10) | copy-start | bytes 1540
  2.4 15.4 %copy-start.5 = (f32[128]{0:T(128)S(1)}, f32[128]{0:T(128)}, u32[]{:S(2)}) copy-start(f32[128]{0:T(128)} %param.11) | copy-start | bytes 1540
  2.5 25.8 %copy-start.2 = (bf16[3,3,3,128,128]{4,3,2,1,0:T(8,128)(2,1)S(1)}, bf16[3,3,3,128,128]{4,3,2,1,0:T(8,128)(2,1)}, u32[]{:S(2)}) copy-start(bf16[3,3,3,128,128]{4,3,2,1,0:T(8,128)(2,1)} %param.16) | copy-start | bytes 2654212

commit v3 on v1

--- a/solution.py
+++ b/solution.py
@@ -87,25 +87,49 @@
     return 0.5 * scale, 0.5 * (shift_ref[...] - mean * scale)
 
 
-def store_taps(values, scale, offset, wide_ref, taps_ref, row):
-    width, channels = values.shape
+def activated(values, scale, offset):
     half = values.astype(jnp.float32) * scale + offset
-    act = half * jnp.tanh(half) + half
-    wide_ref[row, 8 : 8 + width, :] = act
-    wide_ref[row, 7:8, :] = act[0:1]
-    wide_ref[row, 8 + width : 9 + width, :] = act[width - 1 : width]
-    for tap in range(3):
-        shifted = wide_ref[row, 7 + tap : 7 + tap + width, :]
-        taps_ref[row, :, tap * channels : (tap + 1) * channels] = shifted.astype(jnp.bfloat16)
+    return half * jnp.tanh(half) + half
+
+
+def store_blocks(blocks, taps_ref, row):
+    leads = len(blocks)
+    first, final = blocks[0], blocks[-1]
+    sublane = lax.broadcasted_iota(jnp.int32, first.shape, 0)
+    before = jnp.where(sublane == 0, first, pltpu.roll(final, 1, 0))
+    after = jnp.where(sublane == 15, final, pltpu.roll(first, 15, 0))
+    for lead, block in enumerate([before] + blocks + [after]):
+        taps_ref[row, lead * 16 : (lead + 1) * 16, :] = block.astype(jnp.bfloat16)
+
+
+def store_natural(values, scale, offset, wide_ref, taps_ref, row):
+    leads = values.shape[0] // 16
+    wide_ref[row] = activated(values, scale, offset)
+    blocks = [wide_ref[row, pl.ds(lead, 16, stride=leads), :] for lead in range(leads)]
+    store_blocks(blocks, taps_ref, row)
+
+
+def store_permuted(values, scale, offset, taps_ref, row):
+    leads = values.shape[0] // 16
+    act = activated(values, scale, offset)
+    blocks = [act[lead * 16 : (lead + 1) * 16] for lead in range(leads)]
+    store_blocks(blocks, taps_ref, row)
+
+
+def window(taps_ref, row, count, taps):
+    width, lanes = taps_ref.shape[1] - 32, taps_ref.shape[2]
+    parts = [
+        taps_ref[row + tap : row + tap + count, 16 * column : 16 * column + width, :]
+        for tap in range(taps)
+        for column in range(3)
+    ]
+    return jnp.concatenate([part.reshape(count * width, lanes) for part in parts], axis=1)
 
 
 def conv_rows(taps_ref, row, count, weight_ref):
-    _, width, lanes = taps_ref.shape
-    window = jnp.concatenate(
-        [taps_ref[row + tap : row + tap + count].reshape(count * width, lanes) for tap in range(3)],
-        axis=1,
+    both = jnp.dot(
+        window(taps_ref, row, count, 3), weight_ref[...], preferred_element_type=jnp.float32
     )
-    both = jnp.dot(window, weight_ref[...], preferred_element_type=jnp.float32)
     half = both.shape[1] // 2
     return both[:, :half] + both[:, half:]
 
@@ -136,7 +160,7 @@
         else:
             values = jnp.where(even, pair_ref[row - rows - 2], other_ref[row - rows - 2])
             values = jnp.where(index == count - 1, own_ref[rows - 1], values)
-        store_taps(values, scale, offset, wide_ref, taps_ref, row)
+        store_natural(values, scale, offset, wide_ref, taps_ref, row)
 
     total = jnp.zeros((8, channels), jnp.float32)
     square = jnp.zeros((8, channels), jnp.float32)
@@ -177,15 +201,20 @@
         for row in range(rows)
     ]
     for row in range(2):
-        store_taps(hidden_ref[row], scale, offset, wide_ref, taps_ref, row)
+        store_permuted(hidden_ref[row], scale, offset, taps_ref, row)
     for row in range(0, rows, 2):
         for i in range(2, 4):
-            store_taps(hidden_ref[row + i], scale, offset, wide_ref, taps_ref, row + i)
-        window = jnp.concatenate([taps_ref[row + tap] for tap in range(4)], axis=1)
-        both = jnp.dot(window, summed_ref[...], preferred_element_type=jnp.float32)
+            store_permuted(hidden_ref[row + i], scale, offset, taps_ref, row + i)
+        both = jnp.dot(
+            window(taps_ref, row, 1, 4), summed_ref[...], preferred_element_type=jnp.float32
+        )
+        leads = width // 16
         for i in range(2):
             branch = both[:, i * channels : (i + 1) * channels] + params_ref[0:1, :]
-            values = own_ref[row + i].astype(jnp.float32) + branch
+            for lead in range(leads):
+                block = branch[lead * 16 : (lead + 1) * 16]
+                wide_ref[row + i, pl.ds(lead, 16, stride=leads), :] = block
+            values = own_ref[row + i].astype(jnp.float32) + wide_ref[row + i]
             done_ref[row + i] = values.astype(jnp.bfloat16)
             copies[row + i].start()
     for copy in copies:
@@ -236,8 +265,8 @@
         in_specs=[VMEM] * 8 + [HBM] * 3,
         out_specs=[VMEM] * 3,
         scratch_shapes=[
-            pltpu.VMEM((rows + 4, width + 16, channels), jnp.float32),
-            pltpu.VMEM((rows + 4, width, 3 * channels), jnp.bfloat16),
+            pltpu.VMEM((rows + 4, width, channels), jnp.float32),
+            pltpu.VMEM((rows + 4, width + 32, channels), jnp.bfloat16),
             pltpu.VMEM((taps * channels, 2 * channels), jnp.bfloat16),
             pltpu.VMEM((3, 1, channels), jnp.float32),
             pltpu.SemaphoreType.DMA((3,)),
@@ -262,8 +291,8 @@
         in_specs=[VMEM] * 5,
         out_specs=ANY,
         scratch_shapes=[
-            pltpu.VMEM((rows + 2, width + 16, channels), jnp.float32),
-            pltpu.VMEM((rows + 2, width, 3 * channels), jnp.bfloat16),
+            pltpu.VMEM((rows, width, channels), jnp.float32),
+            pltpu.VMEM((rows + 2, width + 32, channels), jnp.bfloat16),
             pltpu.VMEM((taps // 3 * 4 * channels, 2 * channels), jnp.bfloat16),
             pltpu.VMEM(own.shape, jnp.bfloat16),
             pltpu.SemaphoreType.DMA((rows,)),

time: 29.8 us -> 30.1 us (1.010)
  Pallas kernels: 3.22 us -> 3.55 us
where the time goes in v3:
time: 30.1 us; the launch traced here: 29.9 us
  blocking collectives  24.2 us (80%)
  Pallas kernels  3.55 us (12%)
  starting transfers between devices  1.17 us (4%)
  local copies, waits for them, and re-layouts  0.97 us (3%)
    all_to_all x2, blocking collectives, exchanged(): return lax.all_to_all(sums, 'rows', 0, 0)  24.2 us
    pallas_call x1, Pallas kernels, body(): pl.pallas_call(functools.partial(first_kernel, count), out_shape=[jax.Sha...  1.72 us
    pallas_call x1, Pallas kernels, body(): pl.pallas_call(functools.partial(second_kernel, count), out_shape=jax.Sha...  1.69 us
    unnamed x12, local copies, waits for them, and re-layouts  0.97 us
    ppermute x1, starting transfers between devices, body(): other = lax.ppermute(other, 'rows', swap_other)  0.66 us
  transfers between devices with their start and end apart: 2, of which 0 were waited for; matrix products, arithmetic and copies ran while one was open for 0% of the time, Pallas kernels for 0%

profile of v3, /device:TPU:0, one launch (start us, length us, event | category | flops | bytes accessed | tf_op | source)
XLA Modules:
  0.0 29.9 jit_solution(12352580289200731188)
XLA Ops:
  0.0 0.0 copy-start
  0.0 0.9 %copy-done = bf16[1,4,256,128]{3,2,1,0:T(8,128)(2,1)S(1)} copy-done((bf16[1,4,256,128]{3,2,1,0:T(8,128)(2,1)S(1)}, bf16[1,4,256,128]{3,2,1,0:T(8,128)(2,1)}, u32[]{:S(2)}) %copy-start) | copy-done | bytes 262168
  1.0 0.0 copy-start.1
  1.0 0.0 copy-start.3
  1.0 0.0 copy-start.4
  1.0 0.0 copy-start.5
  1.0 0.1 sums.1
  1.1 0.0 copy-start.2
  1.1 0.5 %collective-permute-start = (bf16[2,256,128]{2,1,0:T(8,128)(2,1)S(1)}, bf16[2,256,128]{2,1,0:T(8,128)(2,1)S(1)}, u32[]{:S(2)}, u32[]{:S(2)}) collective-permute-start(bf16[2,256,128]{2,1,0:T(8,128)(2,1)S(1)} %get-tuple-element.12), channel_id=1, source_target_pairs={{0,1},{1,0},{2,3},{3,2},{4,5},{5,4},{6,7},{7,6},{8,9},{9,8},{10,11... | collective-permute-start | bytes 393224 | tf_op jit(solution)/shard_map/ppermute | solution.py:256
  1.6 0.7 %collective-permute-start.1 = (bf16[2,256,128]{2,1,0:T(8,128)(2,1)S(1)}, bf16[2,256,128]{2,1,0:T(8,128)(2,1)S(1)}, u32[]{:S(2)}, u32[]{:S(2)}) collective-permute-start(bf16[2,256,128]{2,1,0:T(8,128)(2,1)S(1)} %get-tuple-element.13), channel_id=1, source_target_pairs={{1,2},{2,1},{3,4},{4,3},{5,6},{6,5},{7,8},{8,7},{9,10},{10,9},{11,... | collective-permute-start | bytes 393224 | tf_op jit(solution)/shard_map/ppermute | solution.py:255
  2.3 15.1 %all_to_all.10.sums_ref = f32[16,2,128]{2,1,0:T(2,128)S(1)} all-to-all(f32[16,2,128]{2,1,0:T(2,128)S(1)} %get-tuple-element.11), channel_id=1, replica_groups=mesh['groups'=2,'rows'=16] {'rows'}, dimensions={0} | all-to-all | bytes 32768 | tf_op jit(solution)/shard_map/all_to_all | solution.py:225
  17.4 0.0 collective-permute-done.pair_ref
  17.4 0.0 collective-permute-done.1.other_ref
  17.4 0.0 copy-done.1
  17.4 0.0 copy-done.3
  17.4 0.0 copy-done.4
  17.4 0.0 copy-done.5
  17.4 1.7 %first.1 = (bf16[6,256,128]{2,1,0:T(8,128)(2,1)S(1)}, f32[16,2,128]{2,1,0:T(2,128)S(1)}, f32[8,128]{1,0:T(8,128)S(1)}) custom-call(f32[16,2,128]{2,1,0:T(2,128)S(1)} %all_to_all.10.sums_ref, bf16[4,256,128]{2,1,0:T(8,128)(2,1)S(1)} %bitcast.11, bf16[2,256,128]{2,1,0:T(8,128)(2,1)S(1)} %collective-permute-done.pair_ref, ...), custom_call_target="tpu_custom_call" | custom-call | tf_op jit(solution)/shard_map/first/pallas_call | solution.py:258
  19.2 9.1 %all_to_all.11.sums_ref = f32[16,2,128]{2,1,0:T(2,128)S(1)} all-to-all(f32[16,2,128]{2,1,0:T(2,128)S(1)} %get-tuple-element.14), channel_id=1, replica_groups=mesh['groups'=2,'rows'=16] {'rows'}, dimensions={0} | all-to-all | bytes 32768 | tf_op jit(solution)/shard_map/all_to_all | solution.py:225
  28.2 0.0 copy-done.2
  28.2 1.7 %second.1 = bf16[4,256,128]{2,1,0:T(8,128)(2,1)} custom-call(f32[16,2,128]{2,1,0:T(2,128)S(1)} %all_to_all.11.sums_ref, bf16[6,256,128]{2,1,0:T(8,128)(2,1)S(1)} %get-tuple-element.15.hidden_ref, bf16[4,256,128]{2,1,0:T(8,128)(2,1)S(1)} %bitcast.12, bf16[3,9,128,128]{3,2,1,0:T(8,128)(2,1)S(1)} %bitcast.14, f32[8,128]{1,0:T(8,128)S(1)} %get-tuple-element.16.params_ref), custom_call_target="tpu_custom_call" | custom-call | tf_op jit(solution)/shard_map/second/pallas_call | solution.py:288
Async XLA Ops:
  0.0 0.9 %copy-start = (bf16[1,4,256,128]{3,2,1,0:T(8,128)(2,1)S(1)}, bf16[1,4,256,128]{3,2,1,0:T(8,128)(2,1)}, u32[]{:S(2)}) copy-start(bf16[1,4,256,128]{3,2,1,0:T(8,128)(2,1)} %param.9) | copy-start | bytes 786436
  1.0 16.4 %copy-start.1 = (bf16[3,3,3,128,128]{4,3,2,1,0:T(8,128)(2,1)S(1)}, bf16[3,3,3,128,128]{4,3,2,1,0:T(8,128)(2,1)}, u32[]{:S(2)}) copy-start(bf16[3,3,3,128,128]{4,3,2,1,0:T(8,128)(2,1)} %param.12) | copy-start | bytes 2654212
  1.0 16.5 %copy-start.3 = (f32[128]{0:T(128)S(1)}, f32[128]{0:T(128)}, u32[]{:S(2)}) copy-start(f32[128]{0:T(128)} %param.13) | copy-start | bytes 1540
  1.0 16.5 %copy-start.4 = (f32[128]{0:T(128)S(1)}, f32[128]{0:T(128)}, u32[]{:S(2)}) copy-start(f32[128]{0:T(128)} %param.10) | copy-start | bytes 1540
  1.0 16.5 %copy-start.5 = (f32[128]{0:T(128)S(1)}, f32[128]{0:T(128)}, u32[]{:S(2)}) copy-start(f32[128]{0:T(128)} %param.11) | copy-start | bytes 1540
  1.1 27.1 %copy-start.2 = (bf16[3,3,3,128,128]{4,3,2,1,0:T(8,128)(2,1)S(1)}, bf16[3,3,3,128,128]{4,3,2,1,0:T(8,128)(2,1)}, u32[]{:S(2)}) copy-start(bf16[3,3,3,128,128]{4,3,2,1,0:T(8,128)(2,1)} %param.16) | copy-start | bytes 2654212
  1.1 16.3 %collective-permute-start = (bf16[2,256,128]{2,1,0:T(8,128)(2,1)S(1)}, bf16[2,256,128]{2,1,0:T(8,128)(2,1)S(1)}, u32[]{:S(2)}, u32[]{:S(2)}) collective-permute-start(bf16[2,256,128]{2,1,0:T(8,128)(2,1)S(1)} %get-tuple-element.12), channel_id=1, source_target_pairs={{0,1},{1,0},{2,3},{3,2},{4,5},{5,4},{6,7},{7,6},{8,9},{9,8},{10,11... | collective-permute-start | bytes 393224 | tf_op jit(solution)/shard_map/ppermute | solution.py:256
  1.6 15.8 %collective-permute-start.1 = (bf16[2,256,128]{2,1,0:T(8,128)(2,1)S(1)}, bf16[2,256,128]{2,1,0:T(8,128)(2,1)S(1)}, u32[]{:S(2)}, u32[]{:S(2)}) collective-permute-start(bf16[2,256,128]{2,1,0:T(8,128)(2,1)S(1)} %get-tuple-element.13), channel_id=1, source_target_pairs={{1,2},{2,1},{3,4},{4,3},{5,6},{6,5},{7,8},{8,7},{9,10},{10,9},{11,... | collective-permute-start | bytes 393224 | tf_op jit(solution)/shard_map/ppermute | solution.py:255

commit v4 on v1

--- a/solution.py
+++ b/solution.py
@@ -193,7 +193,9 @@
 
 
 def exchanged(sums):
-    return lax.all_to_all(sums, "rows", 0, 0)
+    count = lax.axis_size("rows")
+    ends_first = [i // 2 if i % 2 == 0 else count - 1 - i // 2 for i in range(count)]
+    return lax.all_to_all(sums, "rows", 0, 0, axis_index_groups=[ends_first])
 
 
 def body(

time: 29.8 us -> 29.8 us (level)
  no operation moved by 1% of the time
where the time goes in v4:
time: 29.8 us; the launch traced here: 29.5 us
  blocking collectives  24.1 us (81%)
  Pallas kernels  3.21 us (11%)
  starting transfers between devices  1.17 us (4%)
  local copies, waits for them, and re-layouts  0.97 us (3%)
    all_to_all x2, blocking collectives, exchanged(): return lax.all_to_all(sums, 'rows', 0, 0, axis_index_groups=[ends_first])  24.1 us
    pallas_call x1, Pallas kernels, body(): pl.pallas_call(functools.partial(second_kernel, count), out_shape=jax.Sha...  1.58 us
    pallas_call x1, Pallas kernels, body(): pl.pallas_call(functools.partial(first_kernel, count), out_shape=[jax.Sha...  1.49 us
    unnamed x12, local copies, waits for them, and re-layouts  0.97 us
    ppermute x1, starting transfers between devices, body(): other = lax.ppermute(other, 'rows', swap_other)  0.66 us
  transfers between devices with their start and end apart: 2, of which 0 were waited for; matrix products, arithmetic and copies ran while one was open for 0% of the time, Pallas kernels for 0%

profile of v4, /device:TPU:0, one launch (start us, length us, event | category | flops | bytes accessed | tf_op | source)
XLA Modules:
  0.0 29.5 jit_solution(5708878172163390840)
XLA Ops:
  0.0 0.0 copy-start
  0.0 0.9 %copy-done = bf16[1,4,256,128]{3,2,1,0:T(8,128)(2,1)S(1)} copy-done((bf16[1,4,256,128]{3,2,1,0:T(8,128)(2,1)S(1)}, bf16[1,4,256,128]{3,2,1,0:T(8,128)(2,1)}, u32[]{:S(2)}) %copy-start) | copy-done | bytes 262168
  1.0 0.0 copy-start.1
  1.0 0.0 copy-start.3
  1.0 0.0 copy-start.4
  1.0 0.0 copy-start.5
  1.0 0.1 sums.1
  1.1 0.0 copy-start.2
  1.1 0.5 %collective-permute-start = (bf16[2,256,128]{2,1,0:T(8,128)(2,1)S(1)}, bf16[2,256,128]{2,1,0:T(8,128)(2,1)S(1)}, u32[]{:S(2)}, u32[]{:S(2)}) collective-permute-start(bf16[2,256,128]{2,1,0:T(8,128)(2,1)S(1)} %get-tuple-element.12), channel_id=1, source_target_pairs={{0,1},{1,0},{2,3},{3,2},{4,5},{5,4},{6,7},{7,6},{8,9},{9,8},{10,11... | collective-permute-start | bytes 393224 | tf_op jit(solution)/shard_map/ppermute | solution.py:229
  1.6 0.7 %collective-permute-start.1 = (bf16[2,256,128]{2,1,0:T(8,128)(2,1)S(1)}, bf16[2,256,128]{2,1,0:T(8,128)(2,1)S(1)}, u32[]{:S(2)}, u32[]{:S(2)}) collective-permute-start(bf16[2,256,128]{2,1,0:T(8,128)(2,1)S(1)} %get-tuple-element.13), channel_id=1, source_target_pairs={{1,2},{2,1},{3,4},{4,3},{5,6},{6,5},{7,8},{8,7},{9,10},{10,9},{11,... | collective-permute-start | bytes 393224 | tf_op jit(solution)/shard_map/ppermute | solution.py:228
  2.3 15.1 %all_to_all.10.sums_ref = f32[16,2,128]{2,1,0:T(2,128)S(1)} all-to-all(f32[16,2,128]{2,1,0:T(2,128)S(1)} %get-tuple-element.11), channel_id=1, replica_groups={{0,15,1,14,2,13,3,12,4,11,5,10,6,9,7,8},{16,31,17,30,18,29,19,28,20,27,..., dimensions={0} | all-to-all | bytes 32768 | tf_op jit(solution)/shard_map/all_to_all | solution.py:198
  17.4 0.0 collective-permute-done.pair_ref
  17.4 0.0 collective-permute-done.1.other_ref
  17.4 0.0 copy-done.1
  17.4 0.0 copy-done.3
  17.4 0.0 copy-done.4
  17.4 0.0 copy-done.5
  17.4 1.5 %first.1 = (bf16[6,256,128]{2,1,0:T(8,128)(2,1)S(1)}, f32[16,2,128]{2,1,0:T(2,128)S(1)}, f32[8,128]{1,0:T(8,128)S(1)}) custom-call(f32[16,2,128]{2,1,0:T(2,128)S(1)} %all_to_all.10.sums_ref, bf16[4,256,128]{2,1,0:T(8,128)(2,1)S(1)} %bitcast.11, bf16[2,256,128]{2,1,0:T(8,128)(2,1)S(1)} %collective-permute-done.pair_ref, ...), custom_call_target="tpu_custom_call" | custom-call | tf_op jit(solution)/shard_map/first/pallas_call | solution.py:231
  18.9 9.0 %all_to_all.11.sums_ref = f32[16,2,128]{2,1,0:T(2,128)S(1)} all-to-all(f32[16,2,128]{2,1,0:T(2,128)S(1)} %get-tuple-element.14), channel_id=1, replica_groups={{0,15,1,14,2,13,3,12,4,11,5,10,6,9,7,8},{16,31,17,30,18,29,19,28,20,27,..., dimensions={0} | all-to-all | bytes 32768 | tf_op jit(solution)/shard_map/all_to_all | solution.py:198
  28.0 0.0 copy-done.2
  28.0 1.6 %second.1 = bf16[4,256,128]{2,1,0:T(8,128)(2,1)} custom-call(f32[16,2,128]{2,1,0:T(2,128)S(1)} %all_to_all.11.sums_ref, bf16[6,256,128]{2,1,0:T(8,128)(2,1)S(1)} %get-tuple-element.15.hidden_ref, bf16[4,256,128]{2,1,0:T(8,128)(2,1)S(1)} %bitcast.12, bf16[3,9,128,128]{3,2,1,0:T(8,128)(2,1)S(1)} %bitcast.14, f32[8,128]{1,0:T(8,128)S(1)} %get-tuple-element.16.params_ref), custom_call_target="tpu_custom_call" | custom-call | tf_op jit(solution)/shard_map/second/pallas_call | solution.py:261
Async XLA Ops:
  0.0 0.9 %copy-start = (bf16[1,4,256,128]{3,2,1,0:T(8,128)(2,1)S(1)}, bf16[1,4,256,128]{3,2,1,0:T(8,128)(2,1)}, u32[]{:S(2)}) copy-start(bf16[1,4,256,128]{3,2,1,0:T(8,128)(2,1)} %param.9) | copy-start | bytes 786436
  1.0 16.5 %copy-start.1 = (bf16[3,3,3,128,128]{4,3,2,1,0:T(8,128)(2,1)S(1)}, bf16[3,3,3,128,128]{4,3,2,1,0:T(8,128)(2,1)}, u32[]{:S(2)}) copy-start(bf16[3,3,3,128,128]{4,3,2,1,0:T(8,128)(2,1)} %param.12) | copy-start | bytes 2654212
  1.0 16.5 %copy-start.3 = (f32[128]{0:T(128)S(1)}, f32[128]{0:T(128)}, u32[]{:S(2)}) copy-start(f32[128]{0:T(128)} %param.13) | copy-start | bytes 1540
  1.0 16.5 %copy-start.4 = (f32[128]{0:T(128)S(1)}, f32[128]{0:T(128)}, u32[]{:S(2)}) copy-start(f32[128]{0:T(128)} %param.10) | copy-start | bytes 1540
  1.0 16.5 %copy-start.5 = (f32[128]{0:T(128)S(1)}, f32[128]{0:T(128)}, u32[]{:S(2)}) copy-start(f32[128]{0:T(128)} %param.11) | copy-start | bytes 1540
  1.1 26.9 %copy-start.2 = (bf16[3,3,3,128,128]{4,3,2,1,0:T(8,128)(2,1)S(1)}, bf16[3,3,3,128,128]{4,3,2,1,0:T(8,128)(2,1)}, u32[]{:S(2)}) copy-start(bf16[3,3,3,128,128]{4,3,2,1,0:T(8,128)(2,1)} %param.16) | copy-start | bytes 2654212
  1.1 16.3 %collective-permute-start = (bf16[2,256,128]{2,1,0:T(8,128)(2,1)S(1)}, bf16[2,256,128]{2,1,0:T(8,128)(2,1)S(1)}, u32[]{:S(2)}, u32[]{:S(2)}) collective-permute-start(bf16[2,256,128]{2,1,0:T(8,128)(2,1)S(1)} %get-tuple-element.12), channel_id=1, source_target_pairs={{0,1},{1,0},{2,3},{3,2},{4,5},{5,4},{6,7},{7,6},{8,9},{9,8},{10,11... | collective-permute-start | bytes 393224 | tf_op jit(solution)/shard_map/ppermute | solution.py:229
  1.6 15.8 %collective-permute-start.1 = (bf16[2,256,128]{2,1,0:T(8,128)(2,1)S(1)}, bf16[2,256,128]{2,1,0:T(8,128)(2,1)S(1)}, u32[]{:S(2)}, u32[]{:S(2)}) collective-permute-start(bf16[2,256,128]{2,1,0:T(8,128)(2,1)S(1)} %get-tuple-element.13), channel_id=1, source_target_pairs={{1,2},{2,1},{3,4},{4,3},{5,6},{6,5},{7,8},{8,7},{9,10},{10,9},{11,... | collective-permute-start | bytes 393224 | tf_op jit(solution)/shard_map/ppermute | solution.py:228

commit v5 on v4

--- a/solution.py
+++ b/solution.py
@@ -99,13 +99,16 @@
         taps_ref[row, :, tap * channels : (tap + 1) * channels] = shifted.astype(jnp.bfloat16)
 
 
-def conv_rows(taps_ref, row, count, weight_ref):
+def window(taps_ref, row, count):
     _, width, lanes = taps_ref.shape
-    window = jnp.concatenate(
-        [taps_ref[row + tap : row + tap + count].reshape(count * width, lanes) for tap in range(3)],
-        axis=1,
-    )
-    both = jnp.dot(window, weight_ref[...], preferred_element_type=jnp.float32)
+    parts = [
+        taps_ref[row + tap : row + tap + count].reshape(count * width, lanes) for tap in range(3)
+    ]
+    return jnp.concatenate(parts, axis=1)
+
+
+def product(rows, weight_ref):
+    both = jnp.dot(rows, weight_ref[...], preferred_element_type=jnp.float32)
     half = both.shape[1] // 2
     return both[:, :half] + both[:, half:]
 
@@ -140,15 +143,20 @@
 
     total = jnp.zeros((8, channels), jnp.float32)
     square = jnp.zeros((8, channels), jnp.float32)
-    for row in range(rows + 4):
+    for row in range(1, rows + 3):
         make(row)
-    hidden = conv_rows(taps_ref, 0, rows + 2, summed_ref) + bias_ref[...]
+    hidden = product(window(taps_ref, 1, rows), summed_ref) + bias_ref[...]
     hidden = hidden.astype(jnp.bfloat16)
-    for row in range(rows + 2):
+    for row in range(rows):
         values = hidden[row * width : (row + 1) * width]
-        hidden_ref[row] = values
-        if 0 < row <= rows:
-            total, square = add_sums(values.astype(jnp.float32), total, square)
+        hidden_ref[row + 1] = values
+        total, square = add_sums(values.astype(jnp.float32), total, square)
+    make(0)
+    make(rows + 3)
+    halo = jnp.concatenate([window(taps_ref, 0, 1), window(taps_ref, rows + 1, 1)], axis=0)
+    halo = (product(halo, summed_ref) + bias_ref[...]).astype(jnp.bfloat16)
+    hidden_ref[0] = halo[:width]
+    hidden_ref[rows + 1] = halo[width:]
     store_sums(total, square, out_ref)
     for i in range(3):
         copies[i].wait()

time: 29.8 us -> 29.8 us (level)
  no operation moved by 1% of the time
where the time goes in v5:
time: 29.8 us; the launch traced here: 29.6 us
  blocking collectives  24.1 us (81%)
  Pallas kernels  3.23 us (11%)
  starting transfers between devices  1.17 us (4%)
  local copies, waits for them, and re-layouts  0.97 us (3%)
    all_to_all x2, blocking collectives, exchanged(): return lax.all_to_all(sums, 'rows', 0, 0, axis_index_groups=[ends_first])  24.1 us
    pallas_call x1, Pallas kernels, body(): pl.pallas_call(functools.partial(second_kernel, count), out_shape=jax.Sha...  1.58 us
    pallas_call x1, Pallas kernels, body(): pl.pallas_call(functools.partial(first_kernel, count), out_shape=[jax.Sha...  1.51 us
    unnamed x12, local copies, waits for them, and re-layouts  0.97 us
    ppermute x1, starting transfers between devices, body(): other = lax.ppermute(other, 'rows', swap_other)  0.66 us
  transfers between devices with their start and end apart: 2, of which 0 were waited for; matrix products, arithmetic and copies ran while one was open for 0% of the time, Pallas kernels for 0%

profile of v5, /device:TPU:0, one launch (start us, length us, event | category | flops | bytes accessed | tf_op | source)
XLA Modules:
  0.0 29.6 jit_solution(12470200230005388767)
XLA Ops:
  0.0 0.0 copy-start
  0.0 0.9 %copy-done = bf16[1,4,256,128]{3,2,1,0:T(8,128)(2,1)S(1)} copy-done((bf16[1,4,256,128]{3,2,1,0:T(8,128)(2,1)S(1)}, bf16[1,4,256,128]{3,2,1,0:T(8,128)(2,1)}, u32[]{:S(2)}) %copy-start) | copy-done | bytes 262168
  1.0 0.0 copy-start.1
  1.0 0.0 copy-start.3
  1.0 0.0 copy-start.4
  1.0 0.0 copy-start.5
  1.0 0.1 sums.1
  1.1 0.0 copy-start.2
  1.1 0.5 %collective-permute-start = (bf16[2,256,128]{2,1,0:T(8,128)(2,1)S(1)}, bf16[2,256,128]{2,1,0:T(8,128)(2,1)S(1)}, u32[]{:S(2)}, u32[]{:S(2)}) collective-permute-start(bf16[2,256,128]{2,1,0:T(8,128)(2,1)S(1)} %get-tuple-element.12), channel_id=1, source_target_pairs={{0,1},{1,0},{2,3},{3,2},{4,5},{5,4},{6,7},{7,6},{8,9},{9,8},{10,11... | collective-permute-start | bytes 393224 | tf_op jit(solution)/shard_map/ppermute | solution.py:237
  1.6 0.7 %collective-permute-start.1 = (bf16[2,256,128]{2,1,0:T(8,128)(2,1)S(1)}, bf16[2,256,128]{2,1,0:T(8,128)(2,1)S(1)}, u32[]{:S(2)}, u32[]{:S(2)}) collective-permute-start(bf16[2,256,128]{2,1,0:T(8,128)(2,1)S(1)} %get-tuple-element.13), channel_id=1, source_target_pairs={{1,2},{2,1},{3,4},{4,3},{5,6},{6,5},{7,8},{8,7},{9,10},{10,9},{11,... | collective-permute-start | bytes 393224 | tf_op jit(solution)/shard_map/ppermute | solution.py:236
  2.3 15.1 %all_to_all.10.sums_ref = f32[16,2,128]{2,1,0:T(2,128)S(1)} all-to-all(f32[16,2,128]{2,1,0:T(2,128)S(1)} %get-tuple-element.11), channel_id=1, replica_groups={{0,15,1,14,2,13,3,12,4,11,5,10,6,9,7,8},{16,31,17,30,18,29,19,28,20,27,..., dimensions={0} | all-to-all | bytes 32768 | tf_op jit(solution)/shard_map/all_to_all | solution.py:206
  17.4 0.0 collective-permute-done.pair_ref
  17.4 0.0 collective-permute-done.1.other_ref
  17.4 0.0 copy-done.1
  17.4 0.0 copy-done.3
  17.4 0.0 copy-done.4
  17.4 0.0 copy-done.5
  17.4 1.5 %first.1 = (bf16[6,256,128]{2,1,0:T(8,128)(2,1)S(1)}, f32[16,2,128]{2,1,0:T(2,128)S(1)}, f32[8,128]{1,0:T(8,128)S(1)}) custom-call(f32[16,2,128]{2,1,0:T(2,128)S(1)} %all_to_all.10.sums_ref, bf16[4,256,128]{2,1,0:T(8,128)(2,1)S(1)} %bitcast.11, bf16[2,256,128]{2,1,0:T(8,128)(2,1)S(1)} %collective-permute-done.pair_ref, ...), custom_call_target="tpu_custom_call" | custom-call | tf_op jit(solution)/shard_map/first/pallas_call | solution.py:239
  19.0 9.0 %all_to_all.11.sums_ref = f32[16,2,128]{2,1,0:T(2,128)S(1)} all-to-all(f32[16,2,128]{2,1,0:T(2,128)S(1)} %get-tuple-element.14), channel_id=1, replica_groups={{0,15,1,14,2,13,3,12,4,11,5,10,6,9,7,8},{16,31,17,30,18,29,19,28,20,27,..., dimensions={0} | all-to-all | bytes 32768 | tf_op jit(solution)/shard_map/all_to_all | solution.py:206
  28.0 0.0 copy-done.2
  28.0 1.6 %second.1 = bf16[4,256,128]{2,1,0:T(8,128)(2,1)} custom-call(f32[16,2,128]{2,1,0:T(2,128)S(1)} %all_to_all.11.sums_ref, bf16[6,256,128]{2,1,0:T(8,128)(2,1)S(1)} %get-tuple-element.15.hidden_ref, bf16[4,256,128]{2,1,0:T(8,128)(2,1)S(1)} %bitcast.12, bf16[3,9,128,128]{3,2,1,0:T(8,128)(2,1)S(1)} %bitcast.14, f32[8,128]{1,0:T(8,128)S(1)} %get-tuple-element.16.params_ref), custom_call_target="tpu_custom_call" | custom-call | tf_op jit(solution)/shard_map/second/pallas_call | solution.py:269
Async XLA Ops:
  0.0 0.9 %copy-start = (bf16[1,4,256,128]{3,2,1,0:T(8,128)(2,1)S(1)}, bf16[1,4,256,128]{3,2,1,0:T(8,128)(2,1)}, u32[]{:S(2)}) copy-start(bf16[1,4,256,128]{3,2,1,0:T(8,128)(2,1)} %param.9) | copy-start | bytes 786436
  1.0 16.5 %copy-start.1 = (bf16[3,3,3,128,128]{4,3,2,1,0:T(8,128)(2,1)S(1)}, bf16[3,3,3,128,128]{4,3,2,1,0:T(8,128)(2,1)}, u32[]{:S(2)}) copy-start(bf16[3,3,3,128,128]{4,3,2,1,0:T(8,128)(2,1)} %param.12) | copy-start | bytes 2654212
  1.0 16.5 %copy-start.3 = (f32[128]{0:T(128)S(1)}, f32[128]{0:T(128)}, u32[]{:S(2)}) copy-start(f32[128]{0:T(128)} %param.13) | copy-start | bytes 1540
  1.0 16.5 %copy-start.4 = (f32[128]{0:T(128)S(1)}, f32[128]{0:T(128)}, u32[]{:S(2)}) copy-start(f32[128]{0:T(128)} %param.10) | copy-start | bytes 1540
  1.0 16.5 %copy-start.5 = (f32[128]{0:T(128)S(1)}, f32[128]{0:T(128)}, u32[]{:S(2)}) copy-start(f32[128]{0:T(128)} %param.11) | copy-start | bytes 1540
  1.1 26.9 %copy-start.2 = (bf16[3,3,3,128,128]{4,3,2,1,0:T(8,128)(2,1)S(1)}, bf16[3,3,3,128,128]{4,3,2,1,0:T(8,128)(2,1)}, u32[]{:S(2)}) copy-start(bf16[3,3,3,128,128]{4,3,2,1,0:T(8,128)(2,1)} %param.16) | copy-start | bytes 2654212
  1.1 16.3 %collective-permute-start = (bf16[2,256,128]{2,1,0:T(8,128)(2,1)S(1)}, bf16[2,256,128]{2,1,0:T(8,128)(2,1)S(1)}, u32[]{:S(2)}, u32[]{:S(2)}) collective-permute-start(bf16[2,256,128]{2,1,0:T(8,128)(2,1)S(1)} %get-tuple-element.12), channel_id=1, source_target_pairs={{0,1},{1,0},{2,3},{3,2},{4,5},{5,4},{6,7},{7,6},{8,9},{9,8},{10,11... | collective-permute-start | bytes 393224 | tf_op jit(solution)/shard_map/ppermute | solution.py:237
  1.6 15.8 %collective-permute-start.1 = (bf16[2,256,128]{2,1,0:T(8,128)(2,1)S(1)}, bf16[2,256,128]{2,1,0:T(8,128)(2,1)S(1)}, u32[]{:S(2)}, u32[]{:S(2)}) collective-permute-start(bf16[2,256,128]{2,1,0:T(8,128)(2,1)S(1)} %get-tuple-element.13), channel_id=1, source_target_pairs={{1,2},{2,1},{3,4},{4,3},{5,6},{6,5},{7,8},{8,7},{9,10},{10,9},{11,... | collective-permute-start | bytes 393224 | tf_op jit(solution)/shard_map/ppermute | solution.py:236

commit v6 on v4

--- a/solution.py
+++ b/solution.py
@@ -82,7 +82,7 @@
         total += jnp.where(member < per_group - step, pltpu.roll(sums, channels - step, 1), 0.0)
     total = total * (1.0 / (entries * per_group))
     mean = total[0:1]
-    var = total[1:2] - mean * mean
+    var = jnp.maximum(total[1:2] - mean * mean, 0.0)
     scale = gain_ref[...] * lax.rsqrt(var + 1e-06)
     return 0.5 * scale, 0.5 * (shift_ref[...] - mean * scale)
 
@@ -172,22 +172,32 @@
         sums_ref, params_ref.at[1:2], params_ref.at[2:3], rows * width * count
     )
     sum_paired(weight_ref, summed_ref)
-    copies = [
-        pltpu.make_async_copy(done_ref.at[row], out_ref.at[row], sems.at[row])
-        for row in range(rows)
-    ]
+    copies = []
     for row in range(2):
         store_taps(hidden_ref[row], scale, offset, wide_ref, taps_ref, row)
     for row in range(0, rows, 2):
         for i in range(2, 4):
             store_taps(hidden_ref[row + i], scale, offset, wide_ref, taps_ref, row + i)
-        window = jnp.concatenate([taps_ref[row + tap] for tap in range(4)], axis=1)
-        both = jnp.dot(window, summed_ref[...], preferred_element_type=jnp.float32)
-        for i in range(2):
-            branch = both[:, i * channels : (i + 1) * channels] + params_ref[0:1, :]
-            values = own_ref[row + i].astype(jnp.float32) + branch
-            done_ref[row + i] = values.astype(jnp.bfloat16)
-            copies[row + i].start()
+        parts = 2 if row == rows - 2 else 1
+        for part in range(parts):
+            size = width // parts
+            columns = pl.ds(part * size, size)
+            window = jnp.concatenate(
+                [taps_ref[row + tap, columns, :] for tap in range(4)], axis=1
+            )
+            both = jnp.dot(window, summed_ref[...], preferred_element_type=jnp.float32)
+            for i in range(2):
+                branch = both[:, i * channels : (i + 1) * channels] + params_ref[0:1, :]
+                values = own_ref[row + i, columns, :].astype(jnp.float32) + branch
+                done_ref[row + i, columns, :] = values.astype(jnp.bfloat16)
+                copies.append(
+                    pltpu.make_async_copy(
+                        done_ref.at[row + i, columns],
+                        out_ref.at[row + i, columns],
+                        sems.at[len(copies)],
+                    )
+                )
+                copies[-1].start()
     for copy in copies:
         copy.wait()
 
@@ -268,7 +278,7 @@
             pltpu.VMEM((rows + 2, width, 3 * channels), jnp.bfloat16),
             pltpu.VMEM((taps // 3 * 4 * channels, 2 * channels), jnp.bfloat16),
             pltpu.VMEM(own.shape, jnp.bfloat16),
-            pltpu.SemaphoreType.DMA((rows,)),
+            pltpu.SemaphoreType.DMA((rows + 2,)),
         ],
         compiler_params=PARAMS, name="second",
     )(sums, hidden, own, raw(weight_two), params)

time: 29.8 us -> 29.8 us (level)
  no operation moved by 1% of the time
where the time goes in v6:
time: 29.8 us; the launch traced here: 29.6 us
  blocking collectives  24.1 us (81%)
  Pallas kernels  3.24 us (11%)
  starting transfers between devices  1.17 us (4%)
  local copies, waits for them, and re-layouts  0.97 us (3%)
    all_to_all x2, blocking collectives, exchanged(): return lax.all_to_all(sums, 'rows', 0, 0, axis_index_groups=[ends_first])  24.1 us
    pallas_call x1, Pallas kernels, body(): pl.pallas_call(functools.partial(second_kernel, count), out_shape=jax.Sha...  1.6 us
    pallas_call x1, Pallas kernels, body(): pl.pallas_call(functools.partial(first_kernel, count), out_shape=[jax.Sha...  1.5 us
    unnamed x12, local copies, waits for them, and re-layouts  0.97 us
    ppermute x1, starting transfers between devices, body(): other = lax.ppermute(other, 'rows', swap_other)  0.66 us
  transfers between devices with their start and end apart: 2, of which 0 were waited for; matrix products, arithmetic and copies ran while one was open for 0% of the time, Pallas kernels for 0%

profile of v6, /device:TPU:0, one launch (start us, length us, event | category | flops | bytes accessed | tf_op | source)
XLA Modules:
  0.0 29.6 jit_solution(299806334705508752)
XLA Ops:
  0.0 0.0 copy-start
  0.0 0.9 %copy-done = bf16[1,4,256,128]{3,2,1,0:T(8,128)(2,1)S(1)} copy-done((bf16[1,4,256,128]{3,2,1,0:T(8,128)(2,1)S(1)}, bf16[1,4,256,128]{3,2,1,0:T(8,128)(2,1)}, u32[]{:S(2)}) %copy-start) | copy-done | bytes 262168
  1.0 0.0 copy-start.1
  1.0 0.0 copy-start.3
  1.0 0.0 copy-start.4
  1.0 0.0 copy-start.5
  1.0 0.1 sums.1
  1.1 0.0 copy-start.2
  1.1 0.5 %collective-permute-start = (bf16[2,256,128]{2,1,0:T(8,128)(2,1)S(1)}, bf16[2,256,128]{2,1,0:T(8,128)(2,1)S(1)}, u32[]{:S(2)}, u32[]{:S(2)}) collective-permute-start(bf16[2,256,128]{2,1,0:T(8,128)(2,1)S(1)} %get-tuple-element.12), channel_id=1, source_target_pairs={{0,1},{1,0},{2,3},{3,2},{4,5},{5,4},{6,7},{7,6},{8,9},{9,8},{10,11... | collective-permute-start | bytes 393224 | tf_op jit(solution)/shard_map/ppermute | solution.py:239
  1.6 0.7 %collective-permute-start.1 = (bf16[2,256,128]{2,1,0:T(8,128)(2,1)S(1)}, bf16[2,256,128]{2,1,0:T(8,128)(2,1)S(1)}, u32[]{:S(2)}, u32[]{:S(2)}) collective-permute-start(bf16[2,256,128]{2,1,0:T(8,128)(2,1)S(1)} %get-tuple-element.13), channel_id=1, source_target_pairs={{1,2},{2,1},{3,4},{4,3},{5,6},{6,5},{7,8},{8,7},{9,10},{10,9},{11,... | collective-permute-start | bytes 393224 | tf_op jit(solution)/shard_map/ppermute | solution.py:238
  2.3 15.1 %all_to_all.10.sums_ref = f32[16,2,128]{2,1,0:T(2,128)S(1)} all-to-all(f32[16,2,128]{2,1,0:T(2,128)S(1)} %get-tuple-element.11), channel_id=1, replica_groups={{0,15,1,14,2,13,3,12,4,11,5,10,6,9,7,8},{16,31,17,30,18,29,19,28,20,27,..., dimensions={0} | all-to-all | bytes 32768 | tf_op jit(solution)/shard_map/all_to_all | solution.py:208
  17.4 0.0 collective-permute-done.pair_ref
  17.4 0.0 collective-permute-done.1.other_ref
  17.4 0.0 copy-done.1
  17.4 0.0 copy-done.3
  17.4 0.0 copy-done.4
  17.4 0.0 copy-done.5
  17.4 1.5 %first.1 = (bf16[6,256,128]{2,1,0:T(8,128)(2,1)S(1)}, f32[16,2,128]{2,1,0:T(2,128)S(1)}, f32[8,128]{1,0:T(8,128)S(1)}) custom-call(f32[16,2,128]{2,1,0:T(2,128)S(1)} %all_to_all.10.sums_ref, bf16[4,256,128]{2,1,0:T(8,128)(2,1)S(1)} %bitcast.11, bf16[2,256,128]{2,1,0:T(8,128)(2,1)S(1)} %collective-permute-done.pair_ref, ...), custom_call_target="tpu_custom_call" | custom-call | tf_op jit(solution)/shard_map/first/pallas_call | solution.py:241
  19.0 9.0 %all_to_all.11.sums_ref = f32[16,2,128]{2,1,0:T(2,128)S(1)} all-to-all(f32[16,2,128]{2,1,0:T(2,128)S(1)} %get-tuple-element.14), channel_id=1, replica_groups={{0,15,1,14,2,13,3,12,4,11,5,10,6,9,7,8},{16,31,17,30,18,29,19,28,20,27,..., dimensions={0} | all-to-all | bytes 32768 | tf_op jit(solution)/shard_map/all_to_all | solution.py:208
  28.0 0.0 copy-done.2
  28.0 1.6 %second.1 = bf16[4,256,128]{2,1,0:T(8,128)(2,1)} custom-call(f32[16,2,128]{2,1,0:T(2,128)S(1)} %all_to_all.11.sums_ref, bf16[6,256,128]{2,1,0:T(8,128)(2,1)S(1)} %get-tuple-element.15.hidden_ref, bf16[4,256,128]{2,1,0:T(8,128)(2,1)S(1)} %bitcast.12, bf16[3,9,128,128]{3,2,1,0:T(8,128)(2,1)S(1)} %bitcast.14, f32[8,128]{1,0:T(8,128)S(1)} %get-tuple-element.16.params_ref), custom_call_target="tpu_custom_call" | custom-call | tf_op jit(solution)/shard_map/second/pallas_call | solution.py:271
Async XLA Ops:
  0.0 0.9 %copy-start = (bf16[1,4,256,128]{3,2,1,0:T(8,128)(2,1)S(1)}, bf16[1,4,256,128]{3,2,1,0:T(8,128)(2,1)}, u32[]{:S(2)}) copy-start(bf16[1,4,256,128]{3,2,1,0:T(8,128)(2,1)} %param.9) | copy-start | bytes 786436
  1.0 16.5 %copy-start.1 = (bf16[3,3,3,128,128]{4,3,2,1,0:T(8,128)(2,1)S(1)}, bf16[3,3,3,128,128]{4,3,2,1,0:T(8,128)(2,1)}, u32[]{:S(2)}) copy-start(bf16[3,3,3,128,128]{4,3,2,1,0:T(8,128)(2,1)} %param.12) | copy-start | bytes 2654212
  1.0 16.5 %copy-start.3 = (f32[128]{0:T(128)S(1)}, f32[128]{0:T(128)}, u32[]{:S(2)}) copy-start(f32[128]{0:T(128)} %param.13) | copy-start | bytes 1540
  1.0 16.5 %copy-start.4 = (f32[128]{0:T(128)S(1)}, f32[128]{0:T(128)}, u32[]{:S(2)}) copy-start(f32[128]{0:T(128)} %param.10) | copy-start | bytes 1540
  1.0 16.5 %copy-start.5 = (f32[128]{0:T(128)S(1)}, f32[128]{0:T(128)}, u32[]{:S(2)}) copy-start(f32[128]{0:T(128)} %param.11) | copy-start | bytes 1540
  1.1 26.9 %copy-start.2 = (bf16[3,3,3,128,128]{4,3,2,1,0:T(8,128)(2,1)S(1)}, bf16[3,3,3,128,128]{4,3,2,1,0:T(8,128)(2,1)}, u32[]{:S(2)}) copy-start(bf16[3,3,3,128,128]{4,3,2,1,0:T(8,128)(2,1)} %param.16) | copy-start | bytes 2654212
  1.1 16.3 %collective-permute-start = (bf16[2,256,128]{2,1,0:T(8,128)(2,1)S(1)}, bf16[2,256,128]{2,1,0:T(8,128)(2,1)S(1)}, u32[]{:S(2)}, u32[]{:S(2)}) collective-permute-start(bf16[2,256,128]{2,1,0:T(8,128)(2,1)S(1)} %get-tuple-element.12), channel_id=1, source_target_pairs={{0,1},{1,0},{2,3},{3,2},{4,5},{5,4},{6,7},{7,6},{8,9},{9,8},{10,11... | collective-permute-start | bytes 393224 | tf_op jit(solution)/shard_map/ppermute | solution.py:239
  1.6 15.8 %collective-permute-start.1 = (bf16[2,256,128]{2,1,0:T(8,128)(2,1)S(1)}, bf16[2,256,128]{2,1,0:T(8,128)(2,1)S(1)}, u32[]{:S(2)}, u32[]{:S(2)}) collective-permute-start(bf16[2,256,128]{2,1,0:T(8,128)(2,1)S(1)} %get-tuple-element.13), channel_id=1, source_target_pairs={{1,2},{2,1},{3,4},{4,3},{5,6},{6,5},{7,8},{8,7},{9,10},{10,9},{11,... | collective-permute-start | bytes 393224 | tf_op jit(solution)/shard_map/ppermute | solution.py:238

commit v7 on v6

--- a/solution.py
+++ b/solution.py
@@ -226,7 +226,7 @@
 
     sums, pair, other = pl.pallas_call(
         sums_kernel,
-        out_shape=[sums_shape, slab_shape, slab_shape],
+        out_shape=[jax.ShapeDtypeStruct((1, 2, channels), jnp.float32), slab_shape, slab_shape],
         in_specs=[VMEM],
         out_specs=[VMEM] * 3,
         compiler_params=PARAMS,
@@ -235,9 +235,12 @@
             flops=40000000000, bytes_accessed=10000000, transcendentals=0
         ),
     )(own)
+    partner = lax.ppermute(sums, "rows", swap_pair)
+    pair = lax.ppermute(pair, "rows", swap_pair)
     other = lax.ppermute(other, "rows", swap_other)
-    pair = lax.ppermute(pair, "rows", swap_pair)
-    sums = exchanged(sums)
+    by_core = [list(range(core, count, 2)) for core in range(2)]
+    sums = jnp.broadcast_to(sums + partner, (count // 2, 2, channels))
+    sums = lax.all_to_all(sums, "rows", 0, 0, axis_index_groups=by_core)
     hidden, sums, params = pl.pallas_call(
         functools.partial(first_kernel, count),
         out_shape=[

time: 29.8 us -> 29.8 us (level)
    all_to_all x2 -> x1, blocking collectives: 24.1 us -> 9 us  [exchanged(): return lax.all_to_all(sums, 'rows', 0, 0, axis_index_groups=[ends_first])]
    all_to_all x0 -> x1, blocking collectives: none -> 14.9 us  [body(): sums = lax.all_to_all(sums, 'rows', 0, 0, axis_index_groups=by_core)]
    ppermute x0 -> x1, starting transfers between devices: none -> 0.52 us  [body(): partner = lax.ppermute(sums, 'rows', swap_pair)]
    ppermute x1, starting transfers between devices: 0.52 us -> 0.08 us  [body(): pair = lax.ppermute(pair, 'rows', swap_pair)]
  transfers between devices with their start and end apart: 2 -> 3, of which waited for: 0 -> 1; matrix products, arithmetic and copies ran while one was open for 0% -> 0% of each run, Pallas kernels for 0% -> 0%
where the time goes in v7:
time: 29.8 us; the launch traced here: 29.6 us
  blocking collectives  24 us (81%)
  Pallas kernels  3.27 us (11%)
  starting transfers between devices  1.25 us (4%)
  local copies, waits for them, and re-layouts  0.98 us (3%)
    all_to_all x1, blocking collectives, body(): sums = lax.all_to_all(sums, 'rows', 0, 0, axis_index_groups=by_core)  14.9 us
    all_to_all x1, blocking collectives, exchanged(): return lax.all_to_all(sums, 'rows', 0, 0, axis_index_groups=[ends_first])  9 us
    pallas_call x1, Pallas kernels, body(): pl.pallas_call(functools.partial(second_kernel, count), out_shape=jax.Sha...  1.62 us
    pallas_call x1, Pallas kernels, body(): pl.pallas_call(functools.partial(first_kernel, count), out_shape=[jax.Sha...  1.52 us
    unnamed x12, local copies, waits for them, and re-layouts  0.97 us
    ppermute x1, starting transfers between devices, body(): other = lax.ppermute(other, 'rows', swap_other)  0.66 us
  transfers between devices with their start and end apart: 3, of which 1 were waited for; matrix products, arithmetic and copies ran while one was open for 0% of the time, Pallas kernels for 0%

profile of v7, /device:TPU:0, one launch (start us, length us, event | category | flops | bytes accessed | tf_op | source)
XLA Modules:
  0.0 29.6 jit_solution(12959107999521324907)
XLA Ops:
  0.0 0.0 copy-start
  0.0 0.9 %copy-done = bf16[1,4,256,128]{3,2,1,0:T(8,128)(2,1)S(1)} copy-done((bf16[1,4,256,128]{3,2,1,0:T(8,128)(2,1)S(1)}, bf16[1,4,256,128]{3,2,1,0:T(8,128)(2,1)}, u32[]{:S(2)}) %copy-start) | copy-done | bytes 262168
  1.0 0.0 copy-start.1
  1.0 0.0 copy-start.3
  1.0 0.0 copy-start.4
  1.0 0.0 copy-start.5
  1.0 0.1 sums.1
  1.1 0.0 copy-start.2
  1.1 0.5 %collective-permute-start = (f32[1,2,128]{2,1,0:T(2,128)S(1)}, f32[1,2,128]{2,1,0:T(2,128)S(1)}, u32[]{:S(2)}, u32[]{:S(2)}) collective-permute-start(f32[1,2,128]{2,1,0:T(2,128)S(1)} %get-tuple-element.11), channel_id=1, source_target_pairs={{0,1},{1,0},{2,3},{3,2},{4,5},{5,4},{6,7},{7,6},{8,9},{9,8},{10,11... | collective-permute-start | bytes 3080 | tf_op jit(solution)/shard_map/ppermute | solution.py:238
  1.6 0.1 collective-permute-start.1
  1.7 0.7 %collective-permute-start.2 = (bf16[2,256,128]{2,1,0:T(8,128)(2,1)S(1)}, bf16[2,256,128]{2,1,0:T(8,128)(2,1)S(1)}, u32[]{:S(2)}, u32[]{:S(2)}) collective-permute-start(bf16[2,256,128]{2,1,0:T(8,128)(2,1)S(1)} %get-tuple-element.13), channel_id=1, source_target_pairs={{1,2},{2,1},{3,4},{4,3},{5,6},{6,5},{7,8},{8,7},{9,10},{10,9},{11,... | collective-permute-start | bytes 393224 | tf_op jit(solution)/shard_map/ppermute | solution.py:240
  2.4 0.1 collective-permute-done
  2.5 14.9 %all_to_all.10.sums_ref = f32[8,2,128]{2,1,0:T(2,128)S(1)} all-to-all(f32[8,2,128]{2,1,0:T(2,128)S(1)} %broadcast_in_dim.11), channel_id=1, replica_groups={{0,2,4,6,8,10,12,14},{1,3,5,7,9,11,13,15},{16,18,20,22,24,26,28,30},{17..., dimensions={0} | all-to-all | bytes 16384 | tf_op jit(solution)/shard_map/all_to_all | solution.py:243
  17.4 0.0 collective-permute-done.1.pair_ref
  17.4 0.0 collective-permute-done.2.other_ref
  17.4 0.0 copy-done.1
  17.4 0.0 copy-done.3
  17.4 0.0 copy-done.4
  17.4 0.0 copy-done.5
  17.5 1.5 %first.1 = (bf16[6,256,128]{2,1,0:T(8,128)(2,1)S(1)}, f32[16,2,128]{2,1,0:T(2,128)S(1)}, f32[8,128]{1,0:T(8,128)S(1)}) custom-call(f32[8,2,128]{2,1,0:T(2,128)S(1)} %all_to_all.10.sums_ref, bf16[4,256,128]{2,1,0:T(8,128)(2,1)S(1)} %bitcast.13, bf16[2,256,128]{2,1,0:T(8,128)(2,1)S(1)} %collective-permute-done.1.pair_ref, ...), custom_call_target="tpu_custom_call" | custom-call | tf_op jit(solution)/shard_map/first/pallas_call | solution.py:244
  19.0 9.0 %all_to_all.11.sums_ref = f32[16,2,128]{2,1,0:T(2,128)S(1)} all-to-all(f32[16,2,128]{2,1,0:T(2,128)S(1)} %get-tuple-element.14), channel_id=1, replica_groups={{0,15,1,14,2,13,3,12,4,11,5,10,6,9,7,8},{16,31,17,30,18,29,19,28,20,27,..., dimensions={0} | all-to-all | bytes 32768 | tf_op jit(solution)/shard_map/all_to_all | solution.py:208
  28.0 0.0 copy-done.2
  28.0 1.6 %second.1 = bf16[4,256,128]{2,1,0:T(8,128)(2,1)} custom-call(f32[16,2,128]{2,1,0:T(2,128)S(1)} %all_to_all.11.sums_ref, bf16[6,256,128]{2,1,0:T(8,128)(2,1)S(1)} %get-tuple-element.15.hidden_ref, bf16[4,256,128]{2,1,0:T(8,128)(2,1)S(1)} %bitcast.14, bf16[3,9,128,128]{3,2,1,0:T(8,128)(2,1)S(1)} %bitcast.16, f32[8,128]{1,0:T(8,128)S(1)} %get-tuple-element.16.params_ref), custom_call_target="tpu_custom_call" | custom-call | tf_op jit(solution)/shard_map/second/pallas_call | solution.py:274
  (2 shorter events, 0.0 us)
Async XLA Ops:
  0.0 0.9 %copy-start = (bf16[1,4,256,128]{3,2,1,0:T(8,128)(2,1)S(1)}, bf16[1,4,256,128]{3,2,1,0:T(8,128)(2,1)}, u32[]{:S(2)}) copy-start(bf16[1,4,256,128]{3,2,1,0:T(8,128)(2,1)} %param.9) | copy-start | bytes 786436
  1.0 16.5 %copy-start.1 = (bf16[3,3,3,128,128]{4,3,2,1,0:T(8,128)(2,1)S(1)}, bf16[3,3,3,128,128]{4,3,2,1,0:T(8,128)(2,1)}, u32[]{:S(2)}) copy-start(bf16[3,3,3,128,128]{4,3,2,1,0:T(8,128)(2,1)} %param.12) | copy-start | bytes 2654212
  1.0 16.5 %copy-start.3 = (f32[128]{0:T(128)S(1)}, f32[128]{0:T(128)}, u32[]{:S(2)}) copy-start(f32[128]{0:T(128)} %param.13) | copy-start | bytes 1540
  1.0 16.5 %copy-start.4 = (f32[128]{0:T(128)S(1)}, f32[128]{0:T(128)}, u32[]{:S(2)}) copy-start(f32[128]{0:T(128)} %param.10) | copy-start | bytes 1540
  1.0 16.5 %copy-start.5 = (f32[128]{0:T(128)S(1)}, f32[128]{0:T(128)}, u32[]{:S(2)}) copy-start(f32[128]{0:T(128)} %param.11) | copy-start | bytes 1540
  1.1 26.9 %copy-start.2 = (bf16[3,3,3,128,128]{4,3,2,1,0:T(8,128)(2,1)S(1)}, bf16[3,3,3,128,128]{4,3,2,1,0:T(8,128)(2,1)}, u32[]{:S(2)}) copy-start(bf16[3,3,3,128,128]{4,3,2,1,0:T(8,128)(2,1)} %param.16) | copy-start | bytes 2654212
  1.1 1.3 %collective-permute-start = (f32[1,2,128]{2,1,0:T(2,128)S(1)}, f32[1,2,128]{2,1,0:T(2,128)S(1)}, u32[]{:S(2)}, u32[]{:S(2)}) collective-permute-start(f32[1,2,128]{2,1,0:T(2,128)S(1)} %get-tuple-element.11), channel_id=1, source_target_pairs={{0,1},{1,0},{2,3},{3,2},{4,5},{5,4},{6,7},{7,6},{8,9},{9,8},{10,11... | collective-permute-start | bytes 3080 | tf_op jit(solution)/shard_map/ppermute | solution.py:238
  1.6 15.8 %collective-permute-start.1 = (bf16[2,256,128]{2,1,0:T(8,128)(2,1)S(1)}, bf16[2,256,128]{2,1,0:T(8,128)(2,1)S(1)}, u32[]{:S(2)}, u32[]{:S(2)}) collective-permute-start(bf16[2,256,128]{2,1,0:T(8,128)(2,1)S(1)} %get-tuple-element.12), channel_id=1, source_target_pairs={{0,1},{1,0},{2,3},{3,2},{4,5},{5,4},{6,7},{7,6},{8,9},{9,8},{10,11... | collective-permute-start | bytes 393224 | tf_op jit(solution)/shard_map/ppermute | solution.py:239
  1.7 15.7 %collective-permute-start.2 = (bf16[2,256,128]{2,1,0:T(8,128)(2,1)S(1)}, bf16[2,256,128]{2,1,0:T(8,128)(2,1)S(1)}, u32[]{:S(2)}, u32[]{:S(2)}) collective-permute-start(bf16[2,256,128]{2,1,0:T(8,128)(2,1)S(1)} %get-tuple-element.13), channel_id=1, source_target_pairs={{1,2},{2,1},{3,4},{4,3},{5,6},{6,5},{7,8},{8,7},{9,10},{10,9},{11,... | collective-permute-start | bytes 393224 | tf_op jit(solution)/shard_map/ppermute | solution.py:240

commit v8 on v6

--- a/solution.py
+++ b/solution.py
@@ -15,10 +15,21 @@
 
 
 def store_sums(total, square, out_ref):
-    total = jnp.sum(total, axis=0, keepdims=True)
-    square = jnp.sum(square, axis=0, keepdims=True)
-    both = jnp.concatenate([total, square], axis=0)
-    out_ref[...] = jnp.broadcast_to(both[None], out_ref.shape)
+    channels = total.shape[1]
+    per_group = channels // GROUPS
+    member = lax.broadcasted_iota(jnp.int32, (8, channels), 1) % per_group
+
+    def grouped(part):
+        part = jnp.broadcast_to(jnp.sum(part, axis=0, keepdims=True), (8, channels))
+        result = part
+        for step in range(1, per_group):
+            result += jnp.where(member >= step, pltpu.roll(part, step, 1), 0.0)
+            rolled = pltpu.roll(part, channels - step, 1)
+            result += jnp.where(member < per_group - step, rolled, 0.0)
+        return result
+
+    row = jnp.where(member == 0, grouped(total), grouped(square))[0:1]
+    out_ref[...] = jnp.broadcast_to(row[None], out_ref.shape)
 
 
 def add_sums(values, total, square):
@@ -74,17 +85,21 @@
     sums = jnp.sum(sums_ref[...], axis=0)
     channels = sums.shape[1]
     per_group = channels // GROUPS
-    sums = jnp.concatenate([sums, jnp.zeros((6, channels), jnp.float32)], axis=0)
+    sums = jnp.broadcast_to(sums, (8, channels)) * (1.0 / (entries * per_group))
     member = lax.broadcasted_iota(jnp.int32, sums.shape, 1) % per_group
-    total = sums
-    for step in range(1, per_group):
-        total += jnp.where(member >= step, pltpu.roll(sums, step, 1), 0.0)
-        total += jnp.where(member < per_group - step, pltpu.roll(sums, channels - step, 1), 0.0)
-    total = total * (1.0 / (entries * per_group))
-    mean = total[0:1]
-    var = jnp.maximum(total[1:2] - mean * mean, 0.0)
+
+    def spread(lane):
+        part = jnp.where(member == lane, sums, 0.0)
+        result = part
+        for target in range(per_group):
+            if target != lane:
+                result += pltpu.roll(part, (target - lane) % channels, 1)
+        return result
+
+    mean = spread(0)
+    var = jnp.maximum(spread(1) - mean * mean, 0.0)
     scale = gain_ref[...] * lax.rsqrt(var + 1e-06)
-    return 0.5 * scale, 0.5 * (shift_ref[...] - mean * scale)
+    return 0.5 * scale[0:1], (0.5 * (shift_ref[...] - mean * scale))[0:1]
 
 
 def store_taps(values, scale, offset, wide_ref, taps_ref, row):
@@ -214,7 +229,7 @@
     count = lax.axis_size("rows")
     own = latents[0]
     rows, width, channels = own.shape
-    sums_shape = jax.ShapeDtypeStruct((count, 2, channels), jnp.float32)
+    sums_shape = jax.ShapeDtypeStruct((count, 1, channels), jnp.float32)
     taps = weight_one.shape[1] * weight_one.shape[2]
     slab_shape = jax.ShapeDtypeStruct((2, width, channels), jnp.bfloat16)
 

time: 29.8 us -> 29.7 us (level)
  no operation moved by 1% of the time
where the time goes in v8:
time: 29.7 us; the launch traced here: 29.5 us
  blocking collectives  23.9 us (80%)
  Pallas kernels  3.31 us (11%)
  starting transfers between devices  1.17 us (4%)
  local copies, waits for them, and re-layouts  0.97 us (3%)
    all_to_all x2, blocking collectives, exchanged(): return lax.all_to_all(sums, 'rows', 0, 0, axis_index_groups=[ends_first])  23.9 us
    pallas_call x1, Pallas kernels, body(): pl.pallas_call(functools.partial(second_kernel, count), out_shape=jax.Sha...  1.59 us
    pallas_call x1, Pallas kernels, body(): pl.pallas_call(functools.partial(first_kernel, count), out_shape=[jax.Sha...  1.53 us
    unnamed x12, local copies, waits for them, and re-layouts  0.97 us
    ppermute x1, starting transfers between devices, body(): other = lax.ppermute(other, 'rows', swap_other)  0.66 us
  transfers between devices with their start and end apart: 2, of which 0 were waited for; matrix products, arithmetic and copies ran while one was open for 0% of the time, Pallas kernels for 0%

profile of v8, /device:TPU:0, one launch (start us, length us, event | category | flops | bytes accessed | tf_op | source)
XLA Modules:
  0.0 29.5 jit_solution(6476979805249601962)
XLA Ops:
  0.0 0.0 copy-start
  0.0 0.9 %copy-done = bf16[1,4,256,128]{3,2,1,0:T(8,128)(2,1)S(1)} copy-done((bf16[1,4,256,128]{3,2,1,0:T(8,128)(2,1)S(1)}, bf16[1,4,256,128]{3,2,1,0:T(8,128)(2,1)}, u32[]{:S(2)}) %copy-start) | copy-done | bytes 262168
  1.0 0.0 copy-start.1
  1.0 0.0 copy-start.3
  1.0 0.0 copy-start.4
  1.0 0.0 copy-start.5
  1.0 0.2 sums.1
  1.1 0.0 copy-start.2
  1.2 0.5 %collective-permute-start = (bf16[2,256,128]{2,1,0:T(8,128)(2,1)S(1)}, bf16[2,256,128]{2,1,0:T(8,128)(2,1)S(1)}, u32[]{:S(2)}, u32[]{:S(2)}) collective-permute-start(bf16[2,256,128]{2,1,0:T(8,128)(2,1)S(1)} %get-tuple-element.12), channel_id=1, source_target_pairs={{0,1},{1,0},{2,3},{3,2},{4,5},{5,4},{6,7},{7,6},{8,9},{9,8},{10,11... | collective-permute-start | bytes 393224 | tf_op jit(solution)/shard_map/ppermute | solution.py:254
  1.7 0.7 %collective-permute-start.1 = (bf16[2,256,128]{2,1,0:T(8,128)(2,1)S(1)}, bf16[2,256,128]{2,1,0:T(8,128)(2,1)S(1)}, u32[]{:S(2)}, u32[]{:S(2)}) collective-permute-start(bf16[2,256,128]{2,1,0:T(8,128)(2,1)S(1)} %get-tuple-element.13), channel_id=1, source_target_pairs={{1,2},{2,1},{3,4},{4,3},{5,6},{6,5},{7,8},{8,7},{9,10},{10,9},{11,... | collective-permute-start | bytes 393224 | tf_op jit(solution)/shard_map/ppermute | solution.py:253
  2.3 15.0 %all_to_all.10.sums_ref = f32[16,1,128]{2,1,0:T(1,128)S(1)} all-to-all(f32[16,1,128]{2,1,0:T(1,128)S(1)} %get-tuple-element.11), channel_id=1, replica_groups={{0,15,1,14,2,13,3,12,4,11,5,10,6,9,7,8},{16,31,17,30,18,29,19,28,20,27,..., dimensions={0} | all-to-all | bytes 16384 | tf_op jit(solution)/shard_map/all_to_all | solution.py:223
  17.4 0.0 collective-permute-done.pair_ref
  17.4 0.0 collective-permute-done.1.other_ref
  17.4 0.0 copy-done.1
  17.4 0.0 copy-done.3
  17.4 0.0 copy-done.4
  17.4 0.0 copy-done.5
  17.4 1.5 %first.1 = (bf16[6,256,128]{2,1,0:T(8,128)(2,1)S(1)}, f32[16,1,128]{2,1,0:T(1,128)S(1)}, f32[8,128]{1,0:T(8,128)S(1)}) custom-call(f32[16,1,128]{2,1,0:T(1,128)S(1)} %all_to_all.10.sums_ref, bf16[4,256,128]{2,1,0:T(8,128)(2,1)S(1)} %bitcast.11, bf16[2,256,128]{2,1,0:T(8,128)(2,1)S(1)} %collective-permute-done.pair_ref, ...), custom_call_target="tpu_custom_call" | custom-call | tf_op jit(solution)/shard_map/first/pallas_call | solution.py:256
  18.9 8.9 %all_to_all.11.sums_ref = f32[16,1,128]{2,1,0:T(1,128)S(1)} all-to-all(f32[16,1,128]{2,1,0:T(1,128)S(1)} %get-tuple-element.14), channel_id=1, replica_groups={{0,15,1,14,2,13,3,12,4,11,5,10,6,9,7,8},{16,31,17,30,18,29,19,28,20,27,..., dimensions={0} | all-to-all | bytes 16384 | tf_op jit(solution)/shard_map/all_to_all | solution.py:223
  27.9 0.0 copy-done.2
  27.9 1.6 %second.1 = bf16[4,256,128]{2,1,0:T(8,128)(2,1)} custom-call(f32[16,1,128]{2,1,0:T(1,128)S(1)} %all_to_all.11.sums_ref, bf16[6,256,128]{2,1,0:T(8,128)(2,1)S(1)} %get-tuple-element.15.hidden_ref, bf16[4,256,128]{2,1,0:T(8,128)(2,1)S(1)} %bitcast.12, bf16[3,9,128,128]{3,2,1,0:T(8,128)(2,1)S(1)} %bitcast.14, f32[8,128]{1,0:T(8,128)S(1)} %get-tuple-element.16.params_ref), custom_call_target="tpu_custom_call" | custom-call | tf_op jit(solution)/shard_map/second/pallas_call | solution.py:286
Async XLA Ops:
  0.0 0.9 %copy-start = (bf16[1,4,256,128]{3,2,1,0:T(8,128)(2,1)S(1)}, bf16[1,4,256,128]{3,2,1,0:T(8,128)(2,1)}, u32[]{:S(2)}) copy-start(bf16[1,4,256,128]{3,2,1,0:T(8,128)(2,1)} %param.9) | copy-start | bytes 786436
  1.0 16.4 %copy-start.1 = (bf16[3,3,3,128,128]{4,3,2,1,0:T(8,128)(2,1)S(1)}, bf16[3,3,3,128,128]{4,3,2,1,0:T(8,128)(2,1)}, u32[]{:S(2)}) copy-start(bf16[3,3,3,128,128]{4,3,2,1,0:T(8,128)(2,1)} %param.12) | copy-start | bytes 2654212
  1.0 16.4 %copy-start.3 = (f32[128]{0:T(128)S(1)}, f32[128]{0:T(128)}, u32[]{:S(2)}) copy-start(f32[128]{0:T(128)} %param.13) | copy-start | bytes 1540
  1.0 16.4 %copy-start.4 = (f32[128]{0:T(128)S(1)}, f32[128]{0:T(128)}, u32[]{:S(2)}) copy-start(f32[128]{0:T(128)} %param.10) | copy-start | bytes 1540
  1.0 16.4 %copy-start.5 = (f32[128]{0:T(128)S(1)}, f32[128]{0:T(128)}, u32[]{:S(2)}) copy-start(f32[128]{0:T(128)} %param.11) | copy-start | bytes 1540
  1.1 26.7 %copy-start.2 = (bf16[3,3,3,128,128]{4,3,2,1,0:T(8,128)(2,1)S(1)}, bf16[3,3,3,128,128]{4,3,2,1,0:T(8,128)(2,1)}, u32[]{:S(2)}) copy-start(bf16[3,3,3,128,128]{4,3,2,1,0:T(8,128)(2,1)} %param.16) | copy-start | bytes 2654212
  1.2 16.2 %collective-permute-start = (bf16[2,256,128]{2,1,0:T(8,128)(2,1)S(1)}, bf16[2,256,128]{2,1,0:T(8,128)(2,1)S(1)}, u32[]{:S(2)}, u32[]{:S(2)}) collective-permute-start(bf16[2,256,128]{2,1,0:T(8,128)(2,1)S(1)} %get-tuple-element.12), channel_id=1, source_target_pairs={{0,1},{1,0},{2,3},{3,2},{4,5},{5,4},{6,7},{7,6},{8,9},{9,8},{10,11... | collective-permute-start | bytes 393224 | tf_op jit(solution)/shard_map/ppermute | solution.py:254
  1.7 15.7 %collective-permute-start.1 = (bf16[2,256,128]{2,1,0:T(8,128)(2,1)S(1)}, bf16[2,256,128]{2,1,0:T(8,128)(2,1)S(1)}, u32[]{:S(2)}, u32[]{:S(2)}) collective-permute-start(bf16[2,256,128]{2,1,0:T(8,128)(2,1)S(1)} %get-tuple-element.13), channel_id=1, source_target_pairs={{1,2},{2,1},{3,4},{4,3},{5,6},{6,5},{7,8},{8,7},{9,10},{10,9},{11,... | collective-permute-start | bytes 393224 | tf_op jit(solution)/shard_map/ppermute | solution.py:253

commit v9 on v8

--- a/solution.py
+++ b/solution.py
@@ -64,21 +64,6 @@
         high = total.astype(jnp.bfloat16)
         low = (total - high.astype(jnp.float32)).astype(jnp.bfloat16)
         target[pl.ds(tap * channels, channels), :] = jnp.concatenate([high, low], axis=1)
-
-
-def sum_paired(source, target):
-    taps, channels = source.shape[1], source.shape[2]
-    columns = taps // 3
-    zeros = jnp.zeros((columns * channels, channels), jnp.bfloat16)
-    for tap in range(taps):
-        total = source[0, tap].astype(jnp.float32)
-        total += source[1, tap].astype(jnp.float32)
-        total += source[2, tap].astype(jnp.float32)
-        total = total.astype(jnp.bfloat16)
-        target[pl.ds(tap * channels, channels), 0:channels] = total
-        target[pl.ds((tap + columns) * channels, channels), channels : 2 * channels] = total
-    target[pl.ds(taps * channels, columns * channels), 0:channels] = zeros
-    target[pl.ds(0, columns * channels), channels : 2 * channels] = zeros
 
 
 def scale_offset(sums_ref, gain_ref, shift_ref, entries):
@@ -186,33 +171,22 @@
     scale, offset = scale_offset(
         sums_ref, params_ref.at[1:2], params_ref.at[2:3], rows * width * count
     )
-    sum_paired(weight_ref, summed_ref)
-    copies = []
-    for row in range(2):
-        store_taps(hidden_ref[row], scale, offset, wide_ref, taps_ref, row)
-    for row in range(0, rows, 2):
-        for i in range(2, 4):
-            store_taps(hidden_ref[row + i], scale, offset, wide_ref, taps_ref, row + i)
-        parts = 2 if row == rows - 2 else 1
-        for part in range(parts):
-            size = width // parts
-            columns = pl.ds(part * size, size)
-            window = jnp.concatenate(
-                [taps_ref[row + tap, columns, :] for tap in range(4)], axis=1
-            )
-            both = jnp.dot(window, summed_ref[...], preferred_element_type=jnp.float32)
-            for i in range(2):
-                branch = both[:, i * channels : (i + 1) * channels] + params_ref[0:1, :]
-                values = own_ref[row + i, columns, :].astype(jnp.float32) + branch
-                done_ref[row + i, columns, :] = values.astype(jnp.bfloat16)
-                copies.append(
-                    pltpu.make_async_copy(
-                        done_ref.at[row + i, columns],
-                        out_ref.at[row + i, columns],
-                        sems.at[len(copies)],
-                    )
-                )
-                copies[-1].start()
+    sum_weight(weight_ref, summed_ref)
+    copies = [
+        pltpu.make_async_copy(done_ref.at[row], out_ref.at[row], sems.at[row])
+        for row in range(rows)
+    ]
+    start = 0
+    for count in (rows - 1, 1):
+        for row in range(start + 2 if start else 0, start + count + 2):
+            store_taps(hidden_ref[row], scale, offset, wide_ref, taps_ref, row)
+        branch = conv_rows(taps_ref, start, count, summed_ref) + params_ref[0:1, :]
+        for i in range(count):
+            row = start + i
+            values = own_ref[row].astype(jnp.float32) + branch[i * width : (i + 1) * width]
+            done_ref[row] = values.astype(jnp.bfloat16)
+            copies[row].start()
+        start += count
     for copy in copies:
         copy.wait()
 
@@ -291,9 +265,9 @@
         scratch_shapes=[
             pltpu.VMEM((rows + 2, width + 16, channels), jnp.float32),
             pltpu.VMEM((rows + 2, width, 3 * channels), jnp.bfloat16),
-            pltpu.VMEM((taps // 3 * 4 * channels, 2 * channels), jnp.bfloat16),
+            pltpu.VMEM((taps * channels, 2 * channels), jnp.bfloat16),
             pltpu.VMEM(own.shape, jnp.bfloat16),
-            pltpu.SemaphoreType.DMA((rows + 2,)),
+            pltpu.SemaphoreType.DMA((rows,)),
         ],
         compiler_params=PARAMS, name="second",
     )(sums, hidden, own, raw(weight_two), params)

time: 29.7 us -> 29.9 us (level)
  no operation moved by 1% of the time
where the time goes in v9:
time: 29.9 us; the launch traced here: 29.6 us
  blocking collectives  23.9 us (80%)
  Pallas kernels  3.49 us (12%)
  starting transfers between devices  1.17 us (4%)
  local copies, waits for them, and re-layouts  0.97 us (3%)
    all_to_all x2, blocking collectives, exchanged(): return lax.all_to_all(sums, 'rows', 0, 0, axis_index_groups=[ends_first])  23.9 us
    pallas_call x1, Pallas kernels, body(): pl.pallas_call(functools.partial(second_kernel, count), out_shape=jax.Sha...  1.77 us
    pallas_call x1, Pallas kernels, body(): pl.pallas_call(functools.partial(first_kernel, count), out_shape=[jax.Sha...  1.53 us
    unnamed x12, local copies, waits for them, and re-layouts  0.97 us
    ppermute x1, starting transfers between devices, body(): other = lax.ppermute(other, 'rows', swap_other)  0.66 us
  transfers between devices with their start and end apart: 2, of which 0 were waited for; matrix products, arithmetic and copies ran while one was open for 0% of the time, Pallas kernels for 0%

profile of v9, /device:TPU:0, one launch (start us, length us, event | category | flops | bytes accessed | tf_op | source)
XLA Modules:
  0.0 29.6 jit_solution(14583316115828603486)
XLA Ops:
  0.0 0.0 copy-start
  0.0 0.9 %copy-done = bf16[1,4,256,128]{3,2,1,0:T(8,128)(2,1)S(1)} copy-done((bf16[1,4,256,128]{3,2,1,0:T(8,128)(2,1)S(1)}, bf16[1,4,256,128]{3,2,1,0:T(8,128)(2,1)}, u32[]{:S(2)}) %copy-start) | copy-done | bytes 262168
  1.0 0.0 copy-start.1
  1.0 0.0 copy-start.3
  1.0 0.0 copy-start.4
  1.0 0.0 copy-start.5
  1.0 0.2 sums.1
  1.1 0.0 copy-start.2
  1.2 0.5 %collective-permute-start = (bf16[2,256,128]{2,1,0:T(8,128)(2,1)S(1)}, bf16[2,256,128]{2,1,0:T(8,128)(2,1)S(1)}, u32[]{:S(2)}, u32[]{:S(2)}) collective-permute-start(bf16[2,256,128]{2,1,0:T(8,128)(2,1)S(1)} %get-tuple-element.12), channel_id=1, source_target_pairs={{0,1},{1,0},{2,3},{3,2},{4,5},{5,4},{6,7},{7,6},{8,9},{9,8},{10,11... | collective-permute-start | bytes 393224 | tf_op jit(solution)/shard_map/ppermute | solution.py:228
  1.7 0.7 %collective-permute-start.1 = (bf16[2,256,128]{2,1,0:T(8,128)(2,1)S(1)}, bf16[2,256,128]{2,1,0:T(8,128)(2,1)S(1)}, u32[]{:S(2)}, u32[]{:S(2)}) collective-permute-start(bf16[2,256,128]{2,1,0:T(8,128)(2,1)S(1)} %get-tuple-element.13), channel_id=1, source_target_pairs={{1,2},{2,1},{3,4},{4,3},{5,6},{6,5},{7,8},{8,7},{9,10},{10,9},{11,... | collective-permute-start | bytes 393224 | tf_op jit(solution)/shard_map/ppermute | solution.py:227
  2.3 15.0 %all_to_all.10.sums_ref = f32[16,1,128]{2,1,0:T(1,128)S(1)} all-to-all(f32[16,1,128]{2,1,0:T(1,128)S(1)} %get-tuple-element.11), channel_id=1, replica_groups={{0,15,1,14,2,13,3,12,4,11,5,10,6,9,7,8},{16,31,17,30,18,29,19,28,20,27,..., dimensions={0} | all-to-all | bytes 16384 | tf_op jit(solution)/shard_map/all_to_all | solution.py:197
  17.4 0.0 collective-permute-done.pair_ref
  17.4 0.0 collective-permute-done.1.other_ref
  17.4 0.0 copy-done.1
  17.4 0.0 copy-done.3
  17.4 0.0 copy-done.4
  17.4 0.0 copy-done.5
  17.4 1.5 %first.1 = (bf16[6,256,128]{2,1,0:T(8,128)(2,1)S(1)}, f32[16,1,128]{2,1,0:T(1,128)S(1)}, f32[8,128]{1,0:T(8,128)S(1)}) custom-call(f32[16,1,128]{2,1,0:T(1,128)S(1)} %all_to_all.10.sums_ref, bf16[4,256,128]{2,1,0:T(8,128)(2,1)S(1)} %bitcast.11, bf16[2,256,128]{2,1,0:T(8,128)(2,1)S(1)} %collective-permute-done.pair_ref, ...), custom_call_target="tpu_custom_call" | custom-call | tf_op jit(solution)/shard_map/first/pallas_call | solution.py:230
  18.9 8.9 %all_to_all.11.sums_ref = f32[16,1,128]{2,1,0:T(1,128)S(1)} all-to-all(f32[16,1,128]{2,1,0:T(1,128)S(1)} %get-tuple-element.14), channel_id=1, replica_groups={{0,15,1,14,2,13,3,12,4,11,5,10,6,9,7,8},{16,31,17,30,18,29,19,28,20,27,..., dimensions={0} | all-to-all | bytes 16384 | tf_op jit(solution)/shard_map/all_to_all | solution.py:197
  27.9 0.0 copy-done.2
  27.9 1.8 %second.1 = bf16[4,256,128]{2,1,0:T(8,128)(2,1)} custom-call(f32[16,1,128]{2,1,0:T(1,128)S(1)} %all_to_all.11.sums_ref, bf16[6,256,128]{2,1,0:T(8,128)(2,1)S(1)} %get-tuple-element.15.hidden_ref, bf16[4,256,128]{2,1,0:T(8,128)(2,1)S(1)} %bitcast.12, bf16[3,9,128,128]{3,2,1,0:T(8,128)(2,1)S(1)} %bitcast.14, f32[8,128]{1,0:T(8,128)S(1)} %get-tuple-element.16.params_ref), custom_call_target="tpu_custom_call" | custom-call | tf_op jit(solution)/shard_map/second/pallas_call | solution.py:260
Async XLA Ops:
  0.0 0.9 %copy-start = (bf16[1,4,256,128]{3,2,1,0:T(8,128)(2,1)S(1)}, bf16[1,4,256,128]{3,2,1,0:T(8,128)(2,1)}, u32[]{:S(2)}) copy-start(bf16[1,4,256,128]{3,2,1,0:T(8,128)(2,1)} %param.9) | copy-start | bytes 786436
  1.0 16.4 %copy-start.1 = (bf16[3,3,3,128,128]{4,3,2,1,0:T(8,128)(2,1)S(1)}, bf16[3,3,3,128,128]{4,3,2,1,0:T(8,128)(2,1)}, u32[]{:S(2)}) copy-start(bf16[3,3,3,128,128]{4,3,2,1,0:T(8,128)(2,1)} %param.12) | copy-start | bytes 2654212
  1.0 16.4 %copy-start.3 = (f32[128]{0:T(128)S(1)}, f32[128]{0:T(128)}, u32[]{:S(2)}) copy-start(f32[128]{0:T(128)} %param.13) | copy-start | bytes 1540
  1.0 16.4 %copy-start.4 = (f32[128]{0:T(128)S(1)}, f32[128]{0:T(128)}, u32[]{:S(2)}) copy-start(f32[128]{0:T(128)} %param.10) | copy-start | bytes 1540
  1.0 16.4 %copy-start.5 = (f32[128]{0:T(128)S(1)}, f32[128]{0:T(128)}, u32[]{:S(2)}) copy-start(f32[128]{0:T(128)} %param.11) | copy-start | bytes 1540
  1.1 26.7 %copy-start.2 = (bf16[3,3,3,128,128]{4,3,2,1,0:T(8,128)(2,1)S(1)}, bf16[3,3,3,128,128]{4,3,2,1,0:T(8,128)(2,1)}, u32[]{:S(2)}) copy-start(bf16[3,3,3,128,128]{4,3,2,1,0:T(8,128)(2,1)} %param.16) | copy-start | bytes 2654212
  1.2 16.2 %collective-permute-start = (bf16[2,256,128]{2,1,0:T(8,128)(2,1)S(1)}, bf16[2,256,128]{2,1,0:T(8,128)(2,1)S(1)}, u32[]{:S(2)}, u32[]{:S(2)}) collective-permute-start(bf16[2,256,128]{2,1,0:T(8,128)(2,1)S(1)} %get-tuple-element.12), channel_id=1, source_target_pairs={{0,1},{1,0},{2,3},{3,2},{4,5},{5,4},{6,7},{7,6},{8,9},{9,8},{10,11... | collective-permute-start | bytes 393224 | tf_op jit(solution)/shard_map/ppermute | solution.py:228
  1.7 15.7 %collective-permute-start.1 = (bf16[2,256,128]{2,1,0:T(8,128)(2,1)S(1)}, bf16[2,256,128]{2,1,0:T(8,128)(2,1)S(1)}, u32[]{:S(2)}, u32[]{:S(2)}) collective-permute-start(bf16[2,256,128]{2,1,0:T(8,128)(2,1)S(1)} %get-tuple-element.13), channel_id=1, source_target_pairs={{1,2},{2,1},{3,4},{4,3},{5,6},{6,5},{7,8},{8,7},{9,10},{10,9},{11,... | collective-permute-start | bytes 393224 | tf_op jit(solution)/shard_map/ppermute | solution.py:227

commit v10 on v9

--- a/solution.py
+++ b/solution.py
@@ -176,17 +176,13 @@
         pltpu.make_async_copy(done_ref.at[row], out_ref.at[row], sems.at[row])
         for row in range(rows)
     ]
-    start = 0
-    for count in (rows - 1, 1):
-        for row in range(start + 2 if start else 0, start + count + 2):
-            store_taps(hidden_ref[row], scale, offset, wide_ref, taps_ref, row)
-        branch = conv_rows(taps_ref, start, count, summed_ref) + params_ref[0:1, :]
-        for i in range(count):
-            row = start + i
-            values = own_ref[row].astype(jnp.float32) + branch[i * width : (i + 1) * width]
-            done_ref[row] = values.astype(jnp.bfloat16)
-            copies[row].start()
-        start += count
+    for row in range(rows + 2):
+        store_taps(hidden_ref[row], scale, offset, wide_ref, taps_ref, row)
+    branch = conv_rows(taps_ref, 0, rows, summed_ref) + params_ref[0:1, :]
+    for row in range(rows):
+        values = own_ref[row].astype(jnp.float32) + branch[row * width : (row + 1) * width]
+        done_ref[row] = values.astype(jnp.bfloat16)
+        copies[row].start()
     for copy in copies:
         copy.wait()
 

time: 29.9 us -> 29.8 us (level)
  no operation moved by 1% of the time
where the time goes in v10:
time: 29.8 us; the launch traced here: 29.6 us
  blocking collectives  23.9 us (80%)
  Pallas kernels  3.45 us (12%)
  starting transfers between devices  1.17 us (4%)
  local copies, waits for them, and re-layouts  0.97 us (3%)
    all_to_all x2, blocking collectives, exchanged(): return lax.all_to_all(sums, 'rows', 0, 0, axis_index_groups=[ends_first])  23.9 us
    pallas_call x1, Pallas kernels, body(): pl.pallas_call(functools.partial(second_kernel, count), out_shape=jax.Sha...  1.74 us
    pallas_call x1, Pallas kernels, body(): pl.pallas_call(functools.partial(first_kernel, count), out_shape=[jax.Sha...  1.53 us
    unnamed x12, local copies, waits for them, and re-layouts  0.97 us
    ppermute x1, starting transfers between devices, body(): other = lax.ppermute(other, 'rows', swap_other)  0.66 us
  transfers between devices with their start and end apart: 2, of which 0 were waited for; matrix products, arithmetic and copies ran while one was open for 0% of the time, Pallas kernels for 0%

profile of v10, /device:TPU:0, one launch (start us, length us, event | category | flops | bytes accessed | tf_op | source)
XLA Modules:
  0.0 29.6 jit_solution(16901781255236710538)
XLA Ops:
  0.0 0.0 copy-start
  0.0 0.9 %copy-done = bf16[1,4,256,128]{3,2,1,0:T(8,128)(2,1)S(1)} copy-done((bf16[1,4,256,128]{3,2,1,0:T(8,128)(2,1)S(1)}, bf16[1,4,256,128]{3,2,1,0:T(8,128)(2,1)}, u32[]{:S(2)}) %copy-start) | copy-done | bytes 262168
  1.0 0.0 copy-start.1
  1.0 0.0 copy-start.3
  1.0 0.0 copy-start.4
  1.0 0.0 copy-start.5
  1.0 0.2 sums.1
  1.1 0.0 copy-start.2
  1.2 0.5 %collective-permute-start = (bf16[2,256,128]{2,1,0:T(8,128)(2,1)S(1)}, bf16[2,256,128]{2,1,0:T(8,128)(2,1)S(1)}, u32[]{:S(2)}, u32[]{:S(2)}) collective-permute-start(bf16[2,256,128]{2,1,0:T(8,128)(2,1)S(1)} %get-tuple-element.12), channel_id=1, source_target_pairs={{0,1},{1,0},{2,3},{3,2},{4,5},{5,4},{6,7},{7,6},{8,9},{9,8},{10,11... | collective-permute-start | bytes 393224 | tf_op jit(solution)/shard_map/ppermute | solution.py:224
  1.7 0.7 %collective-permute-start.1 = (bf16[2,256,128]{2,1,0:T(8,128)(2,1)S(1)}, bf16[2,256,128]{2,1,0:T(8,128)(2,1)S(1)}, u32[]{:S(2)}, u32[]{:S(2)}) collective-permute-start(bf16[2,256,128]{2,1,0:T(8,128)(2,1)S(1)} %get-tuple-element.13), channel_id=1, source_target_pairs={{1,2},{2,1},{3,4},{4,3},{5,6},{6,5},{7,8},{8,7},{9,10},{10,9},{11,... | collective-permute-start | bytes 393224 | tf_op jit(solution)/shard_map/ppermute | solution.py:223
  2.3 15.0 %all_to_all.10.sums_ref = f32[16,1,128]{2,1,0:T(1,128)S(1)} all-to-all(f32[16,1,128]{2,1,0:T(1,128)S(1)} %get-tuple-element.11), channel_id=1, replica_groups={{0,15,1,14,2,13,3,12,4,11,5,10,6,9,7,8},{16,31,17,30,18,29,19,28,20,27,..., dimensions={0} | all-to-all | bytes 16384 | tf_op jit(solution)/shard_map/all_to_all | solution.py:193
  17.4 0.0 collective-permute-done.pair_ref
  17.4 0.0 collective-permute-done.1.other_ref
  17.4 0.0 copy-done.1
  17.4 0.0 copy-done.3
  17.4 0.0 copy-done.4
  17.4 0.0 copy-done.5
  17.4 1.5 %first.1 = (bf16[6,256,128]{2,1,0:T(8,128)(2,1)S(1)}, f32[16,1,128]{2,1,0:T(1,128)S(1)}, f32[8,128]{1,0:T(8,128)S(1)}) custom-call(f32[16,1,128]{2,1,0:T(1,128)S(1)} %all_to_all.10.sums_ref, bf16[4,256,128]{2,1,0:T(8,128)(2,1)S(1)} %bitcast.11, bf16[2,256,128]{2,1,0:T(8,128)(2,1)S(1)} %collective-permute-done.pair_ref, ...), custom_call_target="tpu_custom_call" | custom-call | tf_op jit(solution)/shard_map/first/pallas_call | solution.py:226
  18.9 8.9 %all_to_all.11.sums_ref = f32[16,1,128]{2,1,0:T(1,128)S(1)} all-to-all(f32[16,1,128]{2,1,0:T(1,128)S(1)} %get-tuple-element.14), channel_id=1, replica_groups={{0,15,1,14,2,13,3,12,4,11,5,10,6,9,7,8},{16,31,17,30,18,29,19,28,20,27,..., dimensions={0} | all-to-all | bytes 16384 | tf_op jit(solution)/shard_map/all_to_all | solution.py:193
  27.9 0.0 copy-done.2
  27.9 1.7 %second.1 = bf16[4,256,128]{2,1,0:T(8,128)(2,1)} custom-call(f32[16,1,128]{2,1,0:T(1,128)S(1)} %all_to_all.11.sums_ref, bf16[6,256,128]{2,1,0:T(8,128)(2,1)S(1)} %get-tuple-element.15.hidden_ref, bf16[4,256,128]{2,1,0:T(8,128)(2,1)S(1)} %bitcast.12, bf16[3,9,128,128]{3,2,1,0:T(8,128)(2,1)S(1)} %bitcast.14, f32[8,128]{1,0:T(8,128)S(1)} %get-tuple-element.16.params_ref), custom_call_target="tpu_custom_call" | custom-call | tf_op jit(solution)/shard_map/second/pallas_call | solution.py:256
Async XLA Ops:
  0.0 0.9 %copy-start = (bf16[1,4,256,128]{3,2,1,0:T(8,128)(2,1)S(1)}, bf16[1,4,256,128]{3,2,1,0:T(8,128)(2,1)}, u32[]{:S(2)}) copy-start(bf16[1,4,256,128]{3,2,1,0:T(8,128)(2,1)} %param.9) | copy-start | bytes 786436
  1.0 16.4 %copy-start.1 = (bf16[3,3,3,128,128]{4,3,2,1,0:T(8,128)(2,1)S(1)}, bf16[3,3,3,128,128]{4,3,2,1,0:T(8,128)(2,1)}, u32[]{:S(2)}) copy-start(bf16[3,3,3,128,128]{4,3,2,1,0:T(8,128)(2,1)} %param.12) | copy-start | bytes 2654212
  1.0 16.4 %copy-start.3 = (f32[128]{0:T(128)S(1)}, f32[128]{0:T(128)}, u32[]{:S(2)}) copy-start(f32[128]{0:T(128)} %param.13) | copy-start | bytes 1540
  1.0 16.4 %copy-start.4 = (f32[128]{0:T(128)S(1)}, f32[128]{0:T(128)}, u32[]{:S(2)}) copy-start(f32[128]{0:T(128)} %param.10) | copy-start | bytes 1540
  1.0 16.4 %copy-start.5 = (f32[128]{0:T(128)S(1)}, f32[128]{0:T(128)}, u32[]{:S(2)}) copy-start(f32[128]{0:T(128)} %param.11) | copy-start | bytes 1540
  1.1 26.7 %copy-start.2 = (bf16[3,3,3,128,128]{4,3,2,1,0:T(8,128)(2,1)S(1)}, bf16[3,3,3,128,128]{4,3,2,1,0:T(8,128)(2,1)}, u32[]{:S(2)}) copy-start(bf16[3,3,3,128,128]{4,3,2,1,0:T(8,128)(2,1)} %param.16) | copy-start | bytes 2654212
  1.2 16.2 %collective-permute-start = (bf16[2,256,128]{2,1,0:T(8,128)(2,1)S(1)}, bf16[2,256,128]{2,1,0:T(8,128)(2,1)S(1)}, u32[]{:S(2)}, u32[]{:S(2)}) collective-permute-start(bf16[2,256,128]{2,1,0:T(8,128)(2,1)S(1)} %get-tuple-element.12), channel_id=1, source_target_pairs={{0,1},{1,0},{2,3},{3,2},{4,5},{5,4},{6,7},{7,6},{8,9},{9,8},{10,11... | collective-permute-start | bytes 393224 | tf_op jit(solution)/shard_map/ppermute | solution.py:224
  1.7 15.7 %collective-permute-start.1 = (bf16[2,256,128]{2,1,0:T(8,128)(2,1)S(1)}, bf16[2,256,128]{2,1,0:T(8,128)(2,1)S(1)}, u32[]{:S(2)}, u32[]{:S(2)}) collective-permute-start(bf16[2,256,128]{2,1,0:T(8,128)(2,1)S(1)} %get-tuple-element.13), channel_id=1, source_target_pairs={{1,2},{2,1},{3,4},{4,3},{5,6},{6,5},{7,8},{8,7},{9,10},{10,9},{11,... | collective-permute-start | bytes 393224 | tf_op jit(solution)/shard_map/ppermute | solution.py:223

commit v11 on v10

--- a/solution.py
+++ b/solution.py
@@ -95,7 +95,7 @@
     wide_ref[row, 7:8, :] = act[0:1]
     wide_ref[row, 8 + width : 9 + width, :] = act[width - 1 : width]
     for tap in range(3):
-        shifted = wide_ref[row, 7 + tap : 7 + tap + width, :]
+        shifted = act if tap == 1 else wide_ref[row, 7 + tap : 7 + tap + width, :]
         taps_ref[row, :, tap * channels : (tap + 1) * channels] = shifted.astype(jnp.bfloat16)
 
 

time: 29.8 us -> 29.8 us (level)
  no operation moved by 1% of the time
where the time goes in v11:
time: 29.8 us; the launch traced here: 29.6 us
  blocking collectives  23.9 us (80%)
  Pallas kernels  3.46 us (12%)
  starting transfers between devices  1.17 us (4%)
  local copies, waits for them, and re-layouts  0.97 us (3%)
    all_to_all x2, blocking collectives, exchanged(): return lax.all_to_all(sums, 'rows', 0, 0, axis_index_groups=[ends_first])  23.9 us
    pallas_call x1, Pallas kernels, body(): pl.pallas_call(functools.partial(second_kernel, count), out_shape=jax.Sha...  1.74 us
    pallas_call x1, Pallas kernels, body(): pl.pallas_call(functools.partial(first_kernel, count), out_shape=[jax.Sha...  1.54 us
    unnamed x12, local copies, waits for them, and re-layouts  0.97 us
    ppermute x1, starting transfers between devices, body(): other = lax.ppermute(other, 'rows', swap_other)  0.66 us
  transfers between devices with their start and end apart: 2, of which 0 were waited for; matrix products, arithmetic and copies ran while one was open for 0% of the time, Pallas kernels for 0%

profile of v11, /device:TPU:0, one launch (start us, length us, event | category | flops | bytes accessed | tf_op | source)
XLA Modules:
  0.0 29.6 jit_solution(5643712677377270625)
XLA Ops:
  0.0 0.0 copy-start
  0.0 0.9 %copy-done = bf16[1,4,256,128]{3,2,1,0:T(8,128)(2,1)S(1)} copy-done((bf16[1,4,256,128]{3,2,1,0:T(8,128)(2,1)S(1)}, bf16[1,4,256,128]{3,2,1,0:T(8,128)(2,1)}, u32[]{:S(2)}) %copy-start) | copy-done | bytes 262168
  1.0 0.0 copy-start.1
  1.0 0.0 copy-start.3
  1.0 0.0 copy-start.4
  1.0 0.0 copy-start.5
  1.0 0.2 sums.1
  1.1 0.0 copy-start.2
  1.2 0.5 %collective-permute-start = (bf16[2,256,128]{2,1,0:T(8,128)(2,1)S(1)}, bf16[2,256,128]{2,1,0:T(8,128)(2,1)S(1)}, u32[]{:S(2)}, u32[]{:S(2)}) collective-permute-start(bf16[2,256,128]{2,1,0:T(8,128)(2,1)S(1)} %get-tuple-element.12), channel_id=1, source_target_pairs={{0,1},{1,0},{2,3},{3,2},{4,5},{5,4},{6,7},{7,6},{8,9},{9,8},{10,11... | collective-permute-start | bytes 393224 | tf_op jit(solution)/shard_map/ppermute | solution.py:224
  1.7 0.7 %collective-permute-start.1 = (bf16[2,256,128]{2,1,0:T(8,128)(2,1)S(1)}, bf16[2,256,128]{2,1,0:T(8,128)(2,1)S(1)}, u32[]{:S(2)}, u32[]{:S(2)}) collective-permute-start(bf16[2,256,128]{2,1,0:T(8,128)(2,1)S(1)} %get-tuple-element.13), channel_id=1, source_target_pairs={{1,2},{2,1},{3,4},{4,3},{5,6},{6,5},{7,8},{8,7},{9,10},{10,9},{11,... | collective-permute-start | bytes 393224 | tf_op jit(solution)/shard_map/ppermute | solution.py:223
  2.3 15.0 %all_to_all.10.sums_ref = f32[16,1,128]{2,1,0:T(1,128)S(1)} all-to-all(f32[16,1,128]{2,1,0:T(1,128)S(1)} %get-tuple-element.11), channel_id=1, replica_groups={{0,15,1,14,2,13,3,12,4,11,5,10,6,9,7,8},{16,31,17,30,18,29,19,28,20,27,..., dimensions={0} | all-to-all | bytes 16384 | tf_op jit(solution)/shard_map/all_to_all | solution.py:193
  17.4 0.0 collective-permute-done.pair_ref
  17.4 0.0 collective-permute-done.1.other_ref
  17.4 0.0 copy-done.1
  17.4 0.0 copy-done.3
  17.4 0.0 copy-done.4
  17.4 0.0 copy-done.5
  17.4 1.5 %first.1 = (bf16[6,256,128]{2,1,0:T(8,128)(2,1)S(1)}, f32[16,1,128]{2,1,0:T(1,128)S(1)}, f32[8,128]{1,0:T(8,128)S(1)}) custom-call(f32[16,1,128]{2,1,0:T(1,128)S(1)} %all_to_all.10.sums_ref, bf16[4,256,128]{2,1,0:T(8,128)(2,1)S(1)} %bitcast.11, bf16[2,256,128]{2,1,0:T(8,128)(2,1)S(1)} %collective-permute-done.pair_ref, ...), custom_call_target="tpu_custom_call" | custom-call | tf_op jit(solution)/shard_map/first/pallas_call | solution.py:226
  18.9 8.9 %all_to_all.11.sums_ref = f32[16,1,128]{2,1,0:T(1,128)S(1)} all-to-all(f32[16,1,128]{2,1,0:T(1,128)S(1)} %get-tuple-element.14), channel_id=1, replica_groups={{0,15,1,14,2,13,3,12,4,11,5,10,6,9,7,8},{16,31,17,30,18,29,19,28,20,27,..., dimensions={0} | all-to-all | bytes 16384 | tf_op jit(solution)/shard_map/all_to_all | solution.py:193
  27.9 0.0 copy-done.2
  27.9 1.7 %second.1 = bf16[4,256,128]{2,1,0:T(8,128)(2,1)} custom-call(f32[16,1,128]{2,1,0:T(1,128)S(1)} %all_to_all.11.sums_ref, bf16[6,256,128]{2,1,0:T(8,128)(2,1)S(1)} %get-tuple-element.15.hidden_ref, bf16[4,256,128]{2,1,0:T(8,128)(2,1)S(1)} %bitcast.12, bf16[3,9,128,128]{3,2,1,0:T(8,128)(2,1)S(1)} %bitcast.14, f32[8,128]{1,0:T(8,128)S(1)} %get-tuple-element.16.params_ref), custom_call_target="tpu_custom_call" | custom-call | tf_op jit(solution)/shard_map/second/pallas_call | solution.py:256
Async XLA Ops:
  0.0 0.9 %copy-start = (bf16[1,4,256,128]{3,2,1,0:T(8,128)(2,1)S(1)}, bf16[1,4,256,128]{3,2,1,0:T(8,128)(2,1)}, u32[]{:S(2)}) copy-start(bf16[1,4,256,128]{3,2,1,0:T(8,128)(2,1)} %param.9) | copy-start | bytes 786436
  1.0 16.4 %copy-start.1 = (bf16[3,3,3,128,128]{4,3,2,1,0:T(8,128)(2,1)S(1)}, bf16[3,3,3,128,128]{4,3,2,1,0:T(8,128)(2,1)}, u32[]{:S(2)}) copy-start(bf16[3,3,3,128,128]{4,3,2,1,0:T(8,128)(2,1)} %param.12) | copy-start | bytes 2654212
  1.0 16.4 %copy-start.3 = (f32[128]{0:T(128)S(1)}, f32[128]{0:T(128)}, u32[]{:S(2)}) copy-start(f32[128]{0:T(128)} %param.13) | copy-start | bytes 1540
  1.0 16.4 %copy-start.4 = (f32[128]{0:T(128)S(1)}, f32[128]{0:T(128)}, u32[]{:S(2)}) copy-start(f32[128]{0:T(128)} %param.10) | copy-start | bytes 1540
  1.0 16.4 %copy-start.5 = (f32[128]{0:T(128)S(1)}, f32[128]{0:T(128)}, u32[]{:S(2)}) copy-start(f32[128]{0:T(128)} %param.11) | copy-start | bytes 1540
  1.1 26.7 %copy-start.2 = (bf16[3,3,3,128,128]{4,3,2,1,0:T(8,128)(2,1)S(1)}, bf16[3,3,3,128,128]{4,3,2,1,0:T(8,128)(2,1)}, u32[]{:S(2)}) copy-start(bf16[3,3,3,128,128]{4,3,2,1,0:T(8,128)(2,1)} %param.16) | copy-start | bytes 2654212
  1.2 16.2 %collective-permute-start = (bf16[2,256,128]{2,1,0:T(8,128)(2,1)S(1)}, bf16[2,256,128]{2,1,0:T(8,128)(2,1)S(1)}, u32[]{:S(2)}, u32[]{:S(2)}) collective-permute-start(bf16[2,256,128]{2,1,0:T(8,128)(2,1)S(1)} %get-tuple-element.12), channel_id=1, source_target_pairs={{0,1},{1,0},{2,3},{3,2},{4,5},{5,4},{6,7},{7,6},{8,9},{9,8},{10,11... | collective-permute-start | bytes 393224 | tf_op jit(solution)/shard_map/ppermute | solution.py:224
  1.7 15.7 %collective-permute-start.1 = (bf16[2,256,128]{2,1,0:T(8,128)(2,1)S(1)}, bf16[2,256,128]{2,1,0:T(8,128)(2,1)S(1)}, u32[]{:S(2)}, u32[]{:S(2)}) collective-permute-start(bf16[2,256,128]{2,1,0:T(8,128)(2,1)S(1)} %get-tuple-element.13), channel_id=1, source_target_pairs={{1,2},{2,1},{3,4},{4,3},{5,6},{6,5},{7,8},{8,7},{9,10},{10,9},{11,... | collective-permute-start | bytes 393224 | tf_op jit(solution)/shard_map/ppermute | solution.py:223

commit v12 on v10

--- a/solution.py
+++ b/solution.py
@@ -211,7 +211,7 @@
 
     sums, pair, other = pl.pallas_call(
         sums_kernel,
-        out_shape=[sums_shape, slab_shape, slab_shape],
+        out_shape=[jax.ShapeDtypeStruct((1, 1, channels), jnp.float32), slab_shape, slab_shape],
         in_specs=[VMEM],
         out_specs=[VMEM] * 3,
         compiler_params=PARAMS,
@@ -220,9 +220,14 @@
             flops=40000000000, bytes_accessed=10000000, transcendentals=0
         ),
     )(own)
+    partner = lax.ppermute(sums, "rows", swap_pair)
+    pair = lax.ppermute(pair, "rows", swap_pair)
     other = lax.ppermute(other, "rows", swap_other)
-    pair = lax.ppermute(pair, "rows", swap_pair)
-    sums = exchanged(sums)
+    half = count // 2
+    order = [i // 2 if i % 2 == 0 else half - 1 - i // 2 for i in range(half)]
+    by_core = [[2 * chip + core for chip in order] for core in range(2)]
+    sums = jnp.broadcast_to(sums + partner, (half, 1, channels))
+    sums = lax.all_to_all(sums, "rows", 0, 0, axis_index_groups=by_core)
     hidden, sums, params = pl.pallas_call(
         functools.partial(first_kernel, count),
         out_shape=[

time: 29.8 us -> 29.8 us (level)
    all_to_all x2 -> x1, blocking collectives: 23.9 us -> 8.92 us  [exchanged(): return lax.all_to_all(sums, 'rows', 0, 0, axis_index_groups=[ends_first])]
    all_to_all x0 -> x1, blocking collectives: none -> 14.9 us  [body(): sums = lax.all_to_all(sums, 'rows', 0, 0, axis_index_groups=by_core)]
    ppermute x0 -> x1, starting transfers between devices: none -> 0.52 us  [body(): partner = lax.ppermute(sums, 'rows', swap_pair)]
    ppermute x1, starting transfers between devices: 0.52 us -> 0.08 us  [body(): pair = lax.ppermute(pair, 'rows', swap_pair)]
  transfers between devices with their start and end apart: 2 -> 3, of which waited for: 0 -> 1; matrix products, arithmetic and copies ran while one was open for 0% -> 0% of each run, Pallas kernels for 0% -> 0%
where the time goes in v12:
time: 29.8 us; the launch traced here: 29.6 us
  blocking collectives  23.8 us (80%)
  Pallas kernels  3.45 us (12%)
  starting transfers between devices  1.25 us (4%)
  local copies, waits for them, and re-layouts  0.97 us (3%)
    all_to_all x1, blocking collectives, body(): sums = lax.all_to_all(sums, 'rows', 0, 0, axis_index_groups=by_core)  14.9 us
    all_to_all x1, blocking collectives, exchanged(): return lax.all_to_all(sums, 'rows', 0, 0, axis_index_groups=[ends_first])  8.92 us
    pallas_call x1, Pallas kernels, body(): pl.pallas_call(functools.partial(second_kernel, count), out_shape=jax.Sha...  1.74 us
    pallas_call x1, Pallas kernels, body(): pl.pallas_call(functools.partial(first_kernel, count), out_shape=[jax.Sha...  1.53 us
    unnamed x12, local copies, waits for them, and re-layouts  0.97 us
    ppermute x1, starting transfers between devices, body(): other = lax.ppermute(other, 'rows', swap_other)  0.66 us
  transfers between devices with their start and end apart: 3, of which 1 were waited for; matrix products, arithmetic and copies ran while one was open for 0% of the time, Pallas kernels for 0%

profile of v12, /device:TPU:0, one launch (start us, length us, event | category | flops | bytes accessed | tf_op | source)
XLA Modules:
  0.0 29.6 jit_solution(5041299750659702163)
XLA Ops:
  0.0 0.0 copy-start
  0.0 0.9 %copy-done = bf16[1,4,256,128]{3,2,1,0:T(8,128)(2,1)S(1)} copy-done((bf16[1,4,256,128]{3,2,1,0:T(8,128)(2,1)S(1)}, bf16[1,4,256,128]{3,2,1,0:T(8,128)(2,1)}, u32[]{:S(2)}) %copy-start) | copy-done | bytes 262168
  1.0 0.0 copy-start.1
  1.0 0.0 copy-start.3
  1.0 0.0 copy-start.4
  1.0 0.0 copy-start.5
  1.0 0.2 sums.1
  1.1 0.0 copy-start.2
  1.1 0.5 %collective-permute-start = (f32[1,1,128]{2,1,0:T(1,128)S(1)}, f32[1,1,128]{2,1,0:T(1,128)S(1)}, u32[]{:S(2)}, u32[]{:S(2)}) collective-permute-start(f32[1,1,128]{2,1,0:T(1,128)S(1)} %get-tuple-element.11), channel_id=1, source_target_pairs={{0,1},{1,0},{2,3},{3,2},{4,5},{5,4},{6,7},{7,6},{8,9},{9,8},{10,11... | collective-permute-start | bytes 1544 | tf_op jit(solution)/shard_map/ppermute | solution.py:223
  1.7 0.1 collective-permute-start.1
  1.7 0.7 %collective-permute-start.2 = (bf16[2,256,128]{2,1,0:T(8,128)(2,1)S(1)}, bf16[2,256,128]{2,1,0:T(8,128)(2,1)S(1)}, u32[]{:S(2)}, u32[]{:S(2)}) collective-permute-start(bf16[2,256,128]{2,1,0:T(8,128)(2,1)S(1)} %get-tuple-element.13), channel_id=1, source_target_pairs={{1,2},{2,1},{3,4},{4,3},{5,6},{6,5},{7,8},{8,7},{9,10},{10,9},{11,... | collective-permute-start | bytes 393224 | tf_op jit(solution)/shard_map/ppermute | solution.py:225
  2.4 0.1 collective-permute-done
  2.5 14.9 %all_to_all.10.sums_ref = f32[8,1,128]{2,1,0:T(1,128)S(1)} all-to-all(f32[8,1,128]{2,1,0:T(1,128)S(1)} %broadcast_in_dim.11), channel_id=1, replica_groups={{0,14,2,12,4,10,6,8},{1,15,3,13,5,11,7,9},{16,30,18,28,20,26,22,24},{17..., dimensions={0} | all-to-all | bytes 8192 | tf_op jit(solution)/shard_map/all_to_all | solution.py:230
  17.4 0.0 collective-permute-done.1.pair_ref
  17.4 0.0 collective-permute-done.2.other_ref
  17.4 0.0 copy-done.1
  17.4 0.0 copy-done.3
  17.4 0.0 copy-done.4
  17.4 0.0 copy-done.5
  17.4 1.5 %first.1 = (bf16[6,256,128]{2,1,0:T(8,128)(2,1)S(1)}, f32[16,1,128]{2,1,0:T(1,128)S(1)}, f32[8,128]{1,0:T(8,128)S(1)}) custom-call(f32[8,1,128]{2,1,0:T(1,128)S(1)} %all_to_all.10.sums_ref, bf16[4,256,128]{2,1,0:T(8,128)(2,1)S(1)} %bitcast.13, bf16[2,256,128]{2,1,0:T(8,128)(2,1)S(1)} %collective-permute-done.1.pair_ref, ...), custom_call_target="tpu_custom_call" | custom-call | tf_op jit(solution)/shard_map/first/pallas_call | solution.py:231
  18.9 8.9 %all_to_all.11.sums_ref = f32[16,1,128]{2,1,0:T(1,128)S(1)} all-to-all(f32[16,1,128]{2,1,0:T(1,128)S(1)} %get-tuple-element.14), channel_id=1, replica_groups={{0,15,1,14,2,13,3,12,4,11,5,10,6,9,7,8},{16,31,17,30,18,29,19,28,20,27,..., dimensions={0} | all-to-all | bytes 16384 | tf_op jit(solution)/shard_map/all_to_all | solution.py:193
  27.9 0.0 copy-done.2
  27.9 1.7 %second.1 = bf16[4,256,128]{2,1,0:T(8,128)(2,1)} custom-call(f32[16,1,128]{2,1,0:T(1,128)S(1)} %all_to_all.11.sums_ref, bf16[6,256,128]{2,1,0:T(8,128)(2,1)S(1)} %get-tuple-element.15.hidden_ref, bf16[4,256,128]{2,1,0:T(8,128)(2,1)S(1)} %bitcast.14, bf16[3,9,128,128]{3,2,1,0:T(8,128)(2,1)S(1)} %bitcast.16, f32[8,128]{1,0:T(8,128)S(1)} %get-tuple-element.16.params_ref), custom_call_target="tpu_custom_call" | custom-call | tf_op jit(solution)/shard_map/second/pallas_call | solution.py:261
  (2 shorter events, 0.0 us)
Async XLA Ops:
  0.0 0.9 %copy-start = (bf16[1,4,256,128]{3,2,1,0:T(8,128)(2,1)S(1)}, bf16[1,4,256,128]{3,2,1,0:T(8,128)(2,1)}, u32[]{:S(2)}) copy-start(bf16[1,4,256,128]{3,2,1,0:T(8,128)(2,1)} %param.9) | copy-start | bytes 786436
  1.0 16.4 %copy-start.1 = (bf16[3,3,3,128,128]{4,3,2,1,0:T(8,128)(2,1)S(1)}, bf16[3,3,3,128,128]{4,3,2,1,0:T(8,128)(2,1)}, u32[]{:S(2)}) copy-start(bf16[3,3,3,128,128]{4,3,2,1,0:T(8,128)(2,1)} %param.12) | copy-start | bytes 2654212
  1.0 16.4 %copy-start.3 = (f32[128]{0:T(128)S(1)}, f32[128]{0:T(128)}, u32[]{:S(2)}) copy-start(f32[128]{0:T(128)} %param.13) | copy-start | bytes 1540
  1.0 16.4 %copy-start.4 = (f32[128]{0:T(128)S(1)}, f32[128]{0:T(128)}, u32[]{:S(2)}) copy-start(f32[128]{0:T(128)} %param.10) | copy-start | bytes 1540
  1.0 16.4 %copy-start.5 = (f32[128]{0:T(128)S(1)}, f32[128]{0:T(128)}, u32[]{:S(2)}) copy-start(f32[128]{0:T(128)} %param.11) | copy-start | bytes 1540
  1.1 26.7 %copy-start.2 = (bf16[3,3,3,128,128]{4,3,2,1,0:T(8,128)(2,1)S(1)}, bf16[3,3,3,128,128]{4,3,2,1,0:T(8,128)(2,1)}, u32[]{:S(2)}) copy-start(bf16[3,3,3,128,128]{4,3,2,1,0:T(8,128)(2,1)} %param.16) | copy-start | bytes 2654212
  1.1 1.3 %collective-permute-start = (f32[1,1,128]{2,1,0:T(1,128)S(1)}, f32[1,1,128]{2,1,0:T(1,128)S(1)}, u32[]{:S(2)}, u32[]{:S(2)}) collective-permute-start(f32[1,1,128]{2,1,0:T(1,128)S(1)} %get-tuple-element.11), channel_id=1, source_target_pairs={{0,1},{1,0},{2,3},{3,2},{4,5},{5,4},{6,7},{7,6},{8,9},{9,8},{10,11... | collective-permute-start | bytes 1544 | tf_op jit(solution)/shard_map/ppermute | solution.py:223
  1.7 15.7 %collective-permute-start.1 = (bf16[2,256,128]{2,1,0:T(8,128)(2,1)S(1)}, bf16[2,256,128]{2,1,0:T(8,128)(2,1)S(1)}, u32[]{:S(2)}, u32[]{:S(2)}) collective-permute-start(bf16[2,256,128]{2,1,0:T(8,128)(2,1)S(1)} %get-tuple-element.12), channel_id=1, source_target_pairs={{0,1},{1,0},{2,3},{3,2},{4,5},{5,4},{6,7},{7,6},{8,9},{9,8},{10,11... | collective-permute-start | bytes 393224 | tf_op jit(solution)/shard_map/ppermute | solution.py:224
  1.7 15.6 %collective-permute-start.2 = (bf16[2,256,128]{2,1,0:T(8,128)(2,1)S(1)}, bf16[2,256,128]{2,1,0:T(8,128)(2,1)S(1)}, u32[]{:S(2)}, u32[]{:S(2)}) collective-permute-start(bf16[2,256,128]{2,1,0:T(8,128)(2,1)S(1)} %get-tuple-element.13), channel_id=1, source_target_pairs={{1,2},{2,1},{3,4},{4,3},{5,6},{6,5},{7,8},{8,7},{9,10},{10,9},{11,... | collective-permute-start | bytes 393224 | tf_op jit(solution)/shard_map/ppermute | solution.py:225

commit v13 on v10

--- a/solution.py
+++ b/solution.py
@@ -28,7 +28,7 @@
             result += jnp.where(member < per_group - step, rolled, 0.0)
         return result
 
-    row = jnp.where(member == 0, grouped(total), grouped(square))[0:1]
+    row = jnp.where(member < per_group // 2, grouped(total), grouped(square))[0:1]
     out_ref[...] = jnp.broadcast_to(row[None], out_ref.shape)
 
 
@@ -73,16 +73,10 @@
     sums = jnp.broadcast_to(sums, (8, channels)) * (1.0 / (entries * per_group))
     member = lax.broadcasted_iota(jnp.int32, sums.shape, 1) % per_group
 
-    def spread(lane):
-        part = jnp.where(member == lane, sums, 0.0)
-        result = part
-        for target in range(per_group):
-            if target != lane:
-                result += pltpu.roll(part, (target - lane) % channels, 1)
-        return result
-
-    mean = spread(0)
-    var = jnp.maximum(spread(1) - mean * mean, 0.0)
+    half = per_group // 2
+    mean = jnp.where(member < half, sums, pltpu.roll(sums, half, 1))
+    mean_square = jnp.where(member < half, pltpu.roll(sums, channels - half, 1), sums)
+    var = jnp.maximum(mean_square - mean * mean, 0.0)
     scale = gain_ref[...] * lax.rsqrt(var + 1e-06)
     return 0.5 * scale[0:1], (0.5 * (shift_ref[...] - mean * scale))[0:1]
 

time: 29.8 us -> 29.8 us (level)
  no operation moved by 1% of the time
where the time goes in v13:
time: 29.8 us; the launch traced here: 29.6 us
  blocking collectives  23.9 us (80%)
  Pallas kernels  3.45 us (12%)
  starting transfers between devices  1.17 us (4%)
  local copies, waits for them, and re-layouts  0.97 us (3%)
    all_to_all x2, blocking collectives, exchanged(): return lax.all_to_all(sums, 'rows', 0, 0, axis_index_groups=[ends_first])  23.9 us
    pallas_call x1, Pallas kernels, body(): pl.pallas_call(functools.partial(second_kernel, count), out_shape=jax.Sha...  1.74 us
    pallas_call x1, Pallas kernels, body(): pl.pallas_call(functools.partial(first_kernel, count), out_shape=[jax.Sha...  1.53 us
    unnamed x12, local copies, waits for them, and re-layouts  0.97 us
    ppermute x1, starting transfers between devices, body(): other = lax.ppermute(other, 'rows', swap_other)  0.66 us
  transfers between devices with their start and end apart: 2, of which 0 were waited for; matrix products, arithmetic and copies ran while one was open for 0% of the time, Pallas kernels for 0%

profile of v13, /device:TPU:0, one launch (start us, length us, event | category | flops | bytes accessed | tf_op | source)
XLA Modules:
  0.0 29.6 jit_solution(1800702275364852822)
XLA Ops:
  0.0 0.0 copy-start
  0.0 0.9 %copy-done = bf16[1,4,256,128]{3,2,1,0:T(8,128)(2,1)S(1)} copy-done((bf16[1,4,256,128]{3,2,1,0:T(8,128)(2,1)S(1)}, bf16[1,4,256,128]{3,2,1,0:T(8,128)(2,1)}, u32[]{:S(2)}) %copy-start) | copy-done | bytes 262168
  1.0 0.0 copy-start.1
  1.0 0.0 copy-start.3
  1.0 0.0 copy-start.4
  1.0 0.0 copy-start.5
  1.0 0.2 sums.1
  1.1 0.0 copy-start.2
  1.2 0.5 %collective-permute-start = (bf16[2,256,128]{2,1,0:T(8,128)(2,1)S(1)}, bf16[2,256,128]{2,1,0:T(8,128)(2,1)S(1)}, u32[]{:S(2)}, u32[]{:S(2)}) collective-permute-start(bf16[2,256,128]{2,1,0:T(8,128)(2,1)S(1)} %get-tuple-element.12), channel_id=1, source_target_pairs={{0,1},{1,0},{2,3},{3,2},{4,5},{5,4},{6,7},{7,6},{8,9},{9,8},{10,11... | collective-permute-start | bytes 393224 | tf_op jit(solution)/shard_map/ppermute | solution.py:218
  1.7 0.7 %collective-permute-start.1 = (bf16[2,256,128]{2,1,0:T(8,128)(2,1)S(1)}, bf16[2,256,128]{2,1,0:T(8,128)(2,1)S(1)}, u32[]{:S(2)}, u32[]{:S(2)}) collective-permute-start(bf16[2,256,128]{2,1,0:T(8,128)(2,1)S(1)} %get-tuple-element.13), channel_id=1, source_target_pairs={{1,2},{2,1},{3,4},{4,3},{5,6},{6,5},{7,8},{8,7},{9,10},{10,9},{11,... | collective-permute-start | bytes 393224 | tf_op jit(solution)/shard_map/ppermute | solution.py:217
  2.3 15.0 %all_to_all.10.sums_ref = f32[16,1,128]{2,1,0:T(1,128)S(1)} all-to-all(f32[16,1,128]{2,1,0:T(1,128)S(1)} %get-tuple-element.11), channel_id=1, replica_groups={{0,15,1,14,2,13,3,12,4,11,5,10,6,9,7,8},{16,31,17,30,18,29,19,28,20,27,..., dimensions={0} | all-to-all | bytes 16384 | tf_op jit(solution)/shard_map/all_to_all | solution.py:187
  17.4 0.0 collective-permute-done.pair_ref
  17.4 0.0 collective-permute-done.1.other_ref
  17.4 0.0 copy-done.1
  17.4 0.0 copy-done.3
  17.4 0.0 copy-done.4
  17.4 0.0 copy-done.5
  17.4 1.5 %first.1 = (bf16[6,256,128]{2,1,0:T(8,128)(2,1)S(1)}, f32[16,1,128]{2,1,0:T(1,128)S(1)}, f32[8,128]{1,0:T(8,128)S(1)}) custom-call(f32[16,1,128]{2,1,0:T(1,128)S(1)} %all_to_all.10.sums_ref, bf16[4,256,128]{2,1,0:T(8,128)(2,1)S(1)} %bitcast.11, bf16[2,256,128]{2,1,0:T(8,128)(2,1)S(1)} %collective-permute-done.pair_ref, ...), custom_call_target="tpu_custom_call" | custom-call | tf_op jit(solution)/shard_map/first/pallas_call | solution.py:220
  18.9 8.9 %all_to_all.11.sums_ref = f32[16,1,128]{2,1,0:T(1,128)S(1)} all-to-all(f32[16,1,128]{2,1,0:T(1,128)S(1)} %get-tuple-element.14), channel_id=1, replica_groups={{0,15,1,14,2,13,3,12,4,11,5,10,6,9,7,8},{16,31,17,30,18,29,19,28,20,27,..., dimensions={0} | all-to-all | bytes 16384 | tf_op jit(solution)/shard_map/all_to_all | solution.py:187
  27.9 0.0 copy-done.2
  27.9 1.7 %second.1 = bf16[4,256,128]{2,1,0:T(8,128)(2,1)} custom-call(f32[16,1,128]{2,1,0:T(1,128)S(1)} %all_to_all.11.sums_ref, bf16[6,256,128]{2,1,0:T(8,128)(2,1)S(1)} %get-tuple-element.15.hidden_ref, bf16[4,256,128]{2,1,0:T(8,128)(2,1)S(1)} %bitcast.12, bf16[3,9,128,128]{3,2,1,0:T(8,128)(2,1)S(1)} %bitcast.14, f32[8,128]{1,0:T(8,128)S(1)} %get-tuple-element.16.params_ref), custom_call_target="tpu_custom_call" | custom-call | tf_op jit(solution)/shard_map/second/pallas_call | solution.py:250
Async XLA Ops:
  0.0 0.9 %copy-start = (bf16[1,4,256,128]{3,2,1,0:T(8,128)(2,1)S(1)}, bf16[1,4,256,128]{3,2,1,0:T(8,128)(2,1)}, u32[]{:S(2)}) copy-start(bf16[1,4,256,128]{3,2,1,0:T(8,128)(2,1)} %param.9) | copy-start | bytes 786436
  1.0 16.4 %copy-start.1 = (bf16[3,3,3,128,128]{4,3,2,1,0:T(8,128)(2,1)S(1)}, bf16[3,3,3,128,128]{4,3,2,1,0:T(8,128)(2,1)}, u32[]{:S(2)}) copy-start(bf16[3,3,3,128,128]{4,3,2,1,0:T(8,128)(2,1)} %param.12) | copy-start | bytes 2654212
  1.0 16.4 %copy-start.3 = (f32[128]{0:T(128)S(1)}, f32[128]{0:T(128)}, u32[]{:S(2)}) copy-start(f32[128]{0:T(128)} %param.13) | copy-start | bytes 1540
  1.0 16.4 %copy-start.4 = (f32[128]{0:T(128)S(1)}, f32[128]{0:T(128)}, u32[]{:S(2)}) copy-start(f32[128]{0:T(128)} %param.10) | copy-start | bytes 1540
  1.0 16.4 %copy-start.5 = (f32[128]{0:T(128)S(1)}, f32[128]{0:T(128)}, u32[]{:S(2)}) copy-start(f32[128]{0:T(128)} %param.11) | copy-start | bytes 1540
  1.1 26.7 %copy-start.2 = (bf16[3,3,3,128,128]{4,3,2,1,0:T(8,128)(2,1)S(1)}, bf16[3,3,3,128,128]{4,3,2,1,0:T(8,128)(2,1)}, u32[]{:S(2)}) copy-start(bf16[3,3,3,128,128]{4,3,2,1,0:T(8,128)(2,1)} %param.16) | copy-start | bytes 2654212
  1.2 16.2 %collective-permute-start = (bf16[2,256,128]{2,1,0:T(8,128)(2,1)S(1)}, bf16[2,256,128]{2,1,0:T(8,128)(2,1)S(1)}, u32[]{:S(2)}, u32[]{:S(2)}) collective-permute-start(bf16[2,256,128]{2,1,0:T(8,128)(2,1)S(1)} %get-tuple-element.12), channel_id=1, source_target_pairs={{0,1},{1,0},{2,3},{3,2},{4,5},{5,4},{6,7},{7,6},{8,9},{9,8},{10,11... | collective-permute-start | bytes 393224 | tf_op jit(solution)/shard_map/ppermute | solution.py:218
  1.7 15.7 %collective-permute-start.1 = (bf16[2,256,128]{2,1,0:T(8,128)(2,1)S(1)}, bf16[2,256,128]{2,1,0:T(8,128)(2,1)S(1)}, u32[]{:S(2)}, u32[]{:S(2)}) collective-permute-start(bf16[2,256,128]{2,1,0:T(8,128)(2,1)S(1)} %get-tuple-element.13), channel_id=1, source_target_pairs={{1,2},{2,1},{3,4},{4,3},{5,6},{6,5},{7,8},{8,7},{9,10},{10,9},{11,... | collective-permute-start | bytes 393224 | tf_op jit(solution)/shard_map/ppermute | solution.py:217

commit v14 on v10

--- a/solution.py
+++ b/solution.py
@@ -154,14 +154,6 @@
         copies[i].wait()
         next_ref[pl.ds(i, 1), :] = vectors_ref[i]
 
-    @pl.when(index == 0)
-    def _():
-        hidden_ref[0] = hidden_ref[1]
-
-    @pl.when(index == count - 1)
-    def _():
-        hidden_ref[rows + 1] = hidden_ref[rows]
-
 
 def second_kernel(
     count, sums_ref, hidden_ref, own_ref, weight_ref, params_ref,
@@ -176,8 +168,14 @@
         pltpu.make_async_copy(done_ref.at[row], out_ref.at[row], sems.at[row])
         for row in range(rows)
     ]
+    index = lax.axis_index("rows")
+    ends = {
+        0: jnp.where(index == 0, hidden_ref[1], hidden_ref[0]),
+        rows + 1: jnp.where(index == count - 1, hidden_ref[rows], hidden_ref[rows + 1]),
+    }
     for row in range(rows + 2):
-        store_taps(hidden_ref[row], scale, offset, wide_ref, taps_ref, row)
+        values = ends[row] if row in ends else hidden_ref[row]
+        store_taps(values, scale, offset, wide_ref, taps_ref, row)
     branch = conv_rows(taps_ref, 0, rows, summed_ref) + params_ref[0:1, :]
     for row in range(rows):
         values = own_ref[row].astype(jnp.float32) + branch[row * width : (row + 1) * width]

time: 29.8 us -> 29.8 us (level)
  no operation moved by 1% of the time
where the time goes in v14:
time: 29.8 us; the launch traced here: 29.6 us
  blocking collectives  23.9 us (80%)
  Pallas kernels  3.45 us (12%)
  starting transfers between devices  1.17 us (4%)
  local copies, waits for them, and re-layouts  0.97 us (3%)
    all_to_all x2, blocking collectives, exchanged(): return lax.all_to_all(sums, 'rows', 0, 0, axis_index_groups=[ends_first])  23.9 us
    pallas_call x1, Pallas kernels, body(): pl.pallas_call(functools.partial(second_kernel, count), out_shape=jax.Sha...  1.74 us
    pallas_call x1, Pallas kernels, body(): pl.pallas_call(functools.partial(first_kernel, count), out_shape=[jax.Sha...  1.53 us
    unnamed x12, local copies, waits for them, and re-layouts  0.97 us
    ppermute x1, starting transfers between devices, body(): other = lax.ppermute(other, 'rows', swap_other)  0.66 us
  transfers between devices with their start and end apart: 2, of which 0 were waited for; matrix products, arithmetic and copies ran while one was open for 0% of the time, Pallas kernels for 0%

profile of v14, /device:TPU:0, one launch (start us, length us, event | category | flops | bytes accessed | tf_op | source)
XLA Modules:
  0.0 29.6 jit_solution(388432376100599682)
XLA Ops:
  0.0 0.0 copy-start
  0.0 0.9 %copy-done = bf16[1,4,256,128]{3,2,1,0:T(8,128)(2,1)S(1)} copy-done((bf16[1,4,256,128]{3,2,1,0:T(8,128)(2,1)S(1)}, bf16[1,4,256,128]{3,2,1,0:T(8,128)(2,1)}, u32[]{:S(2)}) %copy-start) | copy-done | bytes 262168
  1.0 0.0 copy-start.1
  1.0 0.0 copy-start.3
  1.0 0.0 copy-start.4
  1.0 0.0 copy-start.5
  1.0 0.2 sums.1
  1.1 0.0 copy-start.2
  1.2 0.5 %collective-permute-start = (bf16[2,256,128]{2,1,0:T(8,128)(2,1)S(1)}, bf16[2,256,128]{2,1,0:T(8,128)(2,1)S(1)}, u32[]{:S(2)}, u32[]{:S(2)}) collective-permute-start(bf16[2,256,128]{2,1,0:T(8,128)(2,1)S(1)} %get-tuple-element.12), channel_id=1, source_target_pairs={{0,1},{1,0},{2,3},{3,2},{4,5},{5,4},{6,7},{7,6},{8,9},{9,8},{10,11... | collective-permute-start | bytes 393224 | tf_op jit(solution)/shard_map/ppermute | solution.py:222
  1.7 0.7 %collective-permute-start.1 = (bf16[2,256,128]{2,1,0:T(8,128)(2,1)S(1)}, bf16[2,256,128]{2,1,0:T(8,128)(2,1)S(1)}, u32[]{:S(2)}, u32[]{:S(2)}) collective-permute-start(bf16[2,256,128]{2,1,0:T(8,128)(2,1)S(1)} %get-tuple-element.13), channel_id=1, source_target_pairs={{1,2},{2,1},{3,4},{4,3},{5,6},{6,5},{7,8},{8,7},{9,10},{10,9},{11,... | collective-permute-start | bytes 393224 | tf_op jit(solution)/shard_map/ppermute | solution.py:221
  2.3 15.0 %all_to_all.10.sums_ref = f32[16,1,128]{2,1,0:T(1,128)S(1)} all-to-all(f32[16,1,128]{2,1,0:T(1,128)S(1)} %get-tuple-element.11), channel_id=1, replica_groups={{0,15,1,14,2,13,3,12,4,11,5,10,6,9,7,8},{16,31,17,30,18,29,19,28,20,27,..., dimensions={0} | all-to-all | bytes 16384 | tf_op jit(solution)/shard_map/all_to_all | solution.py:191
  17.4 0.0 collective-permute-done.pair_ref
  17.4 0.0 collective-permute-done.1.other_ref
  17.4 0.0 copy-done.1
  17.4 0.0 copy-done.3
  17.4 0.0 copy-done.4
  17.4 0.0 copy-done.5
  17.4 1.5 %first.1 = (bf16[6,256,128]{2,1,0:T(8,128)(2,1)S(1)}, f32[16,1,128]{2,1,0:T(1,128)S(1)}, f32[8,128]{1,0:T(8,128)S(1)}) custom-call(f32[16,1,128]{2,1,0:T(1,128)S(1)} %all_to_all.10.sums_ref, bf16[4,256,128]{2,1,0:T(8,128)(2,1)S(1)} %bitcast.11, bf16[2,256,128]{2,1,0:T(8,128)(2,1)S(1)} %collective-permute-done.pair_ref, ...), custom_call_target="tpu_custom_call" | custom-call | tf_op jit(solution)/shard_map/first/pallas_call | solution.py:224
  18.9 8.9 %all_to_all.11.sums_ref = f32[16,1,128]{2,1,0:T(1,128)S(1)} all-to-all(f32[16,1,128]{2,1,0:T(1,128)S(1)} %get-tuple-element.14), channel_id=1, replica_groups={{0,15,1,14,2,13,3,12,4,11,5,10,6,9,7,8},{16,31,17,30,18,29,19,28,20,27,..., dimensions={0} | all-to-all | bytes 16384 | tf_op jit(solution)/shard_map/all_to_all | solution.py:191
  27.9 0.0 copy-done.2
  27.9 1.7 %second.1 = bf16[4,256,128]{2,1,0:T(8,128)(2,1)} custom-call(f32[16,1,128]{2,1,0:T(1,128)S(1)} %all_to_all.11.sums_ref, bf16[6,256,128]{2,1,0:T(8,128)(2,1)S(1)} %get-tuple-element.15.hidden_ref, bf16[4,256,128]{2,1,0:T(8,128)(2,1)S(1)} %bitcast.12, bf16[3,9,128,128]{3,2,1,0:T(8,128)(2,1)S(1)} %bitcast.14, f32[8,128]{1,0:T(8,128)S(1)} %get-tuple-element.16.params_ref), custom_call_target="tpu_custom_call" | custom-call | tf_op jit(solution)/shard_map/second/pallas_call | solution.py:254
Async XLA Ops:
  0.0 0.9 %copy-start = (bf16[1,4,256,128]{3,2,1,0:T(8,128)(2,1)S(1)}, bf16[1,4,256,128]{3,2,1,0:T(8,128)(2,1)}, u32[]{:S(2)}) copy-start(bf16[1,4,256,128]{3,2,1,0:T(8,128)(2,1)} %param.9) | copy-start | bytes 786436
  1.0 16.4 %copy-start.1 = (bf16[3,3,3,128,128]{4,3,2,1,0:T(8,128)(2,1)S(1)}, bf16[3,3,3,128,128]{4,3,2,1,0:T(8,128)(2,1)}, u32[]{:S(2)}) copy-start(bf16[3,3,3,128,128]{4,3,2,1,0:T(8,128)(2,1)} %param.12) | copy-start | bytes 2654212
  1.0 16.4 %copy-start.3 = (f32[128]{0:T(128)S(1)}, f32[128]{0:T(128)}, u32[]{:S(2)}) copy-start(f32[128]{0:T(128)} %param.13) | copy-start | bytes 1540
  1.0 16.4 %copy-start.4 = (f32[128]{0:T(128)S(1)}, f32[128]{0:T(128)}, u32[]{:S(2)}) copy-start(f32[128]{0:T(128)} %param.10) | copy-start | bytes 1540
  1.0 16.4 %copy-start.5 = (f32[128]{0:T(128)S(1)}, f32[128]{0:T(128)}, u32[]{:S(2)}) copy-start(f32[128]{0:T(128)} %param.11) | copy-start | bytes 1540
  1.1 26.7 %copy-start.2 = (bf16[3,3,3,128,128]{4,3,2,1,0:T(8,128)(2,1)S(1)}, bf16[3,3,3,128,128]{4,3,2,1,0:T(8,128)(2,1)}, u32[]{:S(2)}) copy-start(bf16[3,3,3,128,128]{4,3,2,1,0:T(8,128)(2,1)} %param.16) | copy-start | bytes 2654212
  1.2 16.2 %collective-permute-start = (bf16[2,256,128]{2,1,0:T(8,128)(2,1)S(1)}, bf16[2,256,128]{2,1,0:T(8,128)(2,1)S(1)}, u32[]{:S(2)}, u32[]{:S(2)}) collective-permute-start(bf16[2,256,128]{2,1,0:T(8,128)(2,1)S(1)} %get-tuple-element.12), channel_id=1, source_target_pairs={{0,1},{1,0},{2,3},{3,2},{4,5},{5,4},{6,7},{7,6},{8,9},{9,8},{10,11... | collective-permute-start | bytes 393224 | tf_op jit(solution)/shard_map/ppermute | solution.py:222
  1.7 15.7 %collective-permute-start.1 = (bf16[2,256,128]{2,1,0:T(8,128)(2,1)S(1)}, bf16[2,256,128]{2,1,0:T(8,128)(2,1)S(1)}, u32[]{:S(2)}, u32[]{:S(2)}) collective-permute-start(bf16[2,256,128]{2,1,0:T(8,128)(2,1)S(1)} %get-tuple-element.13), channel_id=1, source_target_pairs={{1,2},{2,1},{3,4},{4,3},{5,6},{6,5},{7,8},{8,7},{9,10},{10,9},{11,... | collective-permute-start | bytes 393224 | tf_op jit(solution)/shard_map/ppermute | solution.py:221

commit v15 on v10

--- a/solution.py
+++ b/solution.py
@@ -189,7 +189,7 @@
 
 def exchanged(sums):
     count = lax.axis_size("rows")
-    ends_first = [i // 2 if i % 2 == 0 else count - 1 - i // 2 for i in range(count)]
+    ends_first = sorted(range(count), key=lambda i: (min(i // 2, (count - 1 - i) // 2), i))
     return lax.all_to_all(sums, "rows", 0, 0, axis_index_groups=[ends_first])
 
 

time: 29.8 us -> 29.7 us (level)
  no operation moved by 1% of the time
where the time goes in v15:
time: 29.7 us; the launch traced here: 29.5 us
  blocking collectives  23.8 us (80%)
  Pallas kernels  3.45 us (12%)
  starting transfers between devices  1.17 us (4%)
  local copies, waits for them, and re-layouts  0.97 us (3%)
    all_to_all x2, blocking collectives, exchanged(): return lax.all_to_all(sums, 'rows', 0, 0, axis_index_groups=[ends_first])  23.8 us
    pallas_call x1, Pallas kernels, body(): pl.pallas_call(functools.partial(second_kernel, count), out_shape=jax.Sha...  1.74 us
    pallas_call x1, Pallas kernels, body(): pl.pallas_call(functools.partial(first_kernel, count), out_shape=[jax.Sha...  1.53 us
    unnamed x12, local copies, waits for them, and re-layouts  0.97 us
    ppermute x1, starting transfers between devices, body(): other = lax.ppermute(other, 'rows', swap_other)  0.66 us
  transfers between devices with their start and end apart: 2, of which 0 were waited for; matrix products, arithmetic and copies ran while one was open for 0% of the time, Pallas kernels for 0%

profile of v15, /device:TPU:0, one launch (start us, length us, event | category | flops | bytes accessed | tf_op | source)
XLA Modules:
  0.0 29.5 jit_solution(15271534263565289119)
XLA Ops:
  0.0 0.0 copy-start
  0.0 0.9 %copy-done = bf16[1,4,256,128]{3,2,1,0:T(8,128)(2,1)S(1)} copy-done((bf16[1,4,256,128]{3,2,1,0:T(8,128)(2,1)S(1)}, bf16[1,4,256,128]{3,2,1,0:T(8,128)(2,1)}, u32[]{:S(2)}) %copy-start) | copy-done | bytes 262168
  1.0 0.0 copy-start.1
  1.0 0.0 copy-start.3
  1.0 0.0 copy-start.4
  1.0 0.0 copy-start.5
  1.0 0.2 sums.1
  1.1 0.0 copy-start.2
  1.2 0.5 %collective-permute-start = (bf16[2,256,128]{2,1,0:T(8,128)(2,1)S(1)}, bf16[2,256,128]{2,1,0:T(8,128)(2,1)S(1)}, u32[]{:S(2)}, u32[]{:S(2)}) collective-permute-start(bf16[2,256,128]{2,1,0:T(8,128)(2,1)S(1)} %get-tuple-element.12), channel_id=1, source_target_pairs={{0,1},{1,0},{2,3},{3,2},{4,5},{5,4},{6,7},{7,6},{8,9},{9,8},{10,11... | collective-permute-start | bytes 393224 | tf_op jit(solution)/shard_map/ppermute | solution.py:224
  1.7 0.7 %collective-permute-start.1 = (bf16[2,256,128]{2,1,0:T(8,128)(2,1)S(1)}, bf16[2,256,128]{2,1,0:T(8,128)(2,1)S(1)}, u32[]{:S(2)}, u32[]{:S(2)}) collective-permute-start(bf16[2,256,128]{2,1,0:T(8,128)(2,1)S(1)} %get-tuple-element.13), channel_id=1, source_target_pairs={{1,2},{2,1},{3,4},{4,3},{5,6},{6,5},{7,8},{8,7},{9,10},{10,9},{11,... | collective-permute-start | bytes 393224 | tf_op jit(solution)/shard_map/ppermute | solution.py:223
  2.3 15.0 %all_to_all.10.sums_ref = f32[16,1,128]{2,1,0:T(1,128)S(1)} all-to-all(f32[16,1,128]{2,1,0:T(1,128)S(1)} %get-tuple-element.11), channel_id=1, replica_groups={{0,1,14,15,2,3,12,13,4,5,10,11,6,7,8,9},{16,17,30,31,18,19,28,29,20,21,..., dimensions={0} | all-to-all | bytes 16384 | tf_op jit(solution)/shard_map/all_to_all | solution.py:193
  17.3 0.0 collective-permute-done.pair_ref
  17.3 0.0 collective-permute-done.1.other_ref
  17.3 0.0 copy-done.1
  17.3 0.0 copy-done.3
  17.3 0.0 copy-done.4
  17.3 0.0 copy-done.5
  17.3 1.5 %first.1 = (bf16[6,256,128]{2,1,0:T(8,128)(2,1)S(1)}, f32[16,1,128]{2,1,0:T(1,128)S(1)}, f32[8,128]{1,0:T(8,128)S(1)}) custom-call(f32[16,1,128]{2,1,0:T(1,128)S(1)} %all_to_all.10.sums_ref, bf16[4,256,128]{2,1,0:T(8,128)(2,1)S(1)} %bitcast.11, bf16[2,256,128]{2,1,0:T(8,128)(2,1)S(1)} %collective-permute-done.pair_ref, ...), custom_call_target="tpu_custom_call" | custom-call | tf_op jit(solution)/shard_map/first/pallas_call | solution.py:226
  18.9 8.9 %all_to_all.11.sums_ref = f32[16,1,128]{2,1,0:T(1,128)S(1)} all-to-all(f32[16,1,128]{2,1,0:T(1,128)S(1)} %get-tuple-element.14), channel_id=1, replica_groups={{0,1,14,15,2,3,12,13,4,5,10,11,6,7,8,9},{16,17,30,31,18,19,28,29,20,21,..., dimensions={0} | all-to-all | bytes 16384 | tf_op jit(solution)/shard_map/all_to_all | solution.py:193
  27.7 0.0 copy-done.2
  27.7 1.7 %second.1 = bf16[4,256,128]{2,1,0:T(8,128)(2,1)} custom-call(f32[16,1,128]{2,1,0:T(1,128)S(1)} %all_to_all.11.sums_ref, bf16[6,256,128]{2,1,0:T(8,128)(2,1)S(1)} %get-tuple-element.15.hidden_ref, bf16[4,256,128]{2,1,0:T(8,128)(2,1)S(1)} %bitcast.12, bf16[3,9,128,128]{3,2,1,0:T(8,128)(2,1)S(1)} %bitcast.14, f32[8,128]{1,0:T(8,128)S(1)} %get-tuple-element.16.params_ref), custom_call_target="tpu_custom_call" | custom-call | tf_op jit(solution)/shard_map/second/pallas_call | solution.py:256
Async XLA Ops:
  0.0 0.9 %copy-start = (bf16[1,4,256,128]{3,2,1,0:T(8,128)(2,1)S(1)}, bf16[1,4,256,128]{3,2,1,0:T(8,128)(2,1)}, u32[]{:S(2)}) copy-start(bf16[1,4,256,128]{3,2,1,0:T(8,128)(2,1)} %param.9) | copy-start | bytes 786436
  1.0 16.4 %copy-start.1 = (bf16[3,3,3,128,128]{4,3,2,1,0:T(8,128)(2,1)S(1)}, bf16[3,3,3,128,128]{4,3,2,1,0:T(8,128)(2,1)}, u32[]{:S(2)}) copy-start(bf16[3,3,3,128,128]{4,3,2,1,0:T(8,128)(2,1)} %param.12) | copy-start | bytes 2654212
  1.0 16.4 %copy-start.3 = (f32[128]{0:T(128)S(1)}, f32[128]{0:T(128)}, u32[]{:S(2)}) copy-start(f32[128]{0:T(128)} %param.13) | copy-start | bytes 1540
  1.0 16.4 %copy-start.4 = (f32[128]{0:T(128)S(1)}, f32[128]{0:T(128)}, u32[]{:S(2)}) copy-start(f32[128]{0:T(128)} %param.10) | copy-start | bytes 1540
  1.0 16.4 %copy-start.5 = (f32[128]{0:T(128)S(1)}, f32[128]{0:T(128)}, u32[]{:S(2)}) copy-start(f32[128]{0:T(128)} %param.11) | copy-start | bytes 1540
  1.1 26.6 %copy-start.2 = (bf16[3,3,3,128,128]{4,3,2,1,0:T(8,128)(2,1)S(1)}, bf16[3,3,3,128,128]{4,3,2,1,0:T(8,128)(2,1)}, u32[]{:S(2)}) copy-start(bf16[3,3,3,128,128]{4,3,2,1,0:T(8,128)(2,1)} %param.16) | copy-start | bytes 2654212
  1.2 16.1 %collective-permute-start = (bf16[2,256,128]{2,1,0:T(8,128)(2,1)S(1)}, bf16[2,256,128]{2,1,0:T(8,128)(2,1)S(1)}, u32[]{:S(2)}, u32[]{:S(2)}) collective-permute-start(bf16[2,256,128]{2,1,0:T(8,128)(2,1)S(1)} %get-tuple-element.12), channel_id=1, source_target_pairs={{0,1},{1,0},{2,3},{3,2},{4,5},{5,4},{6,7},{7,6},{8,9},{9,8},{10,11... | collective-permute-start | bytes 393224 | tf_op jit(solution)/shard_map/ppermute | solution.py:224
  1.7 15.6 %collective-permute-start.1 = (bf16[2,256,128]{2,1,0:T(8,128)(2,1)S(1)}, bf16[2,256,128]{2,1,0:T(8,128)(2,1)S(1)}, u32[]{:S(2)}, u32[]{:S(2)}) collective-permute-start(bf16[2,256,128]{2,1,0:T(8,128)(2,1)S(1)} %get-tuple-element.13), channel_id=1, source_target_pairs={{1,2},{2,1},{3,4},{4,3},{5,6},{6,5},{7,8},{8,7},{9,10},{10,9},{11,... | collective-permute-start | bytes 393224 | tf_op jit(solution)/shard_map/ppermute | solution.py:223
